TPU v7x, 32 devices: a whole 2x2x4 slice. The times are simulated.
32 devices in a mesh: bus: 8 (over z, y), tm: 4 (over x, core).
Axes of the slice: x: 2, y: 2, z: 4, core: 2. Of those that a mesh axis runs over, the one named last changes fastest.
Arguments:
- features: bfloat16 [1024, 64, 128], P('bus', 'tm'), may hold values from -6 to 6
- couplings: bfloat16 [16, 8, 64, 64], P('bus'), may hold values from -0.25 to 0.25
- neighbors: int32 [16, 8], P('bus'), may hold values from 0 to 15, as said below
- w_graph: bfloat16 [128, 128], replicated, may hold values from -0.5 to 0.5
- kernel_taps: bfloat16 [64, 128], replicated, may hold values from -0.3984375 to 0.3984375
- w_out: bfloat16 [128, 128], replicated, may hold values from -0.5 to 0.5
- cotangent: bfloat16 [1024, 64, 128], P('bus', 'tm'), may hold values from -6 to 6
Outputs:
- grad_features: bfloat16 [1024, 64, 128], P('bus', 'tm')
- grad_graph: float32 [128, 128], replicated
- grad_out: float32 [128, 128], replicated
- grad_taps: float32 [64, 128], replicated
Inputs may be any that keep to these rules, and one draw needn't show every extreme that they name: neighbors[i, 0] = i. Counting 2 blocks to each index of bus, every entry of block i names a block of the same index, one of the last 1 block of the index before, or one of the first 1 block of the index after.
All inputs are finite; a program needn't handle non-finite values.
Results may differ from a plain program's by a relative error of at most 0.0067.
Values may be sent and summed in bfloat16 or wider, within the bound.
No kernel may reach another device: no remote copies, remote signals or barrier semaphores. Data moves between devices by JAX's collectives and lax.ppermute only.
A program may use at most 64 MiB of HBM per device.

v0:
```python
import math

import jax
import jax.numpy as jnp
from jax import lax
from jax.sharding import PartitionSpec as P


def with_halo(array, sides, width):
    for axis, dim in sides:
        size, length = (lax.axis_size(axis), array.shape[dim])
        up = [(i, (i + 1) % size) for i in range(size - 1)]
        down = [(j, i) for i, j in up]
        last = lax.slice_in_dim(array, length - width, length, axis=dim)
        first = lax.slice_in_dim(array, 0, width, axis=dim)
        before = lax.ppermute(last, axis, up)
        after = lax.ppermute(first, axis, down)
        array = jnp.concatenate([before, array, after], axis=dim)
    return array


def shifted(value, axis, steps):
    count = lax.axis_size(axis)
    first, last = (max(0, -steps), min(count, count - steps))
    return lax.ppermute(value, axis, [(source, source + steps) for source in range(first, last)])


def toeplitz_table(kernel_taps):
    length = kernel_taps.shape[0]
    row_ids = jnp.arange(length, dtype=jnp.int32)
    lagged = row_ids[:, None] - row_ids[None, :]
    picked = jnp.take(kernel_taps.T, jnp.clip(lagged, 0, length - 1), axis=1)
    return jnp.where(lagged[None] >= 0, picked, jnp.zeros_like(picked))


def lag_sums(lag_table):
    channels = lag_table.shape[0]
    length = lag_table.shape[1]
    flipped = lag_table[:, :, ::-1]
    padded = jnp.pad(flipped, ((0, 0), (0, 0), (0, 1)))
    flat_view = padded.reshape(channels, length * (length + 1))
    window = flat_view[:, length - 1 : length - 1 + length * length].reshape(
        channels, length, length
    )
    row_ids = jnp.arange(length, dtype=jnp.int32)
    lag_mask = row_ids[None, :, None] >= row_ids[None, None, :]
    return jnp.sum(jnp.where(lag_mask, window, jnp.zeros_like(window)), axis=1).T


def silu_slope(pre_act):
    sigmoid_val = jax.nn.sigmoid(pre_act)
    return sigmoid_val * (1.0 + pre_act * (1.0 - sigmoid_val))


def shards(features, couplings, neighbors, w_graph, kernel_taps, w_out, cotangent):
    bus_rows, steps_per_shard, channels = features.shape
    blocks_dev = couplings.shape[0]
    slot_count = couplings.shape[1]
    block_rows = couplings.shape[2]
    flat_len = steps_per_shard * channels
    offset = neighbors - lax.axis_index("bus") * blocks_dev
    extended = with_halo(features, (("bus", 0),), blocks_dev * block_rows)
    position = offset + blocks_dev
    ext_blocks = extended.reshape(-1, block_rows, flat_len)
    picked = ext_blocks[position]
    mixed_blocks = jnp.einsum(
        "ikab,ikbn->ian", couplings, picked, preferred_element_type=jnp.float32
    ).astype(jnp.bfloat16)
    mixed_rows = mixed_blocks.reshape(bus_rows * steps_per_shard, channels)
    pre_act = jnp.dot(mixed_rows, w_graph, preferred_element_type=jnp.float32)
    activated = (
        jax.nn.silu(pre_act).astype(jnp.bfloat16).reshape(bus_rows, steps_per_shard, channels)
    )
    act_week, cot_week = (
        lax.all_to_all(activated, "tm", split_axis=0, concat_axis=1, tiled=True),
        lax.all_to_all(cotangent, "tm", split_axis=0, concat_axis=1, tiled=True),
    )
    lag_table = toeplitz_table(kernel_taps)
    convolved_rows = jnp.einsum(
        "cts,bsc->btc", lag_table, act_week, preferred_element_type=jnp.float32
    ).astype(jnp.bfloat16)
    part_out = jnp.einsum(
        "btc,btd->cd", convolved_rows, cot_week, preferred_element_type=jnp.float32
    )
    grad_conv = jnp.einsum(
        "btd,cd->btc", cot_week, w_out, preferred_element_type=jnp.float32
    ).astype(jnp.bfloat16)
    part_taps = lag_sums(
        jnp.einsum("btc,bsc->cts", grad_conv, act_week, preferred_element_type=jnp.float32)
    )
    grad_act = jnp.einsum(
        "cts,btc->bsc", lag_table, grad_conv, preferred_element_type=jnp.float32
    ).astype(jnp.bfloat16)
    grad_back = lax.all_to_all(grad_act, "tm", split_axis=1, concat_axis=0, tiled=True)
    grad_pre = (grad_back.reshape(-1, channels).astype(jnp.float32) * silu_slope(pre_act)).astype(
        jnp.bfloat16
    )
    part_graph = lax.dot_general(
        mixed_rows, grad_pre, (((0,), (0,)), ((), ())), preferred_element_type=jnp.float32
    )
    grad_mixed = lax.dot_general(
        grad_pre, w_graph, (((1,), (1,)), ((), ())), preferred_element_type=jnp.float32
    )
    grad_mixed = grad_mixed.astype(jnp.bfloat16).reshape(blocks_dev, block_rows, flat_len)
    spread = jnp.zeros((blocks_dev + 2 * blocks_dev, block_rows, flat_len), jnp.float32)
    for slot_index in range(slot_count):
        slot_term = jnp.einsum(
            "iab,ian->ibn", couplings[:, slot_index], grad_mixed, preferred_element_type=jnp.float32
        )
        spread = spread.at[position[:, slot_index]].add(slot_term)
    own_part = spread[blocks_dev : blocks_dev + blocks_dev]
    before = spread[:blocks_dev]
    after_part = spread[blocks_dev + blocks_dev :]
    from_after = shifted(before.astype(jnp.bfloat16), "bus", -1).astype(before.dtype)
    from_before = shifted(after_part.astype(jnp.bfloat16), "bus", 1).astype(after_part.dtype)
    own_part = own_part.at[blocks_dev - blocks_dev :].add(from_after)
    own_part = own_part.at[:blocks_dev].add(from_before)
    grad_features = (
        own_part.reshape(bus_rows, steps_per_shard, channels) + cotangent.astype(jnp.float32)
    ).astype(jnp.bfloat16)
    summed = lax.psum((part_graph, part_out, part_taps), ("bus", "tm"))
    total_rows = (
        lax.axis_size("bus") * blocks_dev * block_rows * steps_per_shard * lax.axis_size("tm")
    )
    grad_scale = 1.0 / math.sqrt(total_rows)
    return (grad_features, summed[0] * grad_scale, summed[1] * grad_scale, summed[2] * grad_scale)


def solution(mesh):
    return jax.shard_map(
        shards,
        mesh=mesh,
        in_specs=(
            P("bus", "tm", None),
            P("bus", None, None, None),
            P("bus", None),
            P(),
            P(),
            P(),
            P("bus", "tm", None),
        ),
        out_specs=(P("bus", "tm", None), P(), P(), P()),
        check_vma=False,
    )
```

profile of v0, /device:TPU:0, one launch (start us, length us, event | category | flops | bytes accessed | tf_op | source)
XLA Modules:
  0.0 320.1 jit_solution(4099502147771382947)
XLA Ops:
  7.2 5.0 %collective-permute-start = (bf16[128,16,128]{2,1,0:T(8,128)(2,1)}, bf16[128,16,128]{2,1,0:T(8,128)(2,1)S(1)}, u32[]{:S(2)}, u32[]{:S(2)}) collective-permute-start(bf16[128,16,128]{2,1,0:T(8,128)(2,1)} %param.15), channel_id=1, source_target_pairs={{0,4},{4,8},{8,12},{12,16},{16,20},{20,24},{24,28},{1,5},{5,9},{9,... | collective-permute-start | bytes 1572872 | tf_op jit(solution)/shard_map/ppermute | solution.py:16
  13.5 3.5 %all-to-all-start = ((bf16[128,16,128]{2,1,0:T(8,128)(2,1)}), bf16[128,16,128]{2,1,0:T(8,128)(2,1)S(1)}, u32[]{:S(2)}, u32[]{:S(2)}) async-start(bf16[128,16,128]{2,1,0:T(8,128)(2,1)} %param.21), calls=%async_computation | async-start | bytes 1048576 | tf_op jit(solution)/shard_map/all_to_all | solution.py:76
  17.9 12.1 %gather_fusion = bf16[4096,128]{1,0:T(8,128)(2,1)S(1)} fusion(bf16[128,64]{0,1:T(8,128)(2,1)S(1)} %bitcast.131, s32[4096]{0:T(1024)S(1)} %broadcast_clamp_fusion), kind=kCustom, calls=%fused_computation | custom fusion | bytes 2113536 | tf_op jit(solution)/shard_map/jit(_take)/gather | solution.py:32
  30.1 3.8 %copy.61 = bf16[64,64,128]{1,0,2:T(8,128)(2,1)} copy(bf16[64,64,128]{2,1,0:T(8,128)(2,1)S(1)} %bitcast.133) | data formatting | bytes 2097152 | tf_op jit(solution)/shard_map/jit(_take)/gather | solution.py:32
  37.0 2.6 fusion.15
  39.7 2.3 copy.63
  42.0 4.3 %all-to-all-start.1 = ((bf16[32,64,128]{2,0,1:T(8,128)(2,1)}), bf16[32,64,128]{2,0,1:T(8,128)(2,1)}, u32[]{:S(2)}, u32[]{:S(2)}) async-start(bf16[32,64,128]{2,0,1:T(8,128)(2,1)} %copy.63), calls=%async_computation.1 | async-start | bytes 1048576 | tf_op jit(solution)/shard_map/all_to_all | solution.py:94
  49.4 2.7 gather_fusion.1
  52.2 3.1 fusion.1
  70.2 2.2 scatter_fusion
  72.4 2.2 scatter_fusion.1
  74.6 2.2 scatter_fusion.2
  76.7 2.1 scatter_fusion.3
  78.9 2.2 scatter_fusion.4
  81.1 2.2 scatter_fusion.5
  83.3 2.2 scatter_fusion.6
  85.4 2.2 scatter_fusion.7
  89.0 4.1 %all-to-all-start.2 = ((bf16[128,16,128]{2,1,0:T(8,128)(2,1)}), bf16[128,16,128]{2,1,0:T(8,128)(2,1)}, u32[]{:S(2)}, u32[]{:S(2)}) async-start(bf16[128,16,128]{2,1,0:T(8,128)(2,1)} %bitcast.141), calls=%async_computation.2 | async-start | bytes 1048576 | tf_op jit(solution)/shard_map/all_to_all | solution.py:75
  93.2 2.5 fusion.59
  97.0 5.9 %collective-permute-start.3 = (bf16[2,64,2048]{2,1,0:T(8,128)(2,1)}, bf16[2,64,2048]{2,1,0:T(8,128)(2,1)}, u32[]{:S(2)}, u32[]{:S(2)}) collective-permute-start(bf16[2,64,2048]{2,1,0:T(8,128)(2,1)} %get-tuple-element.55), channel_id=1, source_target_pairs={{0,4},{4,8},{8,12},{12,16},{16,20},{20,24},{24,28},{1,5},{5,9},{9,... | collective-permute-start | bytes 1572872 | tf_op jit(solution)/shard_map/ppermute | solution.py:25
  103.9 1.9 copy.74
  105.8 3.3 %copy.75 = bf16[32,64,128]{1,0,2:T(8,128)(2,1)} copy(bf16[32,64,128]{2,1,0:T(8,128)(2,1)} %bitcast.137) | data formatting | bytes 1048576 | tf_op jit(solution)/shard_map/all_to_all | solution.py:75
  109.1 3.2 %fusion.12 = bf16[32,64,128]{1,0,2:T(8,128)(2,1)S(1)} fusion(bf16[32,64,128]{1,0,2:T(8,128)(2,1)} %copy.75, bf16[64,64,128]{1,0,2:T(8,128)(2,1)} %copy.61, pred[64,64]{1,0:T(8,128)(4,1)S(1)} %get-tuple-element.61, pred[64,64]{1,0:T(8,128)(4,1)S(1)} %get-tuple-element.60), kind=kOutput, calls=%fused_computation.31 | convolution fusion | flops 34865152 | bytes 2105344 | tf_op jit(solution)/shard_map/cts,bsc->btc/dot_general | solution.py:79
  112.4 2.7 fusion.61
  116.5 7.2 %rev.3 = f32[128,64,64]{2,1,0:T(8,128)} reverse(f32[128,64,64]{2,1,0:T(8,128)} %fusion.61), dimensions={2} | reverse | bytes 4194304 | tf_op jit(solution)/shard_map/rev | solution.py:39
  123.8 4.9 %pad.10 = f32[128,64,65]{2,1,0:T(8,128)} pad(f32[128,64,64]{2,1,0:T(8,128)} %rev.3, f32[]{:T(128)} %constant.102.clone.1), padding=0_0x0_0x0_1 | pad | bytes 4227076 | tf_op jit(solution)/shard_map/jit(_pad)/pad | solution.py:40
  128.7 5.1 %reshape.265 = f32[128,4160]{1,0:T(8,128)} reshape(f32[128,64,65]{2,1,0:T(8,128)} %pad.10) | data formatting | bytes 4259840 | tf_op jit(solution)/shard_map/reshape | solution.py:41
  133.8 3.6 %slice.127 = f32[128,4096]{1,0:T(8,128)} slice(f32[128,4160]{1,0:T(8,128)} %reshape.265), slice={[0:128], [63:4159]} | slice | bytes 4194304 | tf_op jit(solution)/shard_map/slice | solution.py:42
  137.3 2.9 copy.90
  140.2 1.9 select_reduce_fusion
  142.2 41.9 %psum.23 = f32[64,128]{1,0:T(8,128)S(1)} all-reduce(f32[64,128]{1,0:T(8,128)S(1)} %bitcast.142), channel_id=1, replica_groups=mesh['bus'=8,'tm'=4] {'bus','tm'}, use_global_device_ids=true, to_apply=%region_11.12 | all-reduce | flops 8192 | bytes 65536 | tf_op jit(solution)/shard_map/psum | solution.py:121
  184.7 123.1 %all-reduce.4.cloned.1.call-done = (f32[128,128]{1,0:T(8,128)}, f32[128,128]{1,0:T(8,128)}) async-done(((f32[128,128]{1,0:T(8,128)}, f32[128,128]{1,0:T(8,128)}), (f32[128,128]{1,0:T(8,128)}, f32[128,128]{1,0:T(8,128)})) %all-reduce.4.cloned.1.call-update) | async-done | bytes 131088 | tf_op jit(solution)/shard_map/psum | solution.py:121
  (80 shorter events, 34.5 us)
Async XLA Ops:
  7.2 50.0 %copy-start = (bf16[128,128]{1,0:T(8,128)(2,1)S(1)}, bf16[128,128]{1,0:T(8,128)(2,1)}, u32[]{:S(2)}) copy-start(bf16[128,128]{1,0:T(8,128)(2,1)} %param.18) | copy-start | bytes 98308
  7.2 10.7 %copy-start.1 = (bf16[64,128]{1,0:T(8,128)(2,1)S(1)}, bf16[64,128]{1,0:T(8,128)(2,1)}, u32[]{:S(2)}) copy-start(bf16[64,128]{1,0:T(8,128)(2,1)} %param.19) | copy-start | bytes 49156
  7.2 39.1 %collective-permute-start = (bf16[128,16,128]{2,1,0:T(8,128)(2,1)}, bf16[128,16,128]{2,1,0:T(8,128)(2,1)S(1)}, u32[]{:S(2)}, u32[]{:S(2)}) collective-permute-start(bf16[128,16,128]{2,1,0:T(8,128)(2,1)} %param.15), channel_id=1, source_target_pairs={{0,4},{4,8},{8,12},{12,16},{16,20},{20,24},{24,28},{1,5},{5,9},{9,... | collective-permute-start | bytes 1572872 | tf_op jit(solution)/shard_map/ppermute | solution.py:16
  12.2 34.9 %collective-permute-start.1 = (bf16[128,16,128]{2,1,0:T(8,128)(2,1)}, bf16[128,16,128]{2,1,0:T(8,128)(2,1)}, u32[]{:S(2)}, u32[]{:S(2)}) collective-permute-start(bf16[128,16,128]{2,1,0:T(8,128)(2,1)} %param.15), channel_id=1, source_target_pairs={{4,0},{8,4},{12,8},{16,12},{20,16},{24,20},{28,24},{5,1},{9,5},{13... | collective-permute-start | bytes 1572872 | tf_op jit(solution)/shard_map/ppermute | solution.py:17
  13.5 20.7 %all-to-all-start = ((bf16[128,16,128]{2,1,0:T(8,128)(2,1)}), bf16[128,16,128]{2,1,0:T(8,128)(2,1)S(1)}, u32[]{:S(2)}, u32[]{:S(2)}) async-start(bf16[128,16,128]{2,1,0:T(8,128)(2,1)} %param.21), calls=%async_computation | async-start | bytes 1048576 | tf_op jit(solution)/shard_map/all_to_all | solution.py:76
  30.0 5.0 %copy-start.14 = (bf16[128,128]{1,0:T(8,128)(2,1)S(1)}, bf16[128,128]{1,0:T(8,128)(2,1)}, u32[]{:S(2)}) copy-start(bf16[128,128]{1,0:T(8,128)(2,1)} %param.20) | copy-start | bytes 98308
  34.3 0.8 copy-start.6
  37.0 2.7 copy-start.2
  42.0 13.6 %all-to-all-start.1 = ((bf16[32,64,128]{2,0,1:T(8,128)(2,1)}), bf16[32,64,128]{2,0,1:T(8,128)(2,1)}, u32[]{:S(2)}, u32[]{:S(2)}) async-start(bf16[32,64,128]{2,0,1:T(8,128)(2,1)} %copy.63), calls=%async_computation.1 | async-start | bytes 1048576 | tf_op jit(solution)/shard_map/all_to_all | solution.py:94
  46.3 0.8 copy-start.13
  49.4 2.8 copy-start.5
  55.5 1.7 copy-start.8
  58.7 3.2 %copy-start.10 = (bf16[2048,128]{1,0:T(8,128)(2,1)}, bf16[2048,128]{1,0:T(8,128)(2,1)S(1)}, u32[]{:S(2)}) copy-start(bf16[2048,128]{1,0:T(8,128)(2,1)S(1)} %get-tuple-element.57) | copy-start | bytes 1572868
  89.0 14.9 %all-to-all-start.2 = ((bf16[128,16,128]{2,1,0:T(8,128)(2,1)}), bf16[128,16,128]{2,1,0:T(8,128)(2,1)}, u32[]{:S(2)}, u32[]{:S(2)}) async-start(bf16[128,16,128]{2,1,0:T(8,128)(2,1)} %bitcast.141), calls=%async_computation.2 | async-start | bytes 1048576 | tf_op jit(solution)/shard_map/all_to_all | solution.py:75
  93.2 214.6 %all-reduce.4.cloned.1.call-start = ((), (), s32[]{:S(2)}) async-start(), calls=%async_computation.3 | async-start | bytes 262144 | tf_op jit(solution)/shard_map/psum | solution.py:121
  93.2 9.7 %copy-start.9 = (bf16[2048,128]{1,0:T(8,128)(2,1)S(1)}, bf16[2048,128]{1,0:T(8,128)(2,1)}, u32[]{:S(2)}) copy-start(bf16[2048,128]{1,0:T(8,128)(2,1)} %copy-done.8) | copy-start | bytes 1572868
  93.2 9.7 %copy-start.11 = (bf16[2048,128]{1,0:T(8,128)(2,1)S(1)}, bf16[2048,128]{1,0:T(8,128)(2,1)}, u32[]{:S(2)}) copy-start(bf16[2048,128]{1,0:T(8,128)(2,1)} %copy-done.10) | copy-start | bytes 1572868
  95.7 215.0 %collective-permute-start.2 = (bf16[2,64,2048]{2,1,0:T(8,128)(2,1)}, bf16[2,64,2048]{2,1,0:T(8,128)(2,1)}, u32[]{:S(2)}, u32[]{:S(2)}) collective-permute-start(bf16[2,64,2048]{2,1,0:T(8,128)(2,1)} %get-tuple-element.54), channel_id=1, source_target_pairs={{4,0},{8,4},{12,8},{16,12},{20,16},{24,20},{28,24},{5,1},{9,5},{13... | collective-permute-start | bytes 1572872 | tf_op jit(solution)/shard_map/ppermute | solution.py:25
  97.0 213.7 %collective-permute-start.3 = (bf16[2,64,2048]{2,1,0:T(8,128)(2,1)}, bf16[2,64,2048]{2,1,0:T(8,128)(2,1)}, u32[]{:S(2)}, u32[]{:S(2)}) collective-permute-start(bf16[2,64,2048]{2,1,0:T(8,128)(2,1)} %get-tuple-element.55), channel_id=1, source_target_pairs={{0,4},{4,8},{8,12},{12,16},{16,20},{20,24},{24,28},{1,5},{5,9},{9,... | collective-permute-start | bytes 1572872 | tf_op jit(solution)/shard_map/ppermute | solution.py:25
  109.1 3.3 %copy-start.3 = (bf16[32,64,128]{1,0,2:T(8,128)(2,1)S(1)}, bf16[32,64,128]{1,0,2:T(8,128)(2,1)}, u32[]{:S(2)}) copy-start(bf16[32,64,128]{1,0,2:T(8,128)(2,1)} %copy-done.2) | copy-start | bytes 1572868
  109.1 3.3 %copy-start.4 = (bf16[32,64,128]{1,0,2:T(8,128)(2,1)S(1)}, bf16[32,64,128]{1,0,2:T(8,128)(2,1)}, u32[]{:S(2)}) copy-start(bf16[32,64,128]{1,0,2:T(8,128)(2,1)} %copy.75) | copy-start | bytes 1572868
  112.4 2.7 copy-start.7
  310.7 1.6 copy-start.12
Sparse Core Ops, SparseCore 0:
  184.2 123.5 all-reduce.3
where the time goes:
time: 322 us; the launch traced here: 320 us
  waiting for transfers between devices  123 us (38%)
  local copies, waits for them, and re-layouts  59.1 us (18%)
  blocking collectives  41.9 us (13%)
  other arithmetic  29.2 us (9%)
  matrix products  26.7 us (8%)
  starting transfers between devices  25.5 us (8%)
  between operations  14.5 us (5%)
    psum x1, waiting for transfers between devices, shards(): summed = lax.psum((part_graph, part_out, part_taps), ('bus', 'tm'))  123 us
    psum x1, blocking collectives, shards(): summed = lax.psum((part_graph, part_out, part_taps), ('bus', 'tm'))  41.9 us
    scatter-add x8, other arithmetic, shards(): spread = spread.at[position[:, slot_index]].add(slot_term)  17.4 us
    gather x2, local copies, waits for them, and re-layouts, toeplitz_table(): picked = jnp.take(kernel_taps.T, jnp.clip(lagged, 0, length - 1), axis=1)  15.9 us
    dot_general x8, matrix products, shards(): jnp.einsum('iab,ian->ibn', couplings[:, slot_index], grad_mixed, preferre...  10.6 us
    rev x1, local copies, waits for them, and re-layouts, lag_sums(): flipped = lag_table[:, :, ::-1]  7.21 us
    ppermute x2, starting transfers between devices, shifted(): lax.ppermute(value, axis, [(source, source + steps) for source in range(f...  7.19 us
  transfers between devices with their start and end apart: 8, of which 1 were waited for; matrix products, arithmetic and copies ran while one was open for 24% of the time, Pallas kernels for 0%

commit v1 on v0

v1 whole, which is shorter than its diff:
```python
import math

import jax
import jax.numpy as jnp
from jax import lax
from jax.experimental import pallas as pl
from jax.experimental.pallas import tpu as pltpu
from jax.sharding import PartitionSpec as P

BF = jnp.bfloat16
F32 = jnp.float32
VMEM = pl.BlockSpec(memory_space=pltpu.VMEM)
LIMIT = 48 * 1024 * 1024


def call(body, outs, *args, scratch=(), flops=1 << 28):
    return pl.pallas_call(
        body,
        out_shape=[jax.ShapeDtypeStruct(shape, dtype) for shape, dtype in outs],
        in_specs=[VMEM] * len(args),
        out_specs=[VMEM] * len(outs),
        scratch_shapes=list(scratch),
        compiler_params=pltpu.CompilerParams(vmem_limit_bytes=LIMIT),
        cost_estimate=pl.CostEstimate(flops=flops, bytes_accessed=1 << 20, transcendentals=0),
    )(*args)


def dot(left, right, dims=((1,), (0,))):
    return lax.dot_general(left, right, (dims, ((), ())), preferred_element_type=F32)


def time_major(value):
    return jnp.swapaxes(value.astype(F32), 0, 1).astype(BF)


def split_body(feat_ref, cot_ref, own_ref, first_ref, last_ref, cot_out_ref):
    rows = feat_ref.shape[0]
    half = first_ref.shape[1]
    for start in range(0, rows, 16):
        part = time_major(feat_ref[start : start + 16])
        own_ref[:, start : start + 16] = part
        if start < half:
            first_ref[:, start : start + 16] = part
        if start >= rows - half:
            at = start - (rows - half)
            last_ref[:, at : at + 16] = part
        cot_out_ref[:, start : start + 16] = time_major(cot_ref[start : start + 16])


def conv_body(slot_ref, c0_ref, c1_ref, c2_ref, c3_ref, taps_ref, wout_ref, grad_ref, cross_ref, conv, lags):
    steps, rows, chans = c0_ref.shape
    total = taps_ref.shape[0]
    near, far = slot_ref[0], slot_ref[1]
    for at, ref in ((0, c0_ref), (near, c1_ref), (2, c2_ref), (far, c3_ref)):
        for s in range(0, steps, 4):
            block = ref[s : s + 4].reshape(4 * rows, chans)
            conv[at, s : s + 4] = (
                dot(block, wout_ref[...], ((1,), (1,))).astype(BF).reshape(4, rows, chans)
            )
        for s in range(0, steps, 2):
            cross_ref[at * (steps // 2) + s // 2, :, 0:rows] = ref[s].T
            cross_ref[at * (steps // 2) + s // 2, :, rows : 2 * rows] = ref[s + 1].T
    cross_ref[2 * steps :] = jnp.zeros_like(cross_ref[2 * steps :])
    lags[0:16] = jnp.zeros((16, 8, chans), F32)
    taps = taps_ref[...].astype(F32)
    for lag in range(total):
        lags[16 + lag] = jnp.broadcast_to(taps[lag : lag + 1], (8, chans))

    def tile(index, carry):
        where = pl.ds(pl.multiple_of(index * 16, 16), 16)
        sums = [[jnp.zeros((8, chans), F32)] * 2 for _ in range(steps)]
        for j in range(4):
            for t in range(steps):
                value = conv[j, t, where, :].astype(F32)
                for s in range(steps):
                    lag = j * steps + t - s
                    if lag < 0:
                        continue
                    tap = lags[16 + lag]
                    sums[s][0] += tap * value[:8]
                    sums[s][1] += tap * value[8:]
        for s in range(steps):
            grad_ref[s, where, :] = jnp.concatenate(sums[s], axis=0).astype(BF)
        return carry

    lax.fori_loop(0, rows // 16, tile, 0)


def main_body(
    own_ref, before_ref, after_ref, mix_ref, mixt_ref, wg_ref, grad_ref,
    act_ref, spread_ref, down_ref, up_ref, graph_ref,
):
    steps, rows, chans = own_ref.shape
    half = before_ref.shape[1]
    group = 4
    mix, mixt, wg = mix_ref[...], mixt_ref[...], wg_ref[...]
    graph = jnp.zeros((chans, chans), F32)
    for s in range(0, steps, group):
        ext = jnp.concatenate(
            [
                jnp.concatenate([before_ref[t], own_ref[t], after_ref[t]], axis=0)
                for t in range(s, s + group)
            ],
            axis=1,
        )
        mixed = dot(mix, ext).astype(BF)
        mixed = jnp.concatenate(
            [mixed[:, t * chans : (t + 1) * chans] for t in range(group)], axis=0
        )
        pre = dot(mixed, wg)
        gate = 1.0 / (1.0 + jnp.exp(-pre))
        act = pre * gate
        act_ref[s : s + group] = act.astype(BF).reshape(group, rows, chans)
        slope = gate * (1.0 + pre * (1.0 - gate))
        grad = grad_ref[s : s + group].reshape(group * rows, chans).astype(F32)
        grad_pre = (grad * slope).astype(BF)
        graph += dot(mixed, grad_pre, ((0,), (0,)))
        grad_mixed = dot(grad_pre, wg, ((1,), (1,))).astype(BF)
        grad_mixed = jnp.concatenate(
            [grad_mixed[t * rows : (t + 1) * rows] for t in range(group)], axis=1
        )
        spread = dot(mixt, grad_mixed)
        for t in range(group):
            part = spread[:, t * chans : (t + 1) * chans]
            down_ref[s + t] = part[:half].astype(BF)
            spread_ref[s + t] = part[half : half + rows]
            up_ref[s + t] = part[half + rows :].astype(BF)
    graph_ref[...] = graph


def lag_body(act_ref, cross_ref, taps_ref, wout_ref, out_ref, lag_ref, stack, acc_ref):
    steps, rows, chans = act_ref.shape
    pairs = cross_ref.shape[0] - steps // 2
    zero = jnp.zeros((rows, chans), BF)
    for i in range(steps // 2 + 1):
        s = 2 * i
        stack[i, 0:rows, 0:chans] = act_ref[s] if s < steps else zero
        stack[i, rows : 2 * rows, 0:chans] = act_ref[s + 1] if s < steps else zero
        stack[i, 0:rows, chans : 2 * chans] = act_ref[s - 1] if s > 0 else zero
        stack[i, rows : 2 * rows, chans : 2 * chans] = act_ref[s] if s < steps else zero
    acc_ref[...] = jnp.zeros_like(acc_ref)
    weight = wout_ref[...].astype(F32).T

    def group(index, carry):
        at = index * 2
        total = jnp.zeros((2 * rows, 2 * chans), F32)
        for i in range(steps // 2 + 1):
            left = cross_ref[pl.ds(at + i, 2)].reshape(2 * rows, 2 * rows)
            total += dot(left, stack[i])
        taps = taps_ref[pl.ds(pl.multiple_of(index * 8, 8), 8)]
        found = []
        acc = jnp.zeros((chans, chans), F32)
        for lag in range(4):
            part = total[(lag // 2) * rows : (lag // 2 + 1) * rows, (lag % 2) * chans : (lag % 2 + 1) * chans]
            acc += part * taps[lag : lag + 1]
            found.append(jnp.sum(part * weight, axis=0, keepdims=True))
        acc_ref[...] += acc
        lag_ref[pl.ds(pl.multiple_of(index * 8, 8), 8)] = jnp.concatenate(found + found, axis=0)
        return carry

    lax.fori_loop(0, pairs // 2, group, 0)
    out_ref[...] = acc_ref[...].T


def final_body(spread_ref, before_ref, after_ref, cot_ref, out_ref):
    rows = spread_ref.shape[1]
    half = before_ref.shape[1]
    for start in range(0, rows, 16):
        value = spread_ref[:, start : start + 16]
        if start < half:
            value = value + before_ref[:, start : start + 16].astype(F32)
        if start >= rows - half:
            at = start - (rows - half)
            value = value + after_ref[:, at : at + 16].astype(F32)
        part = jnp.swapaxes(value, 0, 1) + cot_ref[start : start + 16].astype(F32)
        out_ref[start : start + 16] = part.astype(BF)


def swap(value, axis, distance):
    size = lax.axis_size(axis)
    return lax.ppermute(value, axis, [(i, i ^ distance) for i in range(size)])


def reduce_all(value, bus, tm):
    side = lax.axis_index("tm") & 1
    halves = value.reshape(2, value.shape[0] // 2, value.shape[1])
    keep = lax.dynamic_index_in_dim(halves, side, 0, False)
    send = lax.dynamic_index_in_dim(halves, 1 - side, 0, False)
    keep = keep + swap(send, "tm", 1)
    hops = [("tm", 1 << bit) for bit in range(1, tm.bit_length() - 1)]
    hops += [("bus", 1 << bit) for bit in range(1, bus.bit_length() - 1)] + [("bus", 1)]
    for axis, distance in hops:
        sent = keep.astype(BF)
        keep = sent.astype(F32) + swap(sent, axis, distance).astype(F32)
    other = swap(keep, "tm", 1)
    return jnp.where(
        side == 0, jnp.concatenate([keep, other]), jnp.concatenate([other, keep])
    )


def shards(features, couplings, neighbors, w_graph, kernel_taps, w_out, cotangent):
    bus, tm = lax.axis_size("bus"), lax.axis_size("tm")
    rows, steps, chans = features.shape
    blocks, slots, half = couplings.shape[:3]
    up = [(i, i + 1) for i in range(bus - 1)]
    down = [(i + 1, i) for i in range(bus - 1)]
    wide = (steps, rows, chans)
    edge = (steps, half, chans)

    own, first, last, cot = call(
        split_body, [(wide, BF), (edge, BF), (edge, BF), (wide, BF)], features, cotangent
    )
    far = lax.ppermute(cot, "tm", [(2, 0), (3, 1)])
    before = lax.ppermute(last, "bus", up)
    after = lax.ppermute(first, "bus", down)
    near = lax.ppermute(cot, "tm", [(1, 0), (3, 2)])
    cross = lax.ppermute(far, "tm", [(1, 0), (0, 1)])

    position = neighbors - lax.axis_index("bus") * blocks + 1
    picks = (position[:, :, None] == jnp.arange(blocks + 2)[None, None]).astype(BF)
    mix = jnp.einsum("ikp,ikab->iapb", picks, couplings, preferred_element_type=F32)
    mix = mix.reshape(rows, (blocks + 2) * half).astype(BF)

    odd = lax.axis_index("tm") & 1
    slot = jnp.stack([jnp.where(odd == 0, 1, 3), jnp.where(odd == 0, 3, 1)]).astype(jnp.int32)
    pairs = 2 * steps + steps // 2
    grad_act, crossed = pl.pallas_call(
        conv_body,
        out_shape=[
            jax.ShapeDtypeStruct(wide, BF),
            jax.ShapeDtypeStruct((pairs, chans, 2 * rows), BF),
        ],
        in_specs=[pl.BlockSpec(memory_space=pltpu.SMEM)] + [VMEM] * 6,
        out_specs=[VMEM] * 2,
        scratch_shapes=[pltpu.VMEM((4,) + wide, BF), pltpu.VMEM((16 + 64, 8, chans), F32)],
        compiler_params=pltpu.CompilerParams(vmem_limit_bytes=LIMIT),
        cost_estimate=pl.CostEstimate(flops=1 << 31, bytes_accessed=1 << 20, transcendentals=0),
    )(slot, cot, near, far, cross, kernel_taps, w_out)

    act, spread, to_before, to_after, part_graph = call(
        main_body,
        [(wide, BF), (wide, F32), (edge, BF), (edge, BF), ((chans, chans), F32)],
        own, before, after, mix, mix.T, w_graph, grad_act,
    )
    from_after = lax.ppermute(to_before, "bus", down)
    from_before = lax.ppermute(to_after, "bus", up)

    taps8 = kernel_taps.astype(F32).reshape(-1, 4, chans)
    taps8 = jnp.concatenate([taps8, taps8], axis=1).reshape(-1, chans)
    part_out, part_lags = call(
        lag_body,
        [((chans, chans), F32), ((2 * tm * steps, chans), F32)],
        act, crossed, taps8, w_out,
        scratch=[
            pltpu.VMEM((steps // 2 + 1, 2 * rows, 2 * chans), BF),
            pltpu.VMEM((chans, chans), F32),
        ],
        flops=1 << 32,
    )
    part_lags = part_lags.reshape(-1, 2, 4, chans)[:, 0].reshape(-1, chans)
    summed = reduce_all(jnp.concatenate([part_graph, part_out, part_lags]), bus, tm)
    (grad_features,) = call(
        final_body, [(features.shape, BF)], spread, from_before, from_after, cotangent
    )
    scale = 1.0 / math.sqrt(bus * rows * steps * tm)
    summed = summed * scale
    return grad_features, summed[:chans], summed[chans : 2 * chans], summed[2 * chans :]


def solution(mesh):
    return jax.shard_map(
        shards,
        mesh=mesh,
        in_specs=(
            P("bus", "tm", None),
            P("bus", None, None, None),
            P("bus", None),
            P(),
            P(),
            P(),
            P("bus", "tm", None),
        ),
        out_specs=(P("bus", "tm", None), P(), P(), P()),
        check_vma=False,
    )
```

time: 322 us -> 74.7 us (0.23)
  the two profiles are of different devices: /device:TPU:0 before, /device:TPU:24 now
where the time goes in v1:
time: 74.7 us; the launch traced here: 74.1 us
  waiting for transfers between devices  26.5 us (35%)
  starting transfers between devices  20.9 us (28%)
  Pallas kernels  18.6 us (25%)
  local copies, waits for them, and re-layouts  5.17 us (7%)
  other arithmetic  1.68 us (2%)
  between operations  0.88 us (1%)
    ppermute x6, waiting for transfers between devices, swap(): return lax.ppermute(value, axis, [(i, i ^ distance) for i in range(size)])  13.5 us
    pallas_call x4, Pallas kernels, call(): pl.pallas_call(body, out_shape=[jax.ShapeDtypeStruct(shape, dtype) for sh...  12.6 us
    ppermute x1, waiting for transfers between devices, shards(): far = lax.ppermute(cot, 'tm', [(2, 0), (3, 1)])  6.19 us
    pallas_call x1, Pallas kernels, shards(): pl.pallas_call(conv_body, out_shape=[jax.ShapeDtypeStruct(wide, BF), jax....  6.01 us
    ppermute x1, waiting for transfers between devices, shards(): from_after = lax.ppermute(to_before, 'bus', down)  4.42 us
    ppermute x1, starting transfers between devices, shards(): from_after = lax.ppermute(to_before, 'bus', down)  4.19 us
    unnamed x16, local copies, waits for them, and re-layouts  3.61 us
    ppermute x1, starting transfers between devices, shards(): before = lax.ppermute(last, 'bus', up)  3.43 us
  transfers between devices with their start and end apart: 13, of which 7 were waited for; matrix products, arithmetic and copies ran while one was open for 3% of the time, Pallas kernels for 10%

profile of v1, /device:TPU:24, one launch (start us, length us, event | category | flops | bytes accessed | tf_op | source)
XLA Modules:
  0.0 74.1 jit_solution(2922612490321833249)
XLA Ops:
  0.7 1.1 %copy-done.1 = bf16[128,16,128]{2,1,0:T(8,128)(2,1)S(1)} copy-done((bf16[128,16,128]{2,1,0:T(8,128)(2,1)S(1)}, bf16[128,16,128]{2,1,0:T(8,128)(2,1)}, u32[]{:S(2)}) %copy-start.1) | copy-done | bytes 524312
  1.7 1.0 %copy-done.3 = bf16[128,16,128]{2,1,0:T(8,128)(2,1)S(1)} copy-done((bf16[128,16,128]{2,1,0:T(8,128)(2,1)S(1)}, bf16[128,16,128]{2,1,0:T(8,128)(2,1)}, u32[]{:S(2)}) %copy-start.3) | copy-done | bytes 524312
  2.8 1.0 %shard_map.102 = (bf16[16,128,128]{2,1,0:T(8,128)(2,1)S(1)}, bf16[16,64,128]{2,1,0:T(8,128)(2,1)S(1)}, bf16[16,64,128]{2,1,0:T(8,128)(2,1)}, bf16[16,128,128]{2,1,0:T(8,128)(2,1)S(1)}) custom-call(bf16[128,16,128]{2,1,0:T(8,128)(2,1)S(1)} %copy-done.3, bf16[128,16,128]{2,1,0:T(8,128)(2,1)S(1)} %copy-done.1), custom_call_target="tpu_custom_call" | custom-call | flops 268435456 | bytes 1048576 | tf_op jit(solution)/shard_map/pallas_call | solution.py:17
  3.8 1.3 %collective-permute-start.3 = (bf16[16,128,128]{2,1,0:T(8,128)(2,1)S(1)}, bf16[16,128,128]{2,1,0:T(8,128)(2,1)S(1)}, u32[]{:S(2)}, u32[]{:S(2)}) collective-permute-start(bf16[16,128,128]{2,1,0:T(8,128)(2,1)S(1)} %get-tuple-element.20.c0_ref), channel_id=1, source_target_pairs={{2,0},{3,1},{6,4},{7,5},{10,8},{11,9},{14,12},{15,13},{18,16},{19,... | collective-permute-start | bytes 1572872 | tf_op jit(solution)/shard_map/ppermute | solution.py:213
  5.0 1.3 %collective-permute-start.2 = (bf16[16,128,128]{2,1,0:T(8,128)(2,1)S(1)}, bf16[16,128,128]{2,1,0:T(8,128)(2,1)S(1)}, u32[]{:S(2)}, u32[]{:S(2)}) collective-permute-start(bf16[16,128,128]{2,1,0:T(8,128)(2,1)S(1)} %get-tuple-element.20.c0_ref), channel_id=1, source_target_pairs={{1,0},{3,2},{5,4},{7,6},{9,8},{11,10},{13,12},{15,14},{17,16},{19,... | collective-permute-start | bytes 1572872 | tf_op jit(solution)/shard_map/ppermute | solution.py:216
  6.3 3.4 %collective-permute-start = (bf16[16,64,128]{2,1,0:T(8,128)(2,1)}, bf16[16,64,128]{2,1,0:T(8,128)(2,1)S(1)}, u32[]{:S(2)}, u32[]{:S(2)}) collective-permute-start(bf16[16,64,128]{2,1,0:T(8,128)(2,1)} %get-tuple-element.18), channel_id=1, source_target_pairs={{0,4},{4,8},{8,12},{12,16},{16,20},{20,24},{24,28},{1,5},{5,9},{9,... | collective-permute-start | bytes 786440 | tf_op jit(solution)/shard_map/ppermute | solution.py:214
  9.8 3.3 %collective-permute-start.1 = (bf16[16,64,128]{2,1,0:T(8,128)(2,1)S(1)}, bf16[16,64,128]{2,1,0:T(8,128)(2,1)S(1)}, u32[]{:S(2)}, u32[]{:S(2)}) collective-permute-start(bf16[16,64,128]{2,1,0:T(8,128)(2,1)S(1)} %get-tuple-element.19), channel_id=1, source_target_pairs={{4,0},{8,4},{12,8},{16,12},{20,16},{24,20},{28,24},{5,1},{9,5},{13... | collective-permute-start | bytes 786440 | tf_op jit(solution)/shard_map/ppermute | solution.py:215
  13.1 6.2 %collective-permute-done.3.c2_ref = bf16[16,128,128]{2,1,0:T(8,128)(2,1)S(1)} collective-permute-done((bf16[16,128,128]{2,1,0:T(8,128)(2,1)S(1)}, bf16[16,128,128]{2,1,0:T(8,128)(2,1)S(1)}, u32[]{:S(2)}, u32[]{:S(2)}) %collective-permute-start.3) | collective-permute-done | bytes 524320 | tf_op jit(solution)/shard_map/ppermute | solution.py:213
  19.3 1.9 %collective-permute-start.4 = (bf16[16,128,128]{2,1,0:T(8,128)(2,1)S(1)}, bf16[16,128,128]{2,1,0:T(8,128)(2,1)}, u32[]{:S(2)}, u32[]{:S(2)}) collective-permute-start(bf16[16,128,128]{2,1,0:T(8,128)(2,1)S(1)} %collective-permute-done.3.c2_ref), channel_id=1, source_target_pairs={{1,0},{0,1},{5,4},{4,5},{9,8},{8,9},{13,12},{12,13},{17,16},{16,17... | collective-permute-start | bytes 1572872 | tf_op jit(solution)/shard_map/ppermute | solution.py:217
  21.2 0.7 subtract_add_fusion
  21.9 0.3 fusion
  22.4 0.8 %fusion.4.taps_ref = f32[128,128]{1,0:T(8,128)S(1)} fusion(bf16[16,4,128]{2,1,0:T(4,128)(2,1)} %bitcast.26), kind=kLoop, calls=%fused_computation.14 | loop fusion | flops 81920 | bytes 81920 | tf_op jit(solution)/shard_map/reshape | solution.py:249
  23.4 0.7 copy-done.5
  24.1 0.8 %copy-done.6 = bf16[128,128]{1,0:T(8,128)(2,1)S(1)} copy-done((bf16[128,128]{1,0:T(8,128)(2,1)S(1)}, bf16[128,128]{1,0:T(8,128)(2,1)}, u32[]{:S(2)}) %copy-start.6) | copy-done | bytes 32792
  24.8 6.0 %shard_map.103 = (bf16[16,128,128]{2,1,0:T(8,128)(2,1)S(1)}, bf16[40,128,256]{2,1,0:T(8,128)(2,1)S(1)}) custom-call(s32[2]{0:T(128)S(1)} %pad_add_fusion.slot_ref, bf16[16,128,128]{2,1,0:T(8,128)(2,1)S(1)} %get-tuple-element.20.c0_ref, bf16[16,128,128]{2,1,0:T(8,128)(2,1)S(1)} %collective-permute-done.2.c1_ref, ...), custom_call_target="tpu_custom_call" | custom-call | flops 2147483648 | bytes 1048576 | tf_op jit(solution)/shard_map/pallas_call | solution.py:227
  30.9 2.3 %shard_map.104 = (bf16[16,128,128]{2,1,0:T(8,128)(2,1)S(1)}, f32[16,128,128]{2,1,0:T(8,128)S(1)}, bf16[16,64,128]{2,1,0:T(8,128)(2,1)S(1)}, bf16[16,64,128]{2,1,0:T(8,128)(2,1)S(1)}, f32[128,128]{1,0:T(8,128)S(1)}) custom-call(bf16[16,128,128]{2,1,0:T(8,128)(2,1)S(1)} %get-tuple-element.17.own_ref, bf16[16,64,128]{2,1,0:T(8,128)(2,1)S(1)} %collective-permute-done.before_ref, ...), custom_call_target="tpu_custom_call" | custom-call | flops 268435456 | bytes 1048576 | tf_op jit(solution)/shard_map/pallas_call | solution.py:17
  33.2 8.3 %shard_map.106 = (f32[128,128]{1,0:T(8,128)S(1)}, f32[128,128]{1,0:T(8,128)S(1)}) custom-call(bf16[16,128,128]{2,1,0:T(8,128)(2,1)S(1)} %get-tuple-element.26.act_ref, bf16[40,128,256]{2,1,0:T(8,128)(2,1)S(1)} %get-tuple-element.27.cross_ref, f32[128,128]{1,0:T(8,128)S(1)} %fusion.4.taps_ref, bf16[128,128]{1,0:T(8,128)(2,1)S(1)} %copy-done.7), custom_call_target="tpu_custom_call" | custom-call | flops 4294967296 | bytes 1048576 | tf_op jit(solution)/shard_map/pallas_call | solution.py:17
  41.5 0.6 collective-permute-start.7
  42.1 0.9 %collective-permute-done.7 = f32[160,128]{1,0:T(8,128)S(1)} collective-permute-done((f32[160,128]{1,0:T(8,128)S(1)}, f32[160,128]{1,0:T(8,128)S(1)}, u32[]{:S(2)}, u32[]{:S(2)}) %collective-permute-start.7) | collective-permute-done | bytes 81952 | tf_op jit(solution)/shard_map/ppermute | solution.py:181
  43.1 4.0 %collective-permute-done.8 = bf16[160,128]{1,0:T(8,128)(2,1)S(1)} collective-permute-done((bf16[160,128]{1,0:T(8,128)(2,1)S(1)}, bf16[160,128]{1,0:T(8,128)(2,1)S(1)}, u32[]{:S(2)}, u32[]{:S(2)}) %collective-permute-start.8) | collective-permute-done | bytes 40992 | tf_op jit(solution)/shard_map/ppermute | solution.py:181
  47.1 0.5 collective-permute-start.9
  47.6 3.5 %collective-permute-done.9 = bf16[160,128]{1,0:T(8,128)(2,1)S(1)} collective-permute-done((bf16[160,128]{1,0:T(8,128)(2,1)S(1)}, bf16[160,128]{1,0:T(8,128)(2,1)S(1)}, u32[]{:S(2)}, u32[]{:S(2)}) %collective-permute-start.9) | collective-permute-done | bytes 40992 | tf_op jit(solution)/shard_map/ppermute | solution.py:181
  51.2 0.3 collective-permute-start.10
  51.5 5.0 %collective-permute-done.10 = bf16[160,128]{1,0:T(8,128)(2,1)S(1)} collective-permute-done((bf16[160,128]{1,0:T(8,128)(2,1)S(1)}, bf16[160,128]{1,0:T(8,128)(2,1)S(1)}, u32[]{:S(2)}, u32[]{:S(2)}) %collective-permute-start.10) | collective-permute-done | bytes 40992 | tf_op jit(solution)/shard_map/ppermute | solution.py:181
  56.5 1.4 %collective-permute-start.11 = (bf16[160,128]{1,0:T(8,128)(2,1)S(1)}, bf16[160,128]{1,0:T(8,128)(2,1)S(1)}, u32[]{:S(2)}, u32[]{:S(2)}) collective-permute-start(bf16[160,128]{1,0:T(8,128)(2,1)S(1)} %add_convert_fusion), channel_id=1, source_target_pairs={{0,4},{4,0},{8,12},{12,8},{16,20},{20,16},{24,28},{28,24},{1,5},{5... | collective-permute-start | bytes 122888 | tf_op jit(solution)/shard_map/ppermute | solution.py:181
  58.0 2.5 %collective-permute-start.5 = (bf16[16,64,128]{2,1,0:T(8,128)(2,1)S(1)}, bf16[16,64,128]{2,1,0:T(8,128)(2,1)S(1)}, u32[]{:S(2)}, u32[]{:S(2)}) collective-permute-start(bf16[16,64,128]{2,1,0:T(8,128)(2,1)S(1)} %get-tuple-element.23), channel_id=1, source_target_pairs={{0,4},{4,8},{8,12},{12,16},{16,20},{20,24},{24,28},{1,5},{5,9},{9,... | collective-permute-start | bytes 786440 | tf_op jit(solution)/shard_map/ppermute | solution.py:246
  60.5 4.2 %collective-permute-start.6 = (bf16[16,64,128]{2,1,0:T(8,128)(2,1)S(1)}, bf16[16,64,128]{2,1,0:T(8,128)(2,1)S(1)}, u32[]{:S(2)}, u32[]{:S(2)}) collective-permute-start(bf16[16,64,128]{2,1,0:T(8,128)(2,1)S(1)} %get-tuple-element.24), channel_id=1, source_target_pairs={{4,0},{8,4},{12,8},{16,12},{20,16},{24,20},{28,24},{5,1},{9,5},{13... | collective-permute-start | bytes 786440 | tf_op jit(solution)/shard_map/ppermute | solution.py:245
  64.8 2.4 %collective-permute-done.5.before_ref = bf16[16,64,128]{2,1,0:T(8,128)(2,1)S(1)} collective-permute-done((bf16[16,64,128]{2,1,0:T(8,128)(2,1)S(1)}, bf16[16,64,128]{2,1,0:T(8,128)(2,1)S(1)}, u32[]{:S(2)}, u32[]{:S(2)}) %collective-permute-start.5) | collective-permute-done | bytes 262176 | tf_op jit(solution)/shard_map/ppermute | solution.py:246
  67.2 4.4 %collective-permute-done.6.after_ref = bf16[16,64,128]{2,1,0:T(8,128)(2,1)S(1)} collective-permute-done((bf16[16,64,128]{2,1,0:T(8,128)(2,1)S(1)}, bf16[16,64,128]{2,1,0:T(8,128)(2,1)S(1)}, u32[]{:S(2)}, u32[]{:S(2)}) %collective-permute-start.6) | collective-permute-done | bytes 262176 | tf_op jit(solution)/shard_map/ppermute | solution.py:245
  71.6 1.1 %shard_map.105 = bf16[128,16,128]{2,1,0:T(8,128)(2,1)} custom-call(f32[16,128,128]{2,1,0:T(8,128)S(1)} %get-tuple-element.22.spread_ref, bf16[16,64,128]{2,1,0:T(8,128)(2,1)S(1)} %collective-permute-done.5.before_ref, bf16[16,64,128]{2,1,0:T(8,128)(2,1)S(1)} %collective-permute-done.6.after_ref, bf16[128,16,128]{2,1,0:T(8,128)(2,1)S(1)} %copy-done.2), custom_call_target="tpu_custom_call" | custom-call | flops 268435456 | bytes 1048576 | tf_op jit(solution)/shard_map/pallas_call | solution.py:17
  72.8 0.7 fusion.8
  73.5 0.6 slice.19
  (32 shorter events, 0.7 us)
Async XLA Ops:
  0.6 21.3 %copy-start = (bf16[2,8,64,64]{3,2,1,0:T(8,128)(2,1)S(1)}, bf16[2,8,64,64]{3,2,1,0:T(8,128)(2,1)}, u32[]{:S(2)}) copy-start(bf16[2,8,64,64]{3,2,1,0:T(8,128)(2,1)} %param.8) | copy-start | bytes 393220
  0.6 1.1 %copy-start.1 = (bf16[128,16,128]{2,1,0:T(8,128)(2,1)S(1)}, bf16[128,16,128]{2,1,0:T(8,128)(2,1)}, u32[]{:S(2)}) copy-start(bf16[128,16,128]{2,1,0:T(8,128)(2,1)} %cot_ref.3) | copy-start | bytes 1572868
  1.7 1.0 %copy-start.3 = (bf16[128,16,128]{2,1,0:T(8,128)(2,1)S(1)}, bf16[128,16,128]{2,1,0:T(8,128)(2,1)}, u32[]{:S(2)}) copy-start(bf16[128,16,128]{2,1,0:T(8,128)(2,1)} %feat_ref.1) | copy-start | bytes 1572868
  3.8 15.5 %collective-permute-start.3 = (bf16[16,128,128]{2,1,0:T(8,128)(2,1)S(1)}, bf16[16,128,128]{2,1,0:T(8,128)(2,1)S(1)}, u32[]{:S(2)}, u32[]{:S(2)}) collective-permute-start(bf16[16,128,128]{2,1,0:T(8,128)(2,1)S(1)} %get-tuple-element.20.c0_ref), channel_id=1, source_target_pairs={{2,0},{3,1},{6,4},{7,5},{10,8},{11,9},{14,12},{15,13},{18,16},{19,... | collective-permute-start | bytes 1572872 | tf_op jit(solution)/shard_map/ppermute | solution.py:213
  5.0 18.3 %collective-permute-start.2 = (bf16[16,128,128]{2,1,0:T(8,128)(2,1)S(1)}, bf16[16,128,128]{2,1,0:T(8,128)(2,1)S(1)}, u32[]{:S(2)}, u32[]{:S(2)}) collective-permute-start(bf16[16,128,128]{2,1,0:T(8,128)(2,1)S(1)} %get-tuple-element.20.c0_ref), channel_id=1, source_target_pairs={{1,0},{3,2},{5,4},{7,6},{9,8},{11,10},{13,12},{15,14},{17,16},{19,... | collective-permute-start | bytes 1572872 | tf_op jit(solution)/shard_map/ppermute | solution.py:216
  6.3 24.5 %collective-permute-start = (bf16[16,64,128]{2,1,0:T(8,128)(2,1)}, bf16[16,64,128]{2,1,0:T(8,128)(2,1)S(1)}, u32[]{:S(2)}, u32[]{:S(2)}) collective-permute-start(bf16[16,64,128]{2,1,0:T(8,128)(2,1)} %get-tuple-element.18), channel_id=1, source_target_pairs={{0,4},{4,8},{8,12},{12,16},{16,20},{20,24},{24,28},{1,5},{5,9},{9,... | collective-permute-start | bytes 786440 | tf_op jit(solution)/shard_map/ppermute | solution.py:214
  9.8 21.1 %collective-permute-start.1 = (bf16[16,64,128]{2,1,0:T(8,128)(2,1)S(1)}, bf16[16,64,128]{2,1,0:T(8,128)(2,1)S(1)}, u32[]{:S(2)}, u32[]{:S(2)}) collective-permute-start(bf16[16,64,128]{2,1,0:T(8,128)(2,1)S(1)} %get-tuple-element.19), channel_id=1, source_target_pairs={{4,0},{8,4},{12,8},{16,12},{20,16},{24,20},{28,24},{5,1},{9,5},{13... | collective-permute-start | bytes 786440 | tf_op jit(solution)/shard_map/ppermute | solution.py:215
  19.3 4.0 %collective-permute-start.4 = (bf16[16,128,128]{2,1,0:T(8,128)(2,1)S(1)}, bf16[16,128,128]{2,1,0:T(8,128)(2,1)}, u32[]{:S(2)}, u32[]{:S(2)}) collective-permute-start(bf16[16,128,128]{2,1,0:T(8,128)(2,1)S(1)} %collective-permute-done.3.c2_ref), channel_id=1, source_target_pairs={{1,0},{0,1},{5,4},{4,5},{9,8},{8,9},{13,12},{12,13},{17,16},{16,17... | collective-permute-start | bytes 1572872 | tf_op jit(solution)/shard_map/ppermute | solution.py:217
  23.3 7.5 %copy-start.4 = (bf16[128,128]{1,0:T(8,128)(2,1)S(1)}, bf16[128,128]{1,0:T(8,128)(2,1)}, u32[]{:S(2)}) copy-start(bf16[128,128]{1,0:T(8,128)(2,1)} %wg_ref.1) | copy-start | bytes 98308
  23.4 0.7 copy-start.5
  24.1 0.8 %copy-start.6 = (bf16[128,128]{1,0:T(8,128)(2,1)S(1)}, bf16[128,128]{1,0:T(8,128)(2,1)}, u32[]{:S(2)}) copy-start(bf16[128,128]{1,0:T(8,128)(2,1)} %wout_ref.3) | copy-start | bytes 98308
  24.8 8.3 %copy-start.7 = (bf16[128,128]{1,0:T(8,128)(2,1)S(1)}, bf16[128,128]{1,0:T(8,128)(2,1)}, u32[]{:S(2)}) copy-start(bf16[128,128]{1,0:T(8,128)(2,1)} %wout_ref.3) | copy-start | bytes 98308
  33.2 38.5 %copy-start.2 = (bf16[128,16,128]{2,1,0:T(8,128)(2,1)S(1)}, bf16[128,16,128]{2,1,0:T(8,128)(2,1)}, u32[]{:S(2)}) copy-start(bf16[128,16,128]{2,1,0:T(8,128)(2,1)} %cot_ref.3) | copy-start | bytes 1572868
  41.5 1.5 %collective-permute-start.7 = (f32[160,128]{1,0:T(8,128)S(1)}, f32[160,128]{1,0:T(8,128)S(1)}, u32[]{:S(2)}, u32[]{:S(2)}) collective-permute-start(f32[160,128]{1,0:T(8,128)S(1)} %dynamic-slice_bitcast_fusion), channel_id=1, source_target_pairs={{0,1},{1,0},{2,3},{3,2},{4,5},{5,4},{6,7},{7,6},{8,9},{9,8},{10,11... | collective-permute-start | bytes 245768 | tf_op jit(solution)/shard_map/ppermute | solution.py:181
  43.0 4.1 %collective-permute-start.8 = (bf16[160,128]{1,0:T(8,128)(2,1)S(1)}, bf16[160,128]{1,0:T(8,128)(2,1)S(1)}, u32[]{:S(2)}, u32[]{:S(2)}) collective-permute-start(bf16[160,128]{1,0:T(8,128)(2,1)S(1)} %fusion.3), channel_id=1, source_target_pairs={{0,2},{1,3},{2,0},{3,1},{4,6},{5,7},{6,4},{7,5},{8,10},{9,11},{10,... | collective-permute-start | bytes 122888 | tf_op jit(solution)/shard_map/ppermute | solution.py:181
  47.1 4.1 %collective-permute-start.9 = (bf16[160,128]{1,0:T(8,128)(2,1)S(1)}, bf16[160,128]{1,0:T(8,128)(2,1)S(1)}, u32[]{:S(2)}, u32[]{:S(2)}) collective-permute-start(bf16[160,128]{1,0:T(8,128)(2,1)S(1)} %add_convert_fusion.2), channel_id=1, source_target_pairs={{0,8},{4,12},{8,0},{12,4},{16,24},{20,28},{24,16},{28,20},{1,9},{5... | collective-permute-start | bytes 122888 | tf_op jit(solution)/shard_map/ppermute | solution.py:181
  51.2 5.3 %collective-permute-start.10 = (bf16[160,128]{1,0:T(8,128)(2,1)S(1)}, bf16[160,128]{1,0:T(8,128)(2,1)S(1)}, u32[]{:S(2)}, u32[]{:S(2)}) collective-permute-start(bf16[160,128]{1,0:T(8,128)(2,1)S(1)} %add_convert_fusion.1), channel_id=1, source_target_pairs={{0,16},{4,20},{8,24},{12,28},{16,0},{20,4},{24,8},{28,12},{1,17},{... | collective-permute-start | bytes 122888 | tf_op jit(solution)/shard_map/ppermute | solution.py:181
  56.5 8.2 %collective-permute-start.11 = (bf16[160,128]{1,0:T(8,128)(2,1)S(1)}, bf16[160,128]{1,0:T(8,128)(2,1)S(1)}, u32[]{:S(2)}, u32[]{:S(2)}) collective-permute-start(bf16[160,128]{1,0:T(8,128)(2,1)S(1)} %add_convert_fusion), channel_id=1, source_target_pairs={{0,4},{4,0},{8,12},{12,8},{16,20},{20,16},{24,28},{28,24},{1,5},{5... | collective-permute-start | bytes 122888 | tf_op jit(solution)/shard_map/ppermute | solution.py:181
  58.0 9.3 %collective-permute-start.5 = (bf16[16,64,128]{2,1,0:T(8,128)(2,1)S(1)}, bf16[16,64,128]{2,1,0:T(8,128)(2,1)S(1)}, u32[]{:S(2)}, u32[]{:S(2)}) collective-permute-start(bf16[16,64,128]{2,1,0:T(8,128)(2,1)S(1)} %get-tuple-element.23), channel_id=1, source_target_pairs={{0,4},{4,8},{8,12},{12,16},{16,20},{20,24},{24,28},{1,5},{5,9},{9,... | collective-permute-start | bytes 786440 | tf_op jit(solution)/shard_map/ppermute | solution.py:246
  60.5 11.1 %collective-permute-start.6 = (bf16[16,64,128]{2,1,0:T(8,128)(2,1)S(1)}, bf16[16,64,128]{2,1,0:T(8,128)(2,1)S(1)}, u32[]{:S(2)}, u32[]{:S(2)}) collective-permute-start(bf16[16,64,128]{2,1,0:T(8,128)(2,1)S(1)} %get-tuple-element.24), channel_id=1, source_target_pairs={{4,0},{8,4},{12,8},{16,12},{20,16},{24,20},{28,24},{5,1},{9,5},{13... | collective-permute-start | bytes 786440 | tf_op jit(solution)/shard_map/ppermute | solution.py:245
  64.7 8.0 %collective-permute-start.12 = (f32[160,128]{1,0:T(8,128)S(1)}, f32[160,128]{1,0:T(8,128)S(1)}, u32[]{:S(2)}, u32[]{:S(2)}) collective-permute-start(f32[160,128]{1,0:T(8,128)S(1)} %convert_add_fusion), channel_id=1, source_target_pairs={{0,1},{1,0},{2,3},{3,2},{4,5},{5,4},{6,7},{7,6},{8,9},{9,8},{10,11... | collective-permute-start | bytes 245768 | tf_op jit(solution)/shard_map/ppermute | solution.py:181

commit v2 on v1

v2 whole, which is shorter than its diff:
```python
import functools
import math

import jax
import jax.numpy as jnp
from jax import lax
from jax.experimental import pallas as pl
from jax.experimental.pallas import tpu as pltpu
from jax.sharding import PartitionSpec as P

BF = jnp.bfloat16
F32 = jnp.float32
VMEM = pl.BlockSpec(memory_space=pltpu.VMEM)
LIMIT = 16 << 20


def call(body, outs, *args, scratch=(), far=(), cost=1, kept=None):
    specs = [VMEM] * len(args)
    results = [VMEM] * len(outs)
    args = list(args)
    aliases = {}
    if kept is not None:
        results[kept[1]] = pl.BlockSpec(memory_space=pl.ANY)
        if kept[0] is not None:
            specs[kept[0]] = pl.BlockSpec(memory_space=pl.ANY)
            aliases = {kept[0]: kept[1]}
    for i in far:
        specs[i] = pl.BlockSpec(memory_space=pltpu.HBM)
        args[i] = pltpu.with_memory_space_constraint(args[i], pltpu.HBM)
    return pl.pallas_call(
        body,
        out_shape=[jax.ShapeDtypeStruct(shape, dtype) for shape, dtype in outs],
        in_specs=specs,
        out_specs=results,
        input_output_aliases=aliases,
        scratch_shapes=list(scratch),
        compiler_params=pltpu.CompilerParams(vmem_limit_bytes=LIMIT),
        cost_estimate=pl.CostEstimate(flops=cost, bytes_accessed=1, transcendentals=0),
    )(*args)


def dot(left, right, dims=((1,), (0,))):
    return lax.dot_general(left, right, (dims, ((), ())), preferred_element_type=F32)


def load_all(sems, pairs):
    copies = [
        pltpu.make_async_copy(source, target, sems.at[i])
        for i, (source, target) in enumerate(pairs)
    ]
    for copy in copies:
        copy.start()
    return copies


def split_body(source_ref, own_ref, near_ref, far_ref, feat_ref, sems):
    rows = feat_ref.shape[0]
    half = near_ref.shape[1]
    odd = lax.axis_index("bus") & 1
    for copy in load_all(sems, [(source_ref, feat_ref)]):
        copy.wait()
    for start in range(0, rows, 16):
        part = jnp.swapaxes(feat_ref[start : start + 16].astype(F32), 0, 1).astype(BF)
        own_ref[:, start : start + 16] = part
    low, high = pl.multiple_of(odd * half, half), pl.multiple_of((1 - odd) * half, half)
    near_ref[...] = own_ref[:, pl.ds(high, half)]
    far_ref[...] = own_ref[:, pl.ds(low, half)]


def take_block(block_ref, wout, steady, part, conv):
    steps, rows, chans = steady.shape
    for start in range(0, rows, 16):
        steady[:, start : start + 16] = jnp.swapaxes(
            block_ref[start : start + 16].astype(F32), 0, 1
        ).astype(BF)
    for s in range(0, steps, 4):
        block = steady[s : s + 4].reshape(4 * rows, chans)
        conv[s : s + 4] = dot(block, wout, ((1,), (1,))).astype(BF).reshape(4, rows, chans)
    for s in range(0, steps, 2):
        part[s // 2, :, 0:rows] = steady[s].T
        part[s // 2, :, rows : 2 * rows] = steady[s + 1].T


def place_part(part, cross_ref, slot, sem):
    size = part.shape[0]
    copy = pltpu.make_async_copy(part, cross_ref.at[pl.ds(slot * size, size)], sem)
    copy.start()
    return copy


def add_lags(sums, conv, lags_ref, base, where, causal):
    steps = conv.shape[0]
    for t in range(steps):
        value = conv[t, where, :].astype(F32)
        for s in range(steps):
            if causal and t < s:
                continue
            tap = lags_ref[base + (t - s)]
            sums[s][0] += tap * value[:8]
            sums[s][1] += tap * value[8:]


def early_body(
    ids_src, coup_src, cot_src, taps_src, wout_src, wg_src, near_ref,
    sum_ref, cross_ref, mix_ref, mixt_ref, steady_ref, taps_ref, wout_ref, wg_ref, lags_ref,
    part, conv, other, other_part, other_conv, dense, coup_ref, cot_ref, ids_ref, sems,
):
    copies = load_all(
        sems,
        [
            (cot_src, cot_ref), (wout_src, wout_ref), (taps_src, taps_ref),
            (coup_src, coup_ref), (wg_src, wg_ref), (ids_src, ids_ref),
        ],
    )
    for copy in copies:
        copy.wait()
    rows, steps, chans = cot_ref.shape
    blocks, slots, half = coup_ref.shape[:3]
    bus = lax.axis_index("bus")
    first = bus * blocks - 1
    turned = (bus & 1) == 0
    odd = lax.axis_index("tm") & 1
    take_block(cot_ref, wout_ref[...], steady_ref, part, conv)
    sent = [place_part(part, cross_ref, 0, sems.at[6])]
    take_block(near_ref, wout_ref[...], other, other_part, other_conv)
    sent.append(place_part(other_part, cross_ref, 1 + 2 * odd, sems.at[7]))
    taps = taps_ref[...].astype(F32)
    for lag in range(taps_ref.shape[0]):
        lags_ref[lag] = jnp.broadcast_to(taps[lag : lag + 1], (8, chans))

    def tile(index, carry):
        where = pl.ds(pl.multiple_of(index * 16, 16), 16)
        sums = [[jnp.zeros((8, chans), F32)] * 2 for _ in range(steps)]
        add_lags(sums, conv, lags_ref, 0, where, True)
        add_lags(sums, other_conv, lags_ref, steps, where, False)
        for s in range(steps):
            sum_ref[s, where, :] = jnp.concatenate(sums[s], axis=0)
        return carry

    lax.fori_loop(0, rows // 16, tile, 0)
    dense[...] = jnp.zeros_like(dense)
    for i in range(blocks):
        for k in range(slots):
            place = ids_ref[i, k] - first
            edge = (place == 0) | (place == blocks + 1)
            place = jnp.where(turned & edge, blocks + 1 - place, place)
            dense[i, place] += coup_ref[i, k].astype(F32)
    full = jnp.concatenate(
        [
            jnp.concatenate([dense[i, j] for j in range(blocks + 2)], axis=1)
            for i in range(blocks)
        ],
        axis=0,
    )
    mix_ref[...] = full.astype(BF)
    mixt_ref[...] = full.T.astype(BF)
    for copy in sent:
        copy.wait()


def add_body(last, sum_ref, crossed_ref, block_ref, lags_ref, wout_ref, out_ref, cross_ref, steady, part, conv, sems):
    steps, rows, chans = conv.shape
    slot = 3 - 2 * (lax.axis_index("tm") & 1) if last else 2
    take_block(block_ref, wout_ref[...], steady, part, conv)
    sent = place_part(part, cross_ref, slot, sems.at[0])

    def tile(index, carry):
        where = pl.ds(pl.multiple_of(index * 16, 16), 16)
        sums = [[sum_ref[s, where, :][:8], sum_ref[s, where, :][8:]] for s in range(steps)]
        add_lags(sums, conv, lags_ref, slot * steps, where, False)
        for s in range(steps):
            out_ref[s, where, :] = jnp.concatenate(sums[s], axis=0).astype(out_ref.dtype)
        return carry

    lax.fori_loop(0, rows // 16, tile, 0)
    sent.wait()


def forward_body(
    own_ref, before_ref, after_ref, mix_ref, wg_ref, act_ref, slope_ref, mixed_ref
):
    steps, rows, chans = own_ref.shape
    group = 4
    mix, wg = mix_ref[...], wg_ref[...]
    for s in range(0, steps, group):
        ext = jnp.concatenate(
            [
                jnp.concatenate([before_ref[t], own_ref[t], after_ref[t]], axis=0)
                for t in range(s, s + group)
            ],
            axis=1,
        )
        mixed = dot(mix, ext).astype(BF)
        mixed = jnp.concatenate(
            [mixed[:, t * chans : (t + 1) * chans] for t in range(group)], axis=0
        )
        mixed_ref[s : s + group] = mixed.reshape(group, rows, chans)
        pre = dot(mixed, wg)
        gate = 1.0 / (1.0 + jnp.exp(-pre))
        act_ref[s : s + group] = (pre * gate).astype(BF).reshape(group, rows, chans)
        slope = gate * (1.0 + pre * (1.0 - gate))
        slope_ref[s : s + group] = slope.reshape(group, rows, chans)


def backward_body(
    grad_ref, slope_ref, mixed_ref, mixt_ref, wg_ref, spread_ref, down_ref, up_ref, graph_ref
):
    steps, rows, chans = grad_ref.shape
    half = down_ref.shape[1]
    group = 4
    mixt, wg = mixt_ref[...], wg_ref[...]
    graph = jnp.zeros((chans, chans), F32)
    for s in range(0, steps, group):
        grad = grad_ref[s : s + group].astype(F32) * slope_ref[s : s + group]
        grad_pre = grad.astype(BF).reshape(group * rows, chans)
        mixed = mixed_ref[s : s + group].reshape(group * rows, chans)
        graph += dot(mixed, grad_pre, ((0,), (0,)))
        grad_mixed = dot(grad_pre, wg, ((1,), (1,))).astype(BF)
        grad_mixed = jnp.concatenate(
            [grad_mixed[t * rows : (t + 1) * rows] for t in range(group)], axis=1
        )
        spread = dot(mixt, grad_mixed)
        for t in range(group):
            part = spread[:, t * chans : (t + 1) * chans]
            down_ref[s + t] = part[:half].astype(BF)
            spread_ref[s + t] = part[half : half + rows]
            up_ref[s + t] = part[half + rows :].astype(BF)
    graph_ref[...] = graph


def lag_body(act_ref, cross_ref, taps_ref, wout_ref, graph_ref, keep_ref, send_ref, stack, pack):
    steps, rows, chans = act_ref.shape
    pairs = cross_ref.shape[0]
    group = steps // 2
    zero = jnp.zeros((rows, chans), BF)
    for i in range(group + 1):
        s = 2 * i
        if s < steps:
            stack[i, 0:rows, 0:chans] = act_ref[s]
            stack[i, rows : 2 * rows, 0:chans] = act_ref[s + 1]
            stack[i, rows : 2 * rows, chans : 2 * chans] = act_ref[s]
        else:
            stack[i, 0:rows, 0:chans] = zero
        stack[i, 0:rows, chans : 2 * chans] = act_ref[s - 1] if s > 0 else zero
    weight = wout_ref[...].astype(F32).T
    taps = taps_ref[...].astype(F32)
    out = jnp.zeros((chans, chans), F32)
    found = []
    for at in range(0, pairs, group):
        total = [None] * group
        for i in range(group + 1):
            count = min(group, pairs - at - i)
            if count <= 0:
                continue
            depth = 2 * rows if i < group else rows
            left = cross_ref[at + i : at + i + count, :, 0:depth].reshape(count * rows, depth)
            part = dot(left, stack[i, 0:depth])
            for g in range(count):
                piece = part[g * rows : (g + 1) * rows]
                total[g] = piece if total[g] is None else total[g] + piece
        for g in range(group):
            for side in range(2):
                lag = 2 * (at + g) + side
                part = total[g][:, side * chans : (side + 1) * chans]
                out += part * taps[lag : lag + 1]
                found.append(jnp.sum(part * weight, axis=0, keepdims=True))
    pack[0:chans] = graph_ref[...]
    pack[chans : 2 * chans] = out.T
    pack[2 * chans :] = jnp.concatenate(found, axis=0)
    odd = lax.axis_index("tm") & 1
    size = keep_ref.shape[0]
    keep_ref[...] = pack[pl.ds(pl.multiple_of(odd * size, size), size)]
    send_ref[...] = pack[pl.ds(pl.multiple_of((1 - odd) * size, size), size)]


def fold_body(low_bus, spread_ref, edge_ref, out_ref):
    half = edge_ref.shape[1]
    odd = lax.axis_index("bus") & 1
    at = pl.multiple_of((odd if low_bus else 1 - odd) * half, half)
    rest = pl.multiple_of((1 - odd if low_bus else odd) * half, half)
    for s in range(spread_ref.shape[0]):
        out_ref[s, pl.ds(rest, half)] = spread_ref[s, pl.ds(rest, half)]
        out_ref[s, pl.ds(at, half)] = spread_ref[s, pl.ds(at, half)] + edge_ref[s].astype(F32)


def final_body(spread_ref, even_ref, cot_ref, out_ref, sum_ref):
    rows = spread_ref.shape[1]
    half = even_ref.shape[1]
    odd = lax.axis_index("bus") & 1
    for start in range(0, rows, 16):
        sum_ref[:, start : start + 16] = spread_ref[:, start : start + 16] + cot_ref[
            :, start : start + 16
        ].astype(F32)
    at = pl.multiple_of((1 - odd) * half, half)
    sum_ref[:, pl.ds(at, half)] += even_ref[...].astype(F32)
    for start in range(0, rows, 16):
        out_ref[start : start + 16] = jnp.swapaxes(sum_ref[:, start : start + 16], 0, 1).astype(BF)


def pause_body(value_ref, last_ref, out_ref):
    out_ref[...] = value_ref[0:8] + last_ref[...]


def finish_body(scale, mine_ref, other_ref, mark_ref, graph_ref, out_ref, taps_ref, pack):
    odd = lax.axis_index("tm") & 1
    size = mine_ref.shape[0]
    chans = graph_ref.shape[0]
    pack[pl.ds(pl.multiple_of(odd * size, size), size)] = mine_ref[...] * scale
    pack[pl.ds(pl.multiple_of((1 - odd) * size, size), size)] = other_ref[...] * scale
    graph_ref[...] = pack[0:chans]
    out_ref[...] = pack[chans : 2 * chans]
    taps_ref[...] = pack[2 * chans :]


def swap(value, axis, distance):
    size = lax.axis_size(axis)
    return lax.ppermute(value, axis, [(i, i ^ distance) for i in range(size)])


def pause(value, received, mark):
    (mark,) = call(pause_body, [(mark.shape, F32)], value, mark, cost=1 << 36)
    return lax.optimization_barrier((received, mark))


def shards(features, couplings, neighbors, w_graph, kernel_taps, w_out, cotangent):
    bus, tm = lax.axis_size("bus"), lax.axis_size("tm")
    rows, steps, chans = features.shape
    blocks, slots, half = couplings.shape[:3]
    total = kernel_taps.shape[0]
    evens = [(i, i ^ 1) for i in range(bus)]
    odds = [(i, i + 1) for i in range(1, bus - 1, 2)] + [(i + 1, i) for i in range(1, bus - 1, 2)]
    wide = (steps, rows, chans)
    edge = (steps, half, chans)
    square = (chans, chans)

    own, even_edge, odd_edge = call(
        split_body, [(wide, BF), (edge, BF), (edge, BF)], features,
        scratch=[pltpu.VMEM(features.shape, BF), pltpu.SemaphoreType.DMA((1,))], far=[0],
    )
    near = lax.ppermute(cotangent, "tm", [(1, 0), (3, 2)])
    odd_edge = lax.ppermute(odd_edge, "bus", odds)
    even_edge = lax.ppermute(even_edge, "bus", evens)
    far = lax.ppermute(cotangent, "tm", [(2, 0), (3, 1)])

    pairs = total // 2
    crossing = (pairs, chans, 2 * rows)
    ext = rows + 2 * half
    part = pltpu.VMEM((steps // 2, chans, 2 * rows), BF)
    sums, crossed, mix, mixt, steady, taps, wout, wg, lags = call(
        early_body,
        [
            (wide, F32), (crossing, BF), ((rows, ext), BF), ((ext, rows), BF), (wide, BF),
            (kernel_taps.shape, BF), (square, BF), (square, BF), ((total, 8, chans), F32),
        ],
        neighbors, couplings, cotangent, kernel_taps, w_out, w_graph, near,
        scratch=[
            part, pltpu.VMEM(wide, BF), pltpu.VMEM(wide, BF), part, pltpu.VMEM(wide, BF),
            pltpu.VMEM((blocks, blocks + 2, half, half), F32),
            pltpu.VMEM(couplings.shape, BF),
            pltpu.VMEM(cotangent.shape, BF),
            pltpu.SMEM(neighbors.shape, jnp.int32),
            pltpu.SemaphoreType.DMA((8,)),
        ],
        far=range(6), kept=(None, 1),
    )

    def add_block(last, dtype, sums, crossed, block):
        return call(
            functools.partial(add_body, last), [(wide, dtype), (crossing, BF)],
            sums, crossed, block, lags, wout,
            scratch=[
                pltpu.VMEM(wide, BF), part, pltpu.VMEM(wide, BF), pltpu.SemaphoreType.DMA((1,))
            ],
            kept=(1, 1),
        )

    far, sums = lax.optimization_barrier((far, sums))
    swapped = lax.ppermute(far, "tm", [(1, 0), (0, 1)])
    sums, crossed = add_block(False, F32, sums, crossed, far)
    even_edge, odd_edge, sums = lax.optimization_barrier((even_edge, odd_edge, sums))
    act, slope, mixed = call(
        forward_body, [(wide, BF), (wide, F32), (wide, BF)], own, even_edge, odd_edge, mix, wg,
        cost=1 << 36,
    )
    swapped, act = lax.optimization_barrier((swapped, act))
    grad_act, crossed = add_block(True, BF, sums, crossed, swapped)
    spread, even_grad, odd_grad, part_graph = call(
        backward_body,
        [(wide, F32), (edge, BF), (edge, BF), (square, F32)],
        grad_act, slope, mixed, mixt, wg,
    )

    size = (2 * chans + total) // 2
    keep, send = call(
        lag_body, [((size, chans), F32), ((size, chans), F32)],
        act, crossed, taps, wout, part_graph,
        scratch=[
            pltpu.VMEM((steps // 2 + 1, 2 * rows, 2 * chans), BF),
            pltpu.VMEM((2 * size, chans), F32),
        ],
    )
    mark = send[0:8]
    keep = keep + swap(send, "tm", 1)
    hops = [("tm", 1 << bit) for bit in range(1, tm.bit_length() - 1)]
    hops += [("bus", 1 << bit) for bit in range(1, bus.bit_length() - 1)] + [("bus", 1)]
    odd_grad = lax.ppermute(odd_grad, "bus", odds)
    even_grad = lax.ppermute(even_grad, "bus", evens)
    for place, (axis, distance) in enumerate(hops):
        sent = keep.astype(BF)
        received = swap(sent, axis, distance)
        if place == 1:
            (spread,) = call(
                functools.partial(fold_body, True), [(wide, F32)], spread, odd_grad, cost=1 << 30
            )
            spread, mark = lax.optimization_barrier((spread, mark))
            received, mark = pause(keep, received, mark)
        if place == len(hops) - 2:
            (grad_features,) = call(
                final_body, [(features.shape, BF)], spread, even_grad, steady,
                scratch=[pltpu.VMEM(wide, F32)], cost=1 << 36,
            )
            received, grad_features = lax.optimization_barrier((received, grad_features))
        keep = sent.astype(F32) + received.astype(F32)
    other = swap(keep, "tm", 1)
    scale = 1.0 / math.sqrt(bus * rows * steps * tm)
    grad_graph, grad_out, grad_taps = call(
        functools.partial(finish_body, scale),
        [(square, F32), (square, F32), ((total, chans), F32)],
        keep, other, mark,
        scratch=[pltpu.VMEM((2 * size, chans), F32)],
    )
    return grad_features, grad_graph, grad_out, grad_taps


def solution(mesh):
    return jax.shard_map(
        shards,
        mesh=mesh,
        in_specs=(
            P("bus", "tm", None),
            P("bus", None, None, None),
            P("bus", None),
            P(),
            P(),
            P(),
            P("bus", "tm", None),
        ),
        out_specs=(P("bus", "tm", None), P(), P(), P()),
        check_vma=False,
    )
```

time: 74.7 us -> 57.9 us (0.78)
  the two profiles are of different devices: /device:TPU:24 before, /device:TPU:0 now
where the time goes in v2:
time: 57.9 us; the launch traced here: 57.7 us
  starting transfers between devices  22.1 us (38%)
  Pallas kernels  18 us (31%)
  waiting for transfers between devices  16.7 us (29%)
  between operations  0.81 us (1%)
    pallas_call x11, Pallas kernels, call(): pl.pallas_call(body, out_shape=[jax.ShapeDtypeStruct(shape, dtype) for sh...  18 us
    ppermute x6, waiting for transfers between devices, swap(): return lax.ppermute(value, axis, [(i, i ^ distance) for i in range(size)])  9.74 us
    ppermute x6, starting transfers between devices, swap(): return lax.ppermute(value, axis, [(i, i ^ distance) for i in range(size)])  7.23 us
    ppermute x1, waiting for transfers between devices, shards(): far = lax.ppermute(cotangent, 'tm', [(2, 0), (3, 1)])  5.93 us
    ppermute x1, starting transfers between devices, shards(): even_grad = lax.ppermute(even_grad, 'bus', evens)  5.78 us
    ppermute x1, starting transfers between devices, shards(): even_edge = lax.ppermute(even_edge, 'bus', evens)  3.03 us
    ppermute x1, starting transfers between devices, shards(): swapped = lax.ppermute(far, 'tm', [(1, 0), (0, 1)])  2.11 us
    ppermute x1, starting transfers between devices, shards(): near = lax.ppermute(cotangent, 'tm', [(1, 0), (3, 2)])  1.29 us
  transfers between devices with their start and end apart: 13, of which 7 were waited for; matrix products, arithmetic and copies ran while one was open for 0% of the time, Pallas kernels for 17%

profile of v2, /device:TPU:0, one launch (start us, length us, event | category | flops | bytes accessed | tf_op | source)
XLA Modules:
  0.0 57.7 jit_solution(9157800667432920697)
XLA Ops:
  0.6 1.3 %collective-permute-start.1 = (bf16[128,16,128]{2,1,0:T(8,128)(2,1)}, bf16[128,16,128]{2,1,0:T(8,128)(2,1)S(1)}, u32[]{:S(2)}, u32[]{:S(2)}) collective-permute-start(bf16[128,16,128]{2,1,0:T(8,128)(2,1)} %cot_src.1), channel_id=1, source_target_pairs={{1,0},{3,2},{5,4},{7,6},{9,8},{11,10},{13,12},{15,14},{17,16},{19,... | collective-permute-start | bytes 1572872 | tf_op jit(solution)/shard_map/ppermute | solution.py:340
  1.9 1.3 %collective-permute-start = (bf16[128,16,128]{2,1,0:T(8,128)(2,1)}, bf16[128,16,128]{2,1,0:T(8,128)(2,1)S(1)}, u32[]{:S(2)}, u32[]{:S(2)}) collective-permute-start(bf16[128,16,128]{2,1,0:T(8,128)(2,1)} %cot_src.1), channel_id=1, source_target_pairs={{2,0},{3,1},{6,4},{7,5},{10,8},{11,9},{14,12},{15,13},{18,16},{19,... | collective-permute-start | bytes 1572872 | tf_op jit(solution)/shard_map/ppermute | solution.py:343
  3.2 1.4 %shard_map.103 = (bf16[16,128,128]{2,1,0:T(8,128)(2,1)S(1)}, bf16[16,64,128]{2,1,0:T(8,128)(2,1)S(1)}, bf16[16,64,128]{2,1,0:T(8,128)(2,1)S(1)}) custom-call(bf16[128,16,128]{2,1,0:T(8,128)(2,1)} %source_ref.1), custom_call_target="tpu_custom_call" | custom-call | flops 1 | bytes 1 | tf_op jit(solution)/shard_map/pallas_call | solution.py:30
  4.6 3.0 %collective-permute-start.3 = (bf16[16,64,128]{2,1,0:T(8,128)(2,1)S(1)}, bf16[16,64,128]{2,1,0:T(8,128)(2,1)S(1)}, u32[]{:S(2)}, u32[]{:S(2)}) collective-permute-start(bf16[16,64,128]{2,1,0:T(8,128)(2,1)S(1)} %get-tuple-element.48), channel_id=1, source_target_pairs={{0,4},{4,0},{8,12},{12,8},{16,20},{20,16},{24,28},{28,24},{1,5},{5... | collective-permute-start | bytes 786440 | tf_op jit(solution)/shard_map/ppermute | solution.py:342
  7.6 0.7 %collective-permute-start.4 = (bf16[16,64,128]{2,1,0:T(8,128)(2,1)S(1)}, bf16[16,64,128]{2,1,0:T(8,128)(2,1)S(1)}, u32[]{:S(2)}, u32[]{:S(2)}) collective-permute-start(bf16[16,64,128]{2,1,0:T(8,128)(2,1)S(1)} %get-tuple-element.49), channel_id=1, source_target_pairs={{4,8},{12,16},{20,24},{8,4},{16,12},{24,20},{5,9},{13,17},{21,25},... | collective-permute-start | bytes 786440 | tf_op jit(solution)/shard_map/ppermute | solution.py:341
  8.3 0.0 collective-permute-done.1.near_ref
  8.3 4.5 %shard_map.102 = (f32[16,128,128]{2,1,0:T(8,128)S(1)}, bf16[32,128,256]{2,1,0:T(8,128)(2,1)S(1)}, bf16[128,256]{1,0:T(8,128)(2,1)S(1)}, bf16[256,128]{1,0:T(8,12...) custom-call(s32[2,8]{1,0:T(2,128)} %ids_src.1, ...), custom_call_target="tpu_custom_call" | custom-call | flops 1 | bytes 1 | tf_op jit(solution)/shard_map/pallas_call | solution.py:30
  12.8 5.9 %collective-permute-done.block_ref = bf16[128,16,128]{2,1,0:T(8,128)(2,1)S(1)} collective-permute-done((bf16[128,16,128]{2,1,0:T(8,128)(2,1)}, bf16[128,16,128]{2,1,0:T(8,128)(2,1)S(1)}, u32[]{:S(2)}, u32[]{:S(2)}) %collective-permute-start) | collective-permute-done | bytes 524320 | tf_op jit(solution)/shard_map/ppermute | solution.py:343
  18.7 2.1 %collective-permute-start.2 = (bf16[128,16,128]{2,1,0:T(8,128)(2,1)S(1)}, bf16[128,16,128]{2,1,0:T(8,128)(2,1)S(1)}, u32[]{:S(2)}, u32[]{:S(2)}) collective-permute-start(bf16[128,16,128]{2,1,0:T(8,128)(2,1)S(1)} %collective-permute-done.block_ref), channel_id=1, source_target_pairs={{1,0},{0,1},{5,4},{4,5},{9,8},{8,9},{13,12},{12,13},{17,16},{16,17... | collective-permute-start | bytes 1572872 | tf_op jit(solution)/shard_map/ppermute | solution.py:378
  20.9 1.8 %shard_map.104 = (f32[16,128,128]{2,1,0:T(8,128)S(1)}, bf16[32,128,256]{2,1,0:T(8,128)(2,1)S(1)}) custom-call(f32[16,128,128]{2,1,0:T(8,128)S(1)} %get-tuple-element.50.sum_ref, bf16[32,128,256]{2,1,0:T(8,128)(2,1)S(1)} %get-tuple-element.51.crossed_ref, bf16[128,16,128]{2,1,0:T(8,128)(2,1)S(1)} %collective-permute-done.block_ref, ...), custom_call_target="tpu_custom_call", output_to_operand_aliasing={{1}: (1, {})} | custom-call | flops 1 | bytes 1 | tf_op jit(solution)/shard_map/pallas_call | solution.py:30
  22.6 0.0 collective-permute-done.4.after_ref
  22.6 0.7 %shard_map.105 = (bf16[16,128,128]{2,1,0:T(8,128)(2,1)S(1)}, f32[16,128,128]{2,1,0:T(8,128)S(1)}, bf16[16,128,128]{2,1,0:T(8,128)(2,1)S(1)}) custom-call(bf16[16,128,128]{2,1,0:T(8,128)(2,1)S(1)} %get-tuple-element.47.own_ref, bf16[16,64,128]{2,1,0:T(8,128)(2,1)S(1)} %collective-permute-done.3.before_ref, ...), custom_call_target="tpu_custom_call" | custom-call | flops 68719476736 | bytes 1 | tf_op jit(solution)/shard_map/pallas_call | solution.py:30
  23.4 1.8 %shard_map.106 = (bf16[16,128,128]{2,1,0:T(8,128)(2,1)S(1)}, bf16[32,128,256]{2,1,0:T(8,128)(2,1)S(1)}) custom-call(f32[16,128,128]{2,1,0:T(8,128)S(1)} %get-tuple-element.61.sum_ref, bf16[32,128,256]{2,1,0:T(8,128)(2,1)S(1)} %get-tuple-element.62.crossed_ref, ...), custom_call_target="tpu_custom_call", output_to_operand_aliasing={{1}: (1, {})} | custom-call | flops 1 | bytes 1 | tf_op jit(solution)/shard_map/pallas_call | solution.py:30
  25.1 1.3 %shard_map.107 = (f32[16,128,128]{2,1,0:T(8,128)S(1)}, bf16[16,64,128]{2,1,0:T(8,128)(2,1)S(1)}, bf16[16,64,128]{2,1,0:T(8,128)(2,1)S(1)}, f32[128,128]{1,0:T(8,128)S(1)}) custom-call(bf16[16,128,128]{2,1,0:T(8,128)(2,1)S(1)} %get-tuple-element.66.grad_ref, f32[16,128,128]{2,1,0:T(8,128)S(1)} %get-tuple-element.67.slope_ref, ...), custom_call_target="tpu_custom_call" | custom-call | flops 1 | bytes 1 | tf_op jit(solution)/shard_map/pallas_call | solution.py:30
  26.4 4.7 %shard_map.108 = (f32[160,128]{1,0:T(8,128)S(1)}, f32[160,128]{1,0:T(8,128)S(1)}) custom-call(bf16[16,128,128]{2,1,0:T(8,128)(2,1)S(1)} %get-tuple-element.60.act_ref, bf16[32,128,256]{2,1,0:T(8,128)(2,1)S(1)} %get-tuple-element.64.cross_ref, bf16[64,128]{1,0:T(8,128)(2,1)S(1)} %get-tuple-element.65.taps_ref, ...), custom_call_target="tpu_custom_call" | custom-call | flops 1 | bytes 1 | tf_op jit(solution)/shard_map/pallas_call | solution.py:30
  31.1 0.4 collective-permute-start.5
  31.5 1.0 %collective-permute-done.5 = f32[160,128]{1,0:T(8,128)S(1)} collective-permute-done((f32[160,128]{1,0:T(8,128)S(1)}, f32[160,128]{1,0:T(8,128)S(1)}, u32[]{:S(2)}, u32[]{:S(2)}) %collective-permute-start.5) | collective-permute-done | bytes 81952 | tf_op jit(solution)/shard_map/ppermute | solution.py:317
  32.5 0.1 collective-permute-start.6
  32.6 0.7 %collective-permute-start.8 = (bf16[16,64,128]{2,1,0:T(8,128)(2,1)S(1)}, bf16[16,64,128]{2,1,0:T(8,128)(2,1)S(1)}, u32[]{:S(2)}, u32[]{:S(2)}) collective-permute-start(bf16[16,64,128]{2,1,0:T(8,128)(2,1)S(1)} %get-tuple-element.74), channel_id=1, source_target_pairs={{4,8},{12,16},{20,24},{8,4},{16,12},{24,20},{5,9},{13,17},{21,25},... | collective-permute-start | bytes 786440 | tf_op jit(solution)/shard_map/ppermute | solution.py:406
  33.3 5.8 %collective-permute-start.10 = (bf16[16,64,128]{2,1,0:T(8,128)(2,1)S(1)}, bf16[16,64,128]{2,1,0:T(8,128)(2,1)S(1)}, u32[]{:S(2)}, u32[]{:S(2)}) collective-permute-start(bf16[16,64,128]{2,1,0:T(8,128)(2,1)S(1)} %get-tuple-element.78), channel_id=1, source_target_pairs={{0,4},{4,0},{8,12},{12,8},{16,20},{20,16},{24,28},{28,24},{1,5},{5... | collective-permute-start | bytes 786440 | tf_op jit(solution)/shard_map/ppermute | solution.py:407
  39.1 1.6 %collective-permute-start.7 = (bf16[160,128]{1,0:T(8,128)(2,1)S(1)}, bf16[160,128]{1,0:T(8,128)(2,1)S(1)}, u32[]{:S(2)}, u32[]{:S(2)}) collective-permute-start(bf16[160,128]{1,0:T(8,128)(2,1)S(1)} %get-tuple-element.87), channel_id=1, source_target_pairs={{0,8},{4,12},{8,0},{12,4},{16,24},{20,28},{24,16},{28,20},{1,9},{5... | collective-permute-start | bytes 122888 | tf_op jit(solution)/shard_map/ppermute | solution.py:317
  40.7 0.1 shard_map.109.spread_ref
  40.8 5.4 %collective-permute-done.7 = bf16[160,128]{1,0:T(8,128)(2,1)S(1)} collective-permute-done((bf16[160,128]{1,0:T(8,128)(2,1)S(1)}, bf16[160,128]{1,0:T(8,128)(2,1)S(1)}, u32[]{:S(2)}, u32[]{:S(2)}) %collective-permute-start.7) | collective-permute-done | bytes 40992 | tf_op jit(solution)/shard_map/ppermute | solution.py:317
  46.2 2.6 %collective-permute-start.9 = (bf16[160,128]{1,0:T(8,128)(2,1)S(1)}, bf16[160,128]{1,0:T(8,128)(2,1)S(1)}, u32[]{:S(2)}, u32[]{:S(2)}) collective-permute-start(bf16[160,128]{1,0:T(8,128)(2,1)S(1)} %add_convert_fusion.1), channel_id=1, source_target_pairs={{0,16},{4,20},{8,24},{12,28},{16,0},{20,4},{24,8},{28,12},{1,17},{... | collective-permute-start | bytes 122888 | tf_op jit(solution)/shard_map/ppermute | solution.py:317
  48.9 1.0 %collective-permute-done.10.even_ref = bf16[16,64,128]{2,1,0:T(8,128)(2,1)S(1)} collective-permute-done((bf16[16,64,128]{2,1,0:T(8,128)(2,1)S(1)}, bf16[16,64,128]{2,1,0:T(8,128)(2,1)S(1)}, u32[]{:S(2)}, u32[]{:S(2)}) %collective-permute-start.10) | collective-permute-done | bytes 262176 | tf_op jit(solution)/shard_map/ppermute | solution.py:407
  49.9 1.2 %shard_map.111 = bf16[128,16,128]{2,1,0:T(8,128)(2,1)} custom-call(f32[16,128,128]{2,1,0:T(8,128)S(1)} %shard_map.109.spread_ref, bf16[16,64,128]{2,1,0:T(8,128)(2,1)S(1)} %collective-permute-done.10.even_ref, bf16[16,128,128]{2,1,0:T(8,128)(2,1)S(1)} %get-tuple-element.79.cot_ref), custom_call_target="tpu_custom_call" | custom-call | flops 68719476736 | bytes 1 | tf_op jit(solution)/shard_map/pallas_call | solution.py:30
  51.1 0.1 collective-permute-done.9
  51.2 2.4 %collective-permute-start.11 = (bf16[160,128]{1,0:T(8,128)(2,1)S(1)}, bf16[160,128]{1,0:T(8,128)(2,1)S(1)}, u32[]{:S(2)}, u32[]{:S(2)}) collective-permute-start(bf16[160,128]{1,0:T(8,128)(2,1)S(1)} %add_convert_fusion), channel_id=1, source_target_pairs={{0,4},{4,0},{8,12},{12,8},{16,20},{20,16},{24,28},{28,24},{1,5},{5... | collective-permute-start | bytes 122888 | tf_op jit(solution)/shard_map/ppermute | solution.py:317
  53.7 2.0 %collective-permute-done.11 = bf16[160,128]{1,0:T(8,128)(2,1)S(1)} collective-permute-done((bf16[160,128]{1,0:T(8,128)(2,1)S(1)}, bf16[160,128]{1,0:T(8,128)(2,1)S(1)}, u32[]{:S(2)}, u32[]{:S(2)}) %collective-permute-start.11) | collective-permute-done | bytes 40992 | tf_op jit(solution)/shard_map/ppermute | solution.py:317
  55.7 0.1 collective-permute-start.12
  55.7 1.3 %collective-permute-done.12.other_ref = f32[160,128]{1,0:T(8,128)S(1)} collective-permute-done((f32[160,128]{1,0:T(8,128)S(1)}, f32[160,128]{1,0:T(8,128)S(1)}, u32[]{:S(2)}, u32[]{:S(2)}) %collective-permute-start.12) | collective-permute-done | bytes 81952 | tf_op jit(solution)/shard_map/ppermute | solution.py:317
  57.0 0.7 %shard_map.112 = (f32[128,128]{1,0:T(8,128)}, f32[128,128]{1,0:T(8,128)}, f32[64,128]{1,0:T(8,128)}) custom-call(f32[160,128]{1,0:T(8,128)S(1)} %convert_add_fusion.mine_ref, f32[160,128]{1,0:T(8,128)S(1)} %collective-permute-done.12.other_ref, f32[8,128]{1,0:T(8,128)S(1)} %shard_map.110.mark_ref), custom_call_target="tpu_custom_call" | custom-call | flops 1 | bytes 1 | tf_op jit(solution)/shard_map/pallas_call | solution.py:30
  (11 shorter events, 0.1 us)
Async XLA Ops:
  0.6 7.7 %collective-permute-start.1 = (bf16[128,16,128]{2,1,0:T(8,128)(2,1)}, bf16[128,16,128]{2,1,0:T(8,128)(2,1)S(1)}, u32[]{:S(2)}, u32[]{:S(2)}) collective-permute-start(bf16[128,16,128]{2,1,0:T(8,128)(2,1)} %cot_src.1), channel_id=1, source_target_pairs={{1,0},{3,2},{5,4},{7,6},{9,8},{11,10},{13,12},{15,14},{17,16},{19,... | collective-permute-start | bytes 1572872 | tf_op jit(solution)/shard_map/ppermute | solution.py:340
  1.9 16.8 %collective-permute-start = (bf16[128,16,128]{2,1,0:T(8,128)(2,1)}, bf16[128,16,128]{2,1,0:T(8,128)(2,1)S(1)}, u32[]{:S(2)}, u32[]{:S(2)}) collective-permute-start(bf16[128,16,128]{2,1,0:T(8,128)(2,1)} %cot_src.1), channel_id=1, source_target_pairs={{2,0},{3,1},{6,4},{7,5},{10,8},{11,9},{14,12},{15,13},{18,16},{19,... | collective-permute-start | bytes 1572872 | tf_op jit(solution)/shard_map/ppermute | solution.py:343
  4.6 18.0 %collective-permute-start.3 = (bf16[16,64,128]{2,1,0:T(8,128)(2,1)S(1)}, bf16[16,64,128]{2,1,0:T(8,128)(2,1)S(1)}, u32[]{:S(2)}, u32[]{:S(2)}) collective-permute-start(bf16[16,64,128]{2,1,0:T(8,128)(2,1)S(1)} %get-tuple-element.48), channel_id=1, source_target_pairs={{0,4},{4,0},{8,12},{12,8},{16,20},{20,16},{24,28},{28,24},{1,5},{5... | collective-permute-start | bytes 786440 | tf_op jit(solution)/shard_map/ppermute | solution.py:342
  7.6 15.0 %collective-permute-start.4 = (bf16[16,64,128]{2,1,0:T(8,128)(2,1)S(1)}, bf16[16,64,128]{2,1,0:T(8,128)(2,1)S(1)}, u32[]{:S(2)}, u32[]{:S(2)}) collective-permute-start(bf16[16,64,128]{2,1,0:T(8,128)(2,1)S(1)} %get-tuple-element.49), channel_id=1, source_target_pairs={{4,8},{12,16},{20,24},{8,4},{16,12},{24,20},{5,9},{13,17},{21,25},... | collective-permute-start | bytes 786440 | tf_op jit(solution)/shard_map/ppermute | solution.py:341
  18.7 4.6 %collective-permute-start.2 = (bf16[128,16,128]{2,1,0:T(8,128)(2,1)S(1)}, bf16[128,16,128]{2,1,0:T(8,128)(2,1)S(1)}, u32[]{:S(2)}, u32[]{:S(2)}) collective-permute-start(bf16[128,16,128]{2,1,0:T(8,128)(2,1)S(1)} %collective-permute-done.block_ref), channel_id=1, source_target_pairs={{1,0},{0,1},{5,4},{4,5},{9,8},{8,9},{13,12},{12,13},{17,16},{16,17... | collective-permute-start | bytes 1572872 | tf_op jit(solution)/shard_map/ppermute | solution.py:378
  31.1 1.3 %collective-permute-start.5 = (f32[160,128]{1,0:T(8,128)S(1)}, f32[160,128]{1,0:T(8,128)S(1)}, u32[]{:S(2)}, u32[]{:S(2)}) collective-permute-start(f32[160,128]{1,0:T(8,128)S(1)} %get-tuple-element.72), channel_id=1, source_target_pairs={{0,1},{1,0},{2,3},{3,2},{4,5},{5,4},{6,7},{7,6},{8,9},{9,8},{10,11... | collective-permute-start | bytes 245768 | tf_op jit(solution)/shard_map/ppermute | solution.py:317
  32.5 6.6 %collective-permute-start.6 = (bf16[160,128]{1,0:T(8,128)(2,1)S(1)}, bf16[160,128]{1,0:T(8,128)(2,1)S(1)}, u32[]{:S(2)}, u32[]{:S(2)}) collective-permute-start(bf16[160,128]{1,0:T(8,128)(2,1)S(1)} %add_convert_fusion.2), channel_id=1, source_target_pairs={{0,2},{1,3},{2,0},{3,1},{4,6},{5,7},{6,4},{7,5},{8,10},{9,11},{10,... | collective-permute-start | bytes 122888 | tf_op jit(solution)/shard_map/ppermute | solution.py:317
  32.6 8.1 %collective-permute-start.8 = (bf16[16,64,128]{2,1,0:T(8,128)(2,1)S(1)}, bf16[16,64,128]{2,1,0:T(8,128)(2,1)S(1)}, u32[]{:S(2)}, u32[]{:S(2)}) collective-permute-start(bf16[16,64,128]{2,1,0:T(8,128)(2,1)S(1)} %get-tuple-element.74), channel_id=1, source_target_pairs={{4,8},{12,16},{20,24},{8,4},{16,12},{24,20},{5,9},{13,17},{21,25},... | collective-permute-start | bytes 786440 | tf_op jit(solution)/shard_map/ppermute | solution.py:406
  33.3 16.6 %collective-permute-start.10 = (bf16[16,64,128]{2,1,0:T(8,128)(2,1)S(1)}, bf16[16,64,128]{2,1,0:T(8,128)(2,1)S(1)}, u32[]{:S(2)}, u32[]{:S(2)}) collective-permute-start(bf16[16,64,128]{2,1,0:T(8,128)(2,1)S(1)} %get-tuple-element.78), channel_id=1, source_target_pairs={{0,4},{4,0},{8,12},{12,8},{16,20},{20,16},{24,28},{28,24},{1,5},{5... | collective-permute-start | bytes 786440 | tf_op jit(solution)/shard_map/ppermute | solution.py:407
  39.1 7.1 %collective-permute-start.7 = (bf16[160,128]{1,0:T(8,128)(2,1)S(1)}, bf16[160,128]{1,0:T(8,128)(2,1)S(1)}, u32[]{:S(2)}, u32[]{:S(2)}) collective-permute-start(bf16[160,128]{1,0:T(8,128)(2,1)S(1)} %get-tuple-element.87), channel_id=1, source_target_pairs={{0,8},{4,12},{8,0},{12,4},{16,24},{20,28},{24,16},{28,20},{1,9},{5... | collective-permute-start | bytes 122888 | tf_op jit(solution)/shard_map/ppermute | solution.py:317
  46.2 5.0 %collective-permute-start.9 = (bf16[160,128]{1,0:T(8,128)(2,1)S(1)}, bf16[160,128]{1,0:T(8,128)(2,1)S(1)}, u32[]{:S(2)}, u32[]{:S(2)}) collective-permute-start(bf16[160,128]{1,0:T(8,128)(2,1)S(1)} %add_convert_fusion.1), channel_id=1, source_target_pairs={{0,16},{4,20},{8,24},{12,28},{16,0},{20,4},{24,8},{28,12},{1,17},{... | collective-permute-start | bytes 122888 | tf_op jit(solution)/shard_map/ppermute | solution.py:317
  51.2 4.4 %collective-permute-start.11 = (bf16[160,128]{1,0:T(8,128)(2,1)S(1)}, bf16[160,128]{1,0:T(8,128)(2,1)S(1)}, u32[]{:S(2)}, u32[]{:S(2)}) collective-permute-start(bf16[160,128]{1,0:T(8,128)(2,1)S(1)} %add_convert_fusion), channel_id=1, source_target_pairs={{0,4},{4,0},{8,12},{12,8},{16,20},{20,16},{24,28},{28,24},{1,5},{5... | collective-permute-start | bytes 122888 | tf_op jit(solution)/shard_map/ppermute | solution.py:317
  55.7 1.3 %collective-permute-start.12 = (f32[160,128]{1,0:T(8,128)S(1)}, f32[160,128]{1,0:T(8,128)S(1)}, u32[]{:S(2)}, u32[]{:S(2)}) collective-permute-start(f32[160,128]{1,0:T(8,128)S(1)} %convert_add_fusion.mine_ref), channel_id=1, source_target_pairs={{0,1},{1,0},{2,3},{3,2},{4,5},{5,4},{6,7},{7,6},{8,9},{9,8},{10,11... | collective-permute-start | bytes 245768 | tf_op jit(solution)/shard_map/ppermute | solution.py:317

commit v3 on v2

--- a/solution.py
+++ b/solution.py
@@ -67,12 +67,13 @@
     far_ref[...] = own_ref[:, pl.ds(low, half)]
 
 
-def take_block(block_ref, wout, steady, part, conv):
+def take_block(block_ref, wout, steady, part, conv, valid=None):
     steps, rows, chans = steady.shape
     for start in range(0, rows, 16):
-        steady[:, start : start + 16] = jnp.swapaxes(
-            block_ref[start : start + 16].astype(F32), 0, 1
-        ).astype(BF)
+        block = block_ref[start : start + 16].astype(F32)
+        if valid is not None:
+            block = jnp.where(valid, block, 0.0)
+        steady[:, start : start + 16] = jnp.swapaxes(block, 0, 1).astype(BF)
     for s in range(0, steps, 4):
         block = steady[s : s + 4].reshape(4 * rows, chans)
         conv[s : s + 4] = dot(block, wout, ((1,), (1,))).astype(BF).reshape(4, rows, chans)
@@ -122,7 +123,7 @@
     odd = lax.axis_index("tm") & 1
     take_block(cot_ref, wout_ref[...], steady_ref, part, conv)
     sent = [place_part(part, cross_ref, 0, sems.at[6])]
-    take_block(near_ref, wout_ref[...], other, other_part, other_conv)
+    take_block(near_ref, wout_ref[...], other, other_part, other_conv, odd == 0)
     sent.append(place_part(other_part, cross_ref, 1 + 2 * odd, sems.at[7]))
     taps = taps_ref[...].astype(F32)
     for lag in range(taps_ref.shape[0]):
@@ -161,7 +162,8 @@
 def add_body(last, sum_ref, crossed_ref, block_ref, lags_ref, wout_ref, out_ref, cross_ref, steady, part, conv, sems):
     steps, rows, chans = conv.shape
     slot = 3 - 2 * (lax.axis_index("tm") & 1) if last else 2
-    take_block(block_ref, wout_ref[...], steady, part, conv)
+    valid = lax.axis_index("tm") < 2
+    take_block(block_ref, wout_ref[...], steady, part, conv, valid)
     sent = place_part(part, cross_ref, slot, sems.at[0])
 
     def tile(index, carry):
@@ -329,6 +331,7 @@
     total = kernel_taps.shape[0]
     evens = [(i, i ^ 1) for i in range(bus)]
     odds = [(i, i + 1) for i in range(1, bus - 1, 2)] + [(i + 1, i) for i in range(1, bus - 1, 2)]
+    odds += [(0, 0), (bus - 1, bus - 1)]
     wide = (steps, rows, chans)
     edge = (steps, half, chans)
     square = (chans, chans)
@@ -337,10 +340,10 @@
         split_body, [(wide, BF), (edge, BF), (edge, BF)], features,
         scratch=[pltpu.VMEM(features.shape, BF), pltpu.SemaphoreType.DMA((1,))], far=[0],
     )
-    near = lax.ppermute(cotangent, "tm", [(1, 0), (3, 2)])
+    near = swap(cotangent, "tm", 1)
     odd_edge = lax.ppermute(odd_edge, "bus", odds)
     even_edge = lax.ppermute(even_edge, "bus", evens)
-    far = lax.ppermute(cotangent, "tm", [(2, 0), (3, 1)])
+    far = swap(cotangent, "tm", 2)
 
     pairs = total // 2
     crossing = (pairs, chans, 2 * rows)
@@ -375,7 +378,7 @@
         )
 
     far, sums = lax.optimization_barrier((far, sums))
-    swapped = lax.ppermute(far, "tm", [(1, 0), (0, 1)])
+    swapped = swap(far, "tm", 1)
     sums, crossed = add_block(False, F32, sums, crossed, far)
     even_edge, odd_edge, sums = lax.optimization_barrier((even_edge, odd_edge, sums))
     act, slope, mixed = call(
@@ -401,6 +404,7 @@
     )
     mark = send[0:8]
     keep = keep + swap(send, "tm", 1)
+    keep, even_grad = lax.optimization_barrier((keep, even_grad))
     hops = [("tm", 1 << bit) for bit in range(1, tm.bit_length() - 1)]
     hops += [("bus", 1 << bit) for bit in range(1, bus.bit_length() - 1)] + [("bus", 1)]
     odd_grad = lax.ppermute(odd_grad, "bus", odds)
@@ -408,6 +412,8 @@
     for place, (axis, distance) in enumerate(hops):
         sent = keep.astype(BF)
         received = swap(sent, axis, distance)
+        if place == 0:
+            received, mark = pause(keep, received, mark)
         if place == 1:
             (spread,) = call(
                 functools.partial(fold_body, True), [(wide, F32)], spread, odd_grad, cost=1 << 30

time: 57.9 us -> 51.8 us (0.89)
  waiting for transfers between devices: 16.7 us -> 12.4 us
  starting transfers between devices: 22.1 us -> 20.2 us
    ppermute x6 -> x9, starting transfers between devices: 7.23 us -> 13.2 us  [swap(): return lax.ppermute(value, axis, [(i, i ^ distance) for i in range(size)])]
    ppermute x3 -> x0, waiting for transfers between devices: 5.94 us -> none  [the longest x1 5.93 us: shards(): far = lax.ppermute(cotangent, 'tm', [(2, 0), (3, 1)])]
    ppermute x3 -> x0, starting transfers between devices: 4.7 us -> none  [the longest x1 2.11 us: shards(): swapped = lax.ppermute(far, 'tm', [(1, 0), (0, 1)])]
    ppermute x1, starting transfers between devices: 5.78 us -> 4.04 us  [shards(): even_grad = lax.ppermute(even_grad, 'bus', evens)]
    ppermute x6 -> x9, waiting for transfers between devices: 9.74 us -> 11.4 us  [swap(): return lax.ppermute(value, axis, [(i, i ^ distance) for i in range(size)])]
    ppermute x1, starting transfers between devices: 3.03 us -> 1.58 us  [shards(): even_edge = lax.ppermute(even_edge, 'bus', evens)]
    pallas_call x11 -> x12, Pallas kernels: 18 us -> 18.2 us  [call(): pl.pallas_call(body, out_shape=[jax.ShapeDtypeStruct(shape, dtype) for sh...]
  transfers between devices with their start and end apart: 13 -> 13, of which waited for: 7 -> 7; matrix products, arithmetic and copies ran while one was open for 0% -> 0% of each run, Pallas kernels for 17% -> 19%
where the time goes in v3:
time: 51.8 us; the launch traced here: 51.6 us
  starting transfers between devices  20.2 us (39%)
  Pallas kernels  18.2 us (35%)
  waiting for transfers between devices  12.4 us (24%)
  between operations  0.78 us (2%)
    pallas_call x12, Pallas kernels, call(): pl.pallas_call(body, out_shape=[jax.ShapeDtypeStruct(shape, dtype) for sh...  18.2 us
    ppermute x9, starting transfers between devices, swap(): return lax.ppermute(value, axis, [(i, i ^ distance) for i in range(size)])  13.2 us
    ppermute x9, waiting for transfers between devices, swap(): return lax.ppermute(value, axis, [(i, i ^ distance) for i in range(size)])  11.4 us
    ppermute x1, starting transfers between devices, shards(): even_grad = lax.ppermute(even_grad, 'bus', evens)  4.04 us
    ppermute x1, starting transfers between devices, shards(): even_edge = lax.ppermute(even_edge, 'bus', evens)  1.58 us
  transfers between devices with their start and end apart: 13, of which 7 were waited for; matrix products, arithmetic and copies ran while one was open for 0% of the time, Pallas kernels for 19%

profile of v3, /device:TPU:0, one launch (start us, length us, event | category | flops | bytes accessed | tf_op | source)
XLA Modules:
  0.0 51.6 jit_solution(12489281414422201348)
XLA Ops:
  0.6 0.5 %collective-permute-start.1 = (bf16[128,16,128]{2,1,0:T(8,128)(2,1)}, bf16[128,16,128]{2,1,0:T(8,128)(2,1)S(1)}, u32[]{:S(2)}, u32[]{:S(2)}) collective-permute-start(bf16[128,16,128]{2,1,0:T(8,128)(2,1)} %cot_src.1), channel_id=1, source_target_pairs={{0,1},{1,0},{2,3},{3,2},{4,5},{5,4},{6,7},{7,6},{8,9},{9,8},{10,11... | collective-permute-start | bytes 1572872 | tf_op jit(solution)/shard_map/ppermute | solution.py:319
  1.1 2.6 %collective-permute-start = (bf16[128,16,128]{2,1,0:T(8,128)(2,1)}, bf16[128,16,128]{2,1,0:T(8,128)(2,1)S(1)}, u32[]{:S(2)}, u32[]{:S(2)}) collective-permute-start(bf16[128,16,128]{2,1,0:T(8,128)(2,1)} %cot_src.1), channel_id=1, source_target_pairs={{0,2},{1,3},{2,0},{3,1},{4,6},{5,7},{6,4},{7,5},{8,10},{9,11},{10,... | collective-permute-start | bytes 1572872 | tf_op jit(solution)/shard_map/ppermute | solution.py:319
  3.7 1.4 %shard_map.103 = (bf16[16,128,128]{2,1,0:T(8,128)(2,1)S(1)}, bf16[16,64,128]{2,1,0:T(8,128)(2,1)S(1)}, bf16[16,64,128]{2,1,0:T(8,128)(2,1)S(1)}) custom-call(bf16[128,16,128]{2,1,0:T(8,128)(2,1)} %source_ref.1), custom_call_target="tpu_custom_call" | custom-call | flops 1 | bytes 1 | tf_op jit(solution)/shard_map/pallas_call | solution.py:30
  5.1 1.6 %collective-permute-start.3 = (bf16[16,64,128]{2,1,0:T(8,128)(2,1)S(1)}, bf16[16,64,128]{2,1,0:T(8,128)(2,1)S(1)}, u32[]{:S(2)}, u32[]{:S(2)}) collective-permute-start(bf16[16,64,128]{2,1,0:T(8,128)(2,1)S(1)} %get-tuple-element.52), channel_id=1, source_target_pairs={{0,4},{4,0},{8,12},{12,8},{16,20},{20,16},{24,28},{28,24},{1,5},{5... | collective-permute-start | bytes 786440 | tf_op jit(solution)/shard_map/ppermute | solution.py:345
  6.7 0.7 %collective-permute-start.4 = (bf16[16,64,128]{2,1,0:T(8,128)(2,1)S(1)}, bf16[16,64,128]{2,1,0:T(8,128)(2,1)S(1)}, u32[]{:S(2)}, u32[]{:S(2)}) collective-permute-start(bf16[16,64,128]{2,1,0:T(8,128)(2,1)S(1)} %get-tuple-element.53), channel_id=1, source_target_pairs={{4,8},{12,16},{20,24},{8,4},{16,12},{24,20},{0,0},{28,28},{5,9},{1... | collective-permute-start | bytes 786440 | tf_op jit(solution)/shard_map/ppermute | solution.py:344
  7.3 0.0 collective-permute-done.1.near_ref
  7.4 4.6 %shard_map.102 = (f32[16,128,128]{2,1,0:T(8,128)S(1)}, bf16[32,128,256]{2,1,0:T(8,128)(2,1)S(1)}, bf16[128,256]{1,0:T(8,128)(2,1)S(1)}, bf16[256,128]{1,0:T(8,12...) custom-call(s32[2,8]{1,0:T(2,128)} %ids_src.1, ...), custom_call_target="tpu_custom_call" | custom-call | flops 1 | bytes 1 | tf_op jit(solution)/shard_map/pallas_call | solution.py:30
  11.9 4.5 %collective-permute-done.block_ref = bf16[128,16,128]{2,1,0:T(8,128)(2,1)S(1)} collective-permute-done((bf16[128,16,128]{2,1,0:T(8,128)(2,1)}, bf16[128,16,128]{2,1,0:T(8,128)(2,1)S(1)}, u32[]{:S(2)}, u32[]{:S(2)}) %collective-permute-start) | collective-permute-done | bytes 524320 | tf_op jit(solution)/shard_map/ppermute | solution.py:319
  16.4 1.8 %shard_map.104 = (f32[16,128,128]{2,1,0:T(8,128)S(1)}, bf16[32,128,256]{2,1,0:T(8,128)(2,1)S(1)}) custom-call(f32[16,128,128]{2,1,0:T(8,128)S(1)} %get-tuple-element.54.sum_ref, bf16[32,128,256]{2,1,0:T(8,128)(2,1)S(1)} %get-tuple-element.55.crossed_ref, bf16[128,16,128]{2,1,0:T(8,128)(2,1)S(1)} %collective-permute-done.block_ref, ...), custom_call_target="tpu_custom_call", output_to_operand_aliasing={{1}: (1, {})} | custom-call | flops 1 | bytes 1 | tf_op jit(solution)/shard_map/pallas_call | solution.py:30
  18.3 0.7 %shard_map.105 = (bf16[16,128,128]{2,1,0:T(8,128)(2,1)S(1)}, f32[16,128,128]{2,1,0:T(8,128)S(1)}, bf16[16,128,128]{2,1,0:T(8,128)(2,1)S(1)}) custom-call(bf16[16,128,128]{2,1,0:T(8,128)(2,1)S(1)} %get-tuple-element.51.own_ref, bf16[16,64,128]{2,1,0:T(8,128)(2,1)S(1)} %collective-permute-done.3.before_ref, ...), custom_call_target="tpu_custom_call" | custom-call | flops 68719476736 | bytes 1 | tf_op jit(solution)/shard_map/pallas_call | solution.py:30
  19.0 1.8 %shard_map.106 = (bf16[16,128,128]{2,1,0:T(8,128)(2,1)S(1)}, bf16[32,128,256]{2,1,0:T(8,128)(2,1)S(1)}) custom-call(f32[16,128,128]{2,1,0:T(8,128)S(1)} %get-tuple-element.65.sum_ref, bf16[32,128,256]{2,1,0:T(8,128)(2,1)S(1)} %get-tuple-element.66.crossed_ref, ...), custom_call_target="tpu_custom_call", output_to_operand_aliasing={{1}: (1, {})} | custom-call | flops 1 | bytes 1 | tf_op jit(solution)/shard_map/pallas_call | solution.py:30
  20.8 1.3 %shard_map.107 = (f32[16,128,128]{2,1,0:T(8,128)S(1)}, bf16[16,64,128]{2,1,0:T(8,128)(2,1)S(1)}, bf16[16,64,128]{2,1,0:T(8,128)(2,1)S(1)}, f32[128,128]{1,0:T(8,128)S(1)}) custom-call(bf16[16,128,128]{2,1,0:T(8,128)(2,1)S(1)} %get-tuple-element.70.grad_ref, f32[16,128,128]{2,1,0:T(8,128)S(1)} %get-tuple-element.71.slope_ref, ...), custom_call_target="tpu_custom_call" | custom-call | flops 1 | bytes 1 | tf_op jit(solution)/shard_map/pallas_call | solution.py:30
  22.1 4.7 %shard_map.108 = (f32[160,128]{1,0:T(8,128)S(1)}, f32[160,128]{1,0:T(8,128)S(1)}) custom-call(bf16[16,128,128]{2,1,0:T(8,128)(2,1)S(1)} %get-tuple-element.64.act_ref, bf16[32,128,256]{2,1,0:T(8,128)(2,1)S(1)} %get-tuple-element.68.cross_ref, bf16[64,128]{1,0:T(8,128)(2,1)S(1)} %get-tuple-element.69.taps_ref, ...), custom_call_target="tpu_custom_call" | custom-call | flops 1 | bytes 1 | tf_op jit(solution)/shard_map/pallas_call | solution.py:30
  26.8 0.6 %collective-permute-start.5 = (f32[160,128]{1,0:T(8,128)S(1)}, f32[160,128]{1,0:T(8,128)S(1)}, u32[]{:S(2)}, u32[]{:S(2)}) collective-permute-start(f32[160,128]{1,0:T(8,128)S(1)} %get-tuple-element.76), channel_id=1, source_target_pairs={{0,1},{1,0},{2,3},{3,2},{4,5},{5,4},{6,7},{7,6},{8,9},{9,8},{10,11... | collective-permute-start | bytes 245768 | tf_op jit(solution)/shard_map/ppermute | solution.py:319
  27.4 0.7 %collective-permute-start.8 = (bf16[16,64,128]{2,1,0:T(8,128)(2,1)S(1)}, bf16[16,64,128]{2,1,0:T(8,128)(2,1)S(1)}, u32[]{:S(2)}, u32[]{:S(2)}) collective-permute-start(bf16[16,64,128]{2,1,0:T(8,128)(2,1)S(1)} %get-tuple-element.81), channel_id=1, source_target_pairs={{4,8},{12,16},{20,24},{8,4},{16,12},{24,20},{0,0},{28,28},{5,9},{1... | collective-permute-start | bytes 786440 | tf_op jit(solution)/shard_map/ppermute | solution.py:410
  28.1 0.2 collective-permute-done.5
  28.3 1.8 %collective-permute-start.6 = (bf16[160,128]{1,0:T(8,128)(2,1)S(1)}, bf16[160,128]{1,0:T(8,128)(2,1)S(1)}, u32[]{:S(2)}, u32[]{:S(2)}) collective-permute-start(bf16[160,128]{1,0:T(8,128)(2,1)S(1)} %convert_element_type.36), channel_id=1, source_target_pairs={{0,2},{1,3},{2,0},{3,1},{4,6},{5,7},{6,4},{7,5},{8,10},{9,11},{10,... | collective-permute-start | bytes 122888 | tf_op jit(solution)/shard_map/ppermute | solution.py:319
  30.2 4.0 %collective-permute-start.10 = (bf16[16,64,128]{2,1,0:T(8,128)(2,1)S(1)}, bf16[16,64,128]{2,1,0:T(8,128)(2,1)S(1)}, u32[]{:S(2)}, u32[]{:S(2)}) collective-permute-start(bf16[16,64,128]{2,1,0:T(8,128)(2,1)S(1)} %get-tuple-element.86), channel_id=1, source_target_pairs={{0,4},{4,0},{8,12},{12,8},{16,20},{20,16},{24,28},{28,24},{1,5},{5... | collective-permute-start | bytes 786440 | tf_op jit(solution)/shard_map/ppermute | solution.py:411
  34.2 0.0 collective-permute-done.6
  34.2 2.6 %collective-permute-start.7 = (bf16[160,128]{1,0:T(8,128)(2,1)S(1)}, bf16[160,128]{1,0:T(8,128)(2,1)S(1)}, u32[]{:S(2)}, u32[]{:S(2)}) collective-permute-start(bf16[160,128]{1,0:T(8,128)(2,1)S(1)} %get-tuple-element.95), channel_id=1, source_target_pairs={{0,8},{4,12},{8,0},{12,4},{16,24},{20,28},{24,16},{28,20},{1,9},{5... | collective-permute-start | bytes 122888 | tf_op jit(solution)/shard_map/ppermute | solution.py:319
  36.9 0.0 collective-permute-done.8.edge_ref
  36.9 0.1 shard_map.110.spread_ref
  37.0 3.2 %collective-permute-done.7 = bf16[160,128]{1,0:T(8,128)(2,1)S(1)} collective-permute-done((bf16[160,128]{1,0:T(8,128)(2,1)S(1)}, bf16[160,128]{1,0:T(8,128)(2,1)S(1)}, u32[]{:S(2)}, u32[]{:S(2)}) %collective-permute-start.7) | collective-permute-done | bytes 40992 | tf_op jit(solution)/shard_map/ppermute | solution.py:319
  40.2 2.7 %collective-permute-start.9 = (bf16[160,128]{1,0:T(8,128)(2,1)S(1)}, bf16[160,128]{1,0:T(8,128)(2,1)S(1)}, u32[]{:S(2)}, u32[]{:S(2)}) collective-permute-start(bf16[160,128]{1,0:T(8,128)(2,1)S(1)} %add_convert_fusion.1), channel_id=1, source_target_pairs={{0,16},{4,20},{8,24},{12,28},{16,0},{20,4},{24,8},{28,12},{1,17},{... | collective-permute-start | bytes 122888 | tf_op jit(solution)/shard_map/ppermute | solution.py:319
  42.9 1.0 %collective-permute-done.10.even_ref = bf16[16,64,128]{2,1,0:T(8,128)(2,1)S(1)} collective-permute-done((bf16[16,64,128]{2,1,0:T(8,128)(2,1)S(1)}, bf16[16,64,128]{2,1,0:T(8,128)(2,1)S(1)}, u32[]{:S(2)}, u32[]{:S(2)}) %collective-permute-start.10) | collective-permute-done | bytes 262176 | tf_op jit(solution)/shard_map/ppermute | solution.py:411
  43.9 1.2 %shard_map.112 = bf16[128,16,128]{2,1,0:T(8,128)(2,1)} custom-call(f32[16,128,128]{2,1,0:T(8,128)S(1)} %shard_map.110.spread_ref, bf16[16,64,128]{2,1,0:T(8,128)(2,1)S(1)} %collective-permute-done.10.even_ref, bf16[16,128,128]{2,1,0:T(8,128)(2,1)S(1)} %get-tuple-element.87.cot_ref), custom_call_target="tpu_custom_call" | custom-call | flops 68719476736 | bytes 1 | tf_op jit(solution)/shard_map/pallas_call | solution.py:30
  45.0 0.2 collective-permute-done.9
  45.2 2.4 %collective-permute-start.11 = (bf16[160,128]{1,0:T(8,128)(2,1)S(1)}, bf16[160,128]{1,0:T(8,128)(2,1)S(1)}, u32[]{:S(2)}, u32[]{:S(2)}) collective-permute-start(bf16[160,128]{1,0:T(8,128)(2,1)S(1)} %add_convert_fusion), channel_id=1, source_target_pairs={{0,4},{4,0},{8,12},{12,8},{16,20},{20,16},{24,28},{28,24},{1,5},{5... | collective-permute-start | bytes 122888 | tf_op jit(solution)/shard_map/ppermute | solution.py:319
  47.6 2.0 %collective-permute-done.11 = bf16[160,128]{1,0:T(8,128)(2,1)S(1)} collective-permute-done((bf16[160,128]{1,0:T(8,128)(2,1)S(1)}, bf16[160,128]{1,0:T(8,128)(2,1)S(1)}, u32[]{:S(2)}, u32[]{:S(2)}) %collective-permute-start.11) | collective-permute-done | bytes 40992 | tf_op jit(solution)/shard_map/ppermute | solution.py:319
  49.6 0.1 collective-permute-start.12
  49.7 1.3 %collective-permute-done.12.other_ref = f32[160,128]{1,0:T(8,128)S(1)} collective-permute-done((f32[160,128]{1,0:T(8,128)S(1)}, f32[160,128]{1,0:T(8,128)S(1)}, u32[]{:S(2)}, u32[]{:S(2)}) %collective-permute-start.12) | collective-permute-done | bytes 81952 | tf_op jit(solution)/shard_map/ppermute | solution.py:319
  51.0 0.7 %shard_map.113 = (f32[128,128]{1,0:T(8,128)}, f32[128,128]{1,0:T(8,128)}, f32[64,128]{1,0:T(8,128)}) custom-call(f32[160,128]{1,0:T(8,128)S(1)} %convert_add_fusion.mine_ref, f32[160,128]{1,0:T(8,128)S(1)} %collective-permute-done.12.other_ref, f32[8,128]{1,0:T(8,128)S(1)} %shard_map.111.mark_ref), custom_call_target="tpu_custom_call" | custom-call | flops 1 | bytes 1 | tf_op jit(solution)/shard_map/pallas_call | solution.py:30
  (13 shorter events, 0.1 us)
Async XLA Ops:
  0.6 6.7 %collective-permute-start.1 = (bf16[128,16,128]{2,1,0:T(8,128)(2,1)}, bf16[128,16,128]{2,1,0:T(8,128)(2,1)S(1)}, u32[]{:S(2)}, u32[]{:S(2)}) collective-permute-start(bf16[128,16,128]{2,1,0:T(8,128)(2,1)} %cot_src.1), channel_id=1, source_target_pairs={{0,1},{1,0},{2,3},{3,2},{4,5},{5,4},{6,7},{7,6},{8,9},{9,8},{10,11... | collective-permute-start | bytes 1572872 | tf_op jit(solution)/shard_map/ppermute | solution.py:319
  1.1 15.3 %collective-permute-start = (bf16[128,16,128]{2,1,0:T(8,128)(2,1)}, bf16[128,16,128]{2,1,0:T(8,128)(2,1)S(1)}, u32[]{:S(2)}, u32[]{:S(2)}) collective-permute-start(bf16[128,16,128]{2,1,0:T(8,128)(2,1)} %cot_src.1), channel_id=1, source_target_pairs={{0,2},{1,3},{2,0},{3,1},{4,6},{5,7},{6,4},{7,5},{8,10},{9,11},{10,... | collective-permute-start | bytes 1572872 | tf_op jit(solution)/shard_map/ppermute | solution.py:319
  5.1 13.2 %collective-permute-start.3 = (bf16[16,64,128]{2,1,0:T(8,128)(2,1)S(1)}, bf16[16,64,128]{2,1,0:T(8,128)(2,1)S(1)}, u32[]{:S(2)}, u32[]{:S(2)}) collective-permute-start(bf16[16,64,128]{2,1,0:T(8,128)(2,1)S(1)} %get-tuple-element.52), channel_id=1, source_target_pairs={{0,4},{4,0},{8,12},{12,8},{16,20},{20,16},{24,28},{28,24},{1,5},{5... | collective-permute-start | bytes 786440 | tf_op jit(solution)/shard_map/ppermute | solution.py:345
  6.7 11.6 %collective-permute-start.4 = (bf16[16,64,128]{2,1,0:T(8,128)(2,1)S(1)}, bf16[16,64,128]{2,1,0:T(8,128)(2,1)S(1)}, u32[]{:S(2)}, u32[]{:S(2)}) collective-permute-start(bf16[16,64,128]{2,1,0:T(8,128)(2,1)S(1)} %get-tuple-element.53), channel_id=1, source_target_pairs={{4,8},{12,16},{20,24},{8,4},{16,12},{24,20},{0,0},{28,28},{5,9},{1... | collective-permute-start | bytes 786440 | tf_op jit(solution)/shard_map/ppermute | solution.py:344
  16.4 2.6 %collective-permute-start.2 = (bf16[128,16,128]{2,1,0:T(8,128)(2,1)S(1)}, bf16[128,16,128]{2,1,0:T(8,128)(2,1)S(1)}, u32[]{:S(2)}, u32[]{:S(2)}) collective-permute-start(bf16[128,16,128]{2,1,0:T(8,128)(2,1)S(1)} %collective-permute-done.block_ref), channel_id=1, source_target_pairs={{0,1},{1,0},{2,3},{3,2},{4,5},{5,4},{6,7},{7,6},{8,9},{9,8},{10,11... | collective-permute-start | bytes 1572872 | tf_op jit(solution)/shard_map/ppermute | solution.py:319
  26.8 1.5 %collective-permute-start.5 = (f32[160,128]{1,0:T(8,128)S(1)}, f32[160,128]{1,0:T(8,128)S(1)}, u32[]{:S(2)}, u32[]{:S(2)}) collective-permute-start(f32[160,128]{1,0:T(8,128)S(1)} %get-tuple-element.76), channel_id=1, source_target_pairs={{0,1},{1,0},{2,3},{3,2},{4,5},{5,4},{6,7},{7,6},{8,9},{9,8},{10,11... | collective-permute-start | bytes 245768 | tf_op jit(solution)/shard_map/ppermute | solution.py:319
  27.4 9.5 %collective-permute-start.8 = (bf16[16,64,128]{2,1,0:T(8,128)(2,1)S(1)}, bf16[16,64,128]{2,1,0:T(8,128)(2,1)S(1)}, u32[]{:S(2)}, u32[]{:S(2)}) collective-permute-start(bf16[16,64,128]{2,1,0:T(8,128)(2,1)S(1)} %get-tuple-element.81), channel_id=1, source_target_pairs={{4,8},{12,16},{20,24},{8,4},{16,12},{24,20},{0,0},{28,28},{5,9},{1... | collective-permute-start | bytes 786440 | tf_op jit(solution)/shard_map/ppermute | solution.py:410
  28.3 5.9 %collective-permute-start.6 = (bf16[160,128]{1,0:T(8,128)(2,1)S(1)}, bf16[160,128]{1,0:T(8,128)(2,1)S(1)}, u32[]{:S(2)}, u32[]{:S(2)}) collective-permute-start(bf16[160,128]{1,0:T(8,128)(2,1)S(1)} %convert_element_type.36), channel_id=1, source_target_pairs={{0,2},{1,3},{2,0},{3,1},{4,6},{5,7},{6,4},{7,5},{8,10},{9,11},{10,... | collective-permute-start | bytes 122888 | tf_op jit(solution)/shard_map/ppermute | solution.py:319
  30.2 13.7 %collective-permute-start.10 = (bf16[16,64,128]{2,1,0:T(8,128)(2,1)S(1)}, bf16[16,64,128]{2,1,0:T(8,128)(2,1)S(1)}, u32[]{:S(2)}, u32[]{:S(2)}) collective-permute-start(bf16[16,64,128]{2,1,0:T(8,128)(2,1)S(1)} %get-tuple-element.86), channel_id=1, source_target_pairs={{0,4},{4,0},{8,12},{12,8},{16,20},{20,16},{24,28},{28,24},{1,5},{5... | collective-permute-start | bytes 786440 | tf_op jit(solution)/shard_map/ppermute | solution.py:411
  34.2 6.0 %collective-permute-start.7 = (bf16[160,128]{1,0:T(8,128)(2,1)S(1)}, bf16[160,128]{1,0:T(8,128)(2,1)S(1)}, u32[]{:S(2)}, u32[]{:S(2)}) collective-permute-start(bf16[160,128]{1,0:T(8,128)(2,1)S(1)} %get-tuple-element.95), channel_id=1, source_target_pairs={{0,8},{4,12},{8,0},{12,4},{16,24},{20,28},{24,16},{28,20},{1,9},{5... | collective-permute-start | bytes 122888 | tf_op jit(solution)/shard_map/ppermute | solution.py:319
  40.2 5.0 %collective-permute-start.9 = (bf16[160,128]{1,0:T(8,128)(2,1)S(1)}, bf16[160,128]{1,0:T(8,128)(2,1)S(1)}, u32[]{:S(2)}, u32[]{:S(2)}) collective-permute-start(bf16[160,128]{1,0:T(8,128)(2,1)S(1)} %add_convert_fusion.1), channel_id=1, source_target_pairs={{0,16},{4,20},{8,24},{12,28},{16,0},{20,4},{24,8},{28,12},{1,17},{... | collective-permute-start | bytes 122888 | tf_op jit(solution)/shard_map/ppermute | solution.py:319
  45.2 4.4 %collective-permute-start.11 = (bf16[160,128]{1,0:T(8,128)(2,1)S(1)}, bf16[160,128]{1,0:T(8,128)(2,1)S(1)}, u32[]{:S(2)}, u32[]{:S(2)}) collective-permute-start(bf16[160,128]{1,0:T(8,128)(2,1)S(1)} %add_convert_fusion), channel_id=1, source_target_pairs={{0,4},{4,0},{8,12},{12,8},{16,20},{20,16},{24,28},{28,24},{1,5},{5... | collective-permute-start | bytes 122888 | tf_op jit(solution)/shard_map/ppermute | solution.py:319
  49.6 1.3 %collective-permute-start.12 = (f32[160,128]{1,0:T(8,128)S(1)}, f32[160,128]{1,0:T(8,128)S(1)}, u32[]{:S(2)}, u32[]{:S(2)}) collective-permute-start(f32[160,128]{1,0:T(8,128)S(1)} %convert_add_fusion.mine_ref), channel_id=1, source_target_pairs={{0,1},{1,0},{2,3},{3,2},{4,5},{5,4},{6,7},{7,6},{8,9},{9,8},{10,11... | collective-permute-start | bytes 245768 | tf_op jit(solution)/shard_map/ppermute | solution.py:319

commit v4 on v3

--- a/solution.py
+++ b/solution.py
@@ -14,10 +14,12 @@
 LIMIT = 16 << 20
 
 
-def call(body, outs, *args, scratch=(), far=(), cost=1, kept=None):
+def call(body, outs, *args, scratch=(), far=(), cost=1, kept=None, anywhere=()):
     specs = [VMEM] * len(args)
     results = [VMEM] * len(outs)
     args = list(args)
+    for i in anywhere:
+        specs[i] = pl.BlockSpec(memory_space=pl.ANY)
     aliases = {}
     if kept is not None:
         results[kept[1]] = pl.BlockSpec(memory_space=pl.ANY)
@@ -53,18 +55,22 @@
     return copies
 
 
-def split_body(source_ref, own_ref, near_ref, far_ref, feat_ref, sems):
-    rows = feat_ref.shape[0]
-    half = near_ref.shape[1]
+def edge_body(even, source_ref, edge_ref, feat_ref, sems):
+    half = feat_ref.shape[0]
     odd = lax.axis_index("bus") & 1
-    for copy in load_all(sems, [(source_ref, feat_ref)]):
+    first = pl.multiple_of((1 - odd if even else odd) * half, half)
+    copies = load_all(
+        sems,
+        [
+            (source_ref.at[pl.ds(first + start, 16)], feat_ref.at[pl.ds(start, 16)])
+            for start in range(0, half, 16)
+        ],
+    )
+    for copy, start in zip(copies, range(0, half, 16)):
         copy.wait()
-    for start in range(0, rows, 16):
-        part = jnp.swapaxes(feat_ref[start : start + 16].astype(F32), 0, 1).astype(BF)
-        own_ref[:, start : start + 16] = part
-    low, high = pl.multiple_of(odd * half, half), pl.multiple_of((1 - odd) * half, half)
-    near_ref[...] = own_ref[:, pl.ds(high, half)]
-    far_ref[...] = own_ref[:, pl.ds(low, half)]
+        edge_ref[:, start : start + 16] = jnp.swapaxes(
+            feat_ref[start : start + 16].astype(F32), 0, 1
+        ).astype(BF)
 
 
 def take_block(block_ref, wout, steady, part, conv, valid=None):
@@ -143,8 +149,7 @@
     for i in range(blocks):
         for k in range(slots):
             place = ids_ref[i, k] - first
-            edge = (place == 0) | (place == blocks + 1)
-            place = jnp.where(turned & edge, blocks + 1 - place, place)
+            place = jnp.where(turned, blocks + 1 - place, place)
             dense[i, place] += coup_ref[i, k].astype(F32)
     full = jnp.concatenate(
         [
@@ -159,35 +164,70 @@
         copy.wait()
 
 
-def add_body(last, sum_ref, crossed_ref, block_ref, lags_ref, wout_ref, out_ref, cross_ref, steady, part, conv, sems):
+def far_body(sum_ref, crossed_ref, block_ref, lags_ref, wout_ref, out_ref, cross_ref, steady, part, conv, sems):
     steps, rows, chans = conv.shape
-    slot = 3 - 2 * (lax.axis_index("tm") & 1) if last else 2
-    valid = lax.axis_index("tm") < 2
-    take_block(block_ref, wout_ref[...], steady, part, conv, valid)
-    sent = place_part(part, cross_ref, slot, sems.at[0])
+    take_block(block_ref, wout_ref[...], steady, part, conv, lax.axis_index("tm") < 2)
+    sent = place_part(part, cross_ref, 2, sems.at[0])
 
     def tile(index, carry):
         where = pl.ds(pl.multiple_of(index * 16, 16), 16)
         sums = [[sum_ref[s, where, :][:8], sum_ref[s, where, :][8:]] for s in range(steps)]
-        add_lags(sums, conv, lags_ref, slot * steps, where, False)
+        add_lags(sums, conv, lags_ref, 2 * steps, where, False)
         for s in range(steps):
-            out_ref[s, where, :] = jnp.concatenate(sums[s], axis=0).astype(out_ref.dtype)
+            out_ref[s, where, :] = jnp.concatenate(sums[s], axis=0)
         return carry
 
     lax.fori_loop(0, rows // 16, tile, 0)
     sent.wait()
 
 
-def forward_body(
-    own_ref, before_ref, after_ref, mix_ref, wg_ref, act_ref, slope_ref, mixed_ref
+def lag_steps(sum_ref, conv, lags, base, grad_ref, start):
+    steps = grad_ref.shape[0]
+    where = slice(start, start + 16)
+    sums = []
+    for s in range(steps):
+        value = sum_ref[s, where, :]
+        sums.append([value[:8], value[8:]])
+    for t in range(steps):
+        value = conv[t, where, :].astype(F32)
+        for s in range(steps):
+            tap = lags[base + (t - s)]
+            sums[s][0] += tap * value[:8]
+            sums[s][1] += tap * value[8:]
+        yield
+    for s in range(steps):
+        grad_ref[s, where, :] = jnp.concatenate(sums[s], axis=0).astype(BF)
+    yield
+
+
+def tail_body(
+    even_own, odd_own, even_ref, odd_ref, mix_ref, mixt_ref, wg_ref, wout_ref, taps_ref, lags_ref,
+    sum_ref, swapped_ref, crossed_ref, mark_ref,
+    keep_ref, send_ref, spread_ref, even_out, odd_out,
+    slope_ref, mixed_ref, stack, steady, conv, cross, window, grad_ref, pack, sems,
 ):
-    steps, rows, chans = own_ref.shape
+    steps, rows, chans = mixed_ref.shape
+    half = even_ref.shape[1]
+    pairs = cross.shape[0]
+    tm = lax.axis_index("tm")
+    odd = tm & 1
+    block = steps // 2
+    near_at, slot = 1 + 2 * odd, 3 - 2 * odd
+    copies = []
+    for i, at in enumerate((0, near_at, 2)):
+        where = pl.ds(at * block, block)
+        copies.append(pltpu.make_async_copy(crossed_ref.at[where], cross.at[where], sems.at[i]))
+        copies[-1].start()
+
     group = 4
     mix, wg = mix_ref[...], wg_ref[...]
+    zero = jnp.zeros((rows, chans), BF)
+    stack[0, 0:rows, chans : 2 * chans] = zero
+    stack[block, 0:rows, 0:chans] = zero
     for s in range(0, steps, group):
         ext = jnp.concatenate(
             [
-                jnp.concatenate([before_ref[t], own_ref[t], after_ref[t]], axis=0)
+                jnp.concatenate([even_ref[t], even_own[t], odd_own[t], odd_ref[t]], axis=0)
                 for t in range(s, s + group)
             ],
             axis=1,
@@ -199,18 +239,48 @@
         mixed_ref[s : s + group] = mixed.reshape(group, rows, chans)
         pre = dot(mixed, wg)
         gate = 1.0 / (1.0 + jnp.exp(-pre))
-        act_ref[s : s + group] = (pre * gate).astype(BF).reshape(group, rows, chans)
+        act = (pre * gate).astype(BF).reshape(group, rows, chans)
         slope = gate * (1.0 + pre * (1.0 - gate))
         slope_ref[s : s + group] = slope.reshape(group, rows, chans)
-
-
-def backward_body(
-    grad_ref, slope_ref, mixed_ref, mixt_ref, wg_ref, spread_ref, down_ref, up_ref, graph_ref
-):
-    steps, rows, chans = grad_ref.shape
-    half = down_ref.shape[1]
-    group = 4
-    mixt, wg = mixt_ref[...], wg_ref[...]
+        for t in range(s, s + group):
+            low = (t % 2) * rows
+            stack[t // 2, low : low + rows, 0:chans] = act[t - s]
+            low = ((t + 1) % 2) * rows
+            stack[(t + 1) // 2, low : low + rows, chans : 2 * chans] = act[t - s]
+
+    take_block(swapped_ref, wout_ref[...], steady, cross.at[pl.ds(slot * block, block)], conv, tm < 2)
+    window[0:31] = lags_ref[pl.ds(slot * steps - 15, 31)]
+    for copy in copies:
+        copy.wait()
+
+    weight = wout_ref[...].astype(F32).T
+    taps = taps_ref[...].astype(F32)
+    out = jnp.zeros((chans, chans), F32)
+    found = []
+    for at in range(0, pairs, group):
+        work = lag_steps(sum_ref, conv, window, 15, grad_ref, at * 4)
+        total = [None] * group
+        for i in range(block + 1):
+            count = min(group, pairs - at - i)
+            if count > 0:
+                depth = 2 * rows if i < block else rows
+                left = cross[at + i : at + i + count, :, 0:depth].reshape(count * rows, depth)
+                part = dot(left, stack[i, 0:depth])
+                for g in range(count):
+                    piece = part[g * rows : (g + 1) * rows]
+                    total[g] = piece if total[g] is None else total[g] + piece
+            for _ in range(2):
+                next(work, None)
+        for _ in work:
+            pass
+        for g in range(group):
+            for side in range(2):
+                lag = 2 * (at + g) + side
+                part = total[g][:, side * chans : (side + 1) * chans]
+                out += part * taps[lag : lag + 1]
+                found.append(jnp.sum(part * weight, axis=0, keepdims=True))
+
+    mixt = mixt_ref[...]
     graph = jnp.zeros((chans, chans), F32)
     for s in range(0, steps, group):
         grad = grad_ref[s : s + group].astype(F32) * slope_ref[s : s + group]
@@ -224,79 +294,45 @@
         spread = dot(mixt, grad_mixed)
         for t in range(group):
             part = spread[:, t * chans : (t + 1) * chans]
-            down_ref[s + t] = part[:half].astype(BF)
+            even_out[s + t] = part[:half].astype(BF)
             spread_ref[s + t] = part[half : half + rows]
-            up_ref[s + t] = part[half + rows :].astype(BF)
-    graph_ref[...] = graph
-
-
-def lag_body(act_ref, cross_ref, taps_ref, wout_ref, graph_ref, keep_ref, send_ref, stack, pack):
-    steps, rows, chans = act_ref.shape
-    pairs = cross_ref.shape[0]
-    group = steps // 2
-    zero = jnp.zeros((rows, chans), BF)
-    for i in range(group + 1):
-        s = 2 * i
-        if s < steps:
-            stack[i, 0:rows, 0:chans] = act_ref[s]
-            stack[i, rows : 2 * rows, 0:chans] = act_ref[s + 1]
-            stack[i, rows : 2 * rows, chans : 2 * chans] = act_ref[s]
-        else:
-            stack[i, 0:rows, 0:chans] = zero
-        stack[i, 0:rows, chans : 2 * chans] = act_ref[s - 1] if s > 0 else zero
-    weight = wout_ref[...].astype(F32).T
-    taps = taps_ref[...].astype(F32)
-    out = jnp.zeros((chans, chans), F32)
-    found = []
-    for at in range(0, pairs, group):
-        total = [None] * group
-        for i in range(group + 1):
-            count = min(group, pairs - at - i)
-            if count <= 0:
-                continue
-            depth = 2 * rows if i < group else rows
-            left = cross_ref[at + i : at + i + count, :, 0:depth].reshape(count * rows, depth)
-            part = dot(left, stack[i, 0:depth])
-            for g in range(count):
-                piece = part[g * rows : (g + 1) * rows]
-                total[g] = piece if total[g] is None else total[g] + piece
-        for g in range(group):
-            for side in range(2):
-                lag = 2 * (at + g) + side
-                part = total[g][:, side * chans : (side + 1) * chans]
-                out += part * taps[lag : lag + 1]
-                found.append(jnp.sum(part * weight, axis=0, keepdims=True))
-    pack[0:chans] = graph_ref[...]
+            odd_out[s + t] = part[half + rows :].astype(BF)
+
+    pack[0:chans] = graph
     pack[chans : 2 * chans] = out.T
     pack[2 * chans :] = jnp.concatenate(found, axis=0)
-    odd = lax.axis_index("tm") & 1
     size = keep_ref.shape[0]
     keep_ref[...] = pack[pl.ds(pl.multiple_of(odd * size, size), size)]
     send_ref[...] = pack[pl.ds(pl.multiple_of((1 - odd) * size, size), size)]
 
 
-def fold_body(low_bus, spread_ref, edge_ref, out_ref):
-    half = edge_ref.shape[1]
+def mark_body(first_ref, second_ref, mark_ref):
+    mark_ref[...] = first_ref[0, 0:8].astype(F32) + second_ref[0, 0:8].astype(F32)
+
+
+def fold_body(spread_ref, odd_edge_ref, cot_ref, out_ref):
+    half = odd_edge_ref.shape[1]
     odd = lax.axis_index("bus") & 1
-    at = pl.multiple_of((odd if low_bus else 1 - odd) * half, half)
-    rest = pl.multiple_of((1 - odd if low_bus else odd) * half, half)
+    low, high = pl.multiple_of(odd * half, half), pl.multiple_of((1 - odd) * half, half)
     for s in range(spread_ref.shape[0]):
-        out_ref[s, pl.ds(rest, half)] = spread_ref[s, pl.ds(rest, half)]
-        out_ref[s, pl.ds(at, half)] = spread_ref[s, pl.ds(at, half)] + edge_ref[s].astype(F32)
-
-
-def final_body(spread_ref, even_ref, cot_ref, out_ref, sum_ref):
-    rows = spread_ref.shape[1]
+        out_ref[s, :half] = spread_ref[s, :half] + cot_ref[s, pl.ds(high, half)].astype(F32)
+        out_ref[s, half:] = (
+            spread_ref[s, half:]
+            + cot_ref[s, pl.ds(low, half)].astype(F32)
+            + odd_edge_ref[s].astype(F32)
+        )
+
+
+def final_body(spread_ref, even_ref, out_ref):
     half = even_ref.shape[1]
     odd = lax.axis_index("bus") & 1
-    for start in range(0, rows, 16):
-        sum_ref[:, start : start + 16] = spread_ref[:, start : start + 16] + cot_ref[
-            :, start : start + 16
-        ].astype(F32)
-    at = pl.multiple_of((1 - odd) * half, half)
-    sum_ref[:, pl.ds(at, half)] += even_ref[...].astype(F32)
-    for start in range(0, rows, 16):
-        out_ref[start : start + 16] = jnp.swapaxes(sum_ref[:, start : start + 16], 0, 1).astype(BF)
+    for start in range(0, half, 16):
+        part = spread_ref[:, start : start + 16] + even_ref[:, start : start + 16].astype(F32)
+        where = pl.ds((1 - odd) * half + start, 16)
+        out_ref[where] = jnp.swapaxes(part, 0, 1).astype(BF)
+        part = spread_ref[:, half + start : half + start + 16]
+        where = pl.ds(odd * half + start, 16)
+        out_ref[where] = jnp.swapaxes(part, 0, 1).astype(BF)
 
 
 def pause_body(value_ref, last_ref, out_ref):
@@ -336,13 +372,20 @@
     edge = (steps, half, chans)
     square = (chans, chans)
 
-    own, even_edge, odd_edge = call(
-        split_body, [(wide, BF), (edge, BF), (edge, BF)], features,
-        scratch=[pltpu.VMEM(features.shape, BF), pltpu.SemaphoreType.DMA((1,))], far=[0],
-    )
+    def edge_of(even):
+        (found,) = call(
+            functools.partial(edge_body, even), [(edge, BF)], features,
+            scratch=[
+                pltpu.VMEM((half,) + features.shape[1:], BF), pltpu.SemaphoreType.DMA((half // 16,))
+            ],
+            far=[0],
+        )
+        return found
+
+    even_own, odd_own = edge_of(True), edge_of(False)
     near = swap(cotangent, "tm", 1)
-    odd_edge = lax.ppermute(odd_edge, "bus", odds)
-    even_edge = lax.ppermute(even_edge, "bus", evens)
+    odd_edge = lax.ppermute(odd_own, "bus", odds)
+    even_edge = lax.ppermute(even_own, "bus", evens)
     far = swap(cotangent, "tm", 2)
 
     pairs = total // 2
@@ -367,63 +410,54 @@
         far=range(6), kept=(None, 1),
     )
 
-    def add_block(last, dtype, sums, crossed, block):
-        return call(
-            functools.partial(add_body, last), [(wide, dtype), (crossing, BF)],
-            sums, crossed, block, lags, wout,
-            scratch=[
-                pltpu.VMEM(wide, BF), part, pltpu.VMEM(wide, BF), pltpu.SemaphoreType.DMA((1,))
-            ],
-            kept=(1, 1),
-        )
-
     far, sums = lax.optimization_barrier((far, sums))
     swapped = swap(far, "tm", 1)
-    sums, crossed = add_block(False, F32, sums, crossed, far)
+    sums, crossed = call(
+        far_body, [(wide, F32), (crossing, BF)], sums, crossed, far, lags, wout,
+        scratch=[
+            pltpu.VMEM(wide, BF), part, pltpu.VMEM(wide, BF), pltpu.SemaphoreType.DMA((1,))
+        ],
+        kept=(1, 1),
+    )
     even_edge, odd_edge, sums = lax.optimization_barrier((even_edge, odd_edge, sums))
-    act, slope, mixed = call(
-        forward_body, [(wide, BF), (wide, F32), (wide, BF)], own, even_edge, odd_edge, mix, wg,
-        cost=1 << 36,
-    )
-    swapped, act = lax.optimization_barrier((swapped, act))
-    grad_act, crossed = add_block(True, BF, sums, crossed, swapped)
-    spread, even_grad, odd_grad, part_graph = call(
-        backward_body,
-        [(wide, F32), (edge, BF), (edge, BF), (square, F32)],
-        grad_act, slope, mixed, mixt, wg,
-    )
-
+    (mark,) = call(mark_body, [((8, chans), F32)], even_edge, odd_edge, cost=1 << 36)
+    swapped, mark = lax.optimization_barrier((swapped, mark))
     size = (2 * chans + total) // 2
-    keep, send = call(
-        lag_body, [((size, chans), F32), ((size, chans), F32)],
-        act, crossed, taps, wout, part_graph,
+    keep, send, spread, even_grad, odd_grad = call(
+        tail_body,
+        [((size, chans), F32), ((size, chans), F32), (wide, F32), (edge, BF), (edge, BF)],
+        even_own, odd_own, even_edge, odd_edge, mix, mixt, wg, wout, taps, lags,
+        sums, swapped, crossed, mark,
         scratch=[
+            pltpu.VMEM(wide, F32), pltpu.VMEM(wide, BF),
             pltpu.VMEM((steps // 2 + 1, 2 * rows, 2 * chans), BF),
-            pltpu.VMEM((2 * size, chans), F32),
-        ],
+            pltpu.VMEM(wide, BF), pltpu.VMEM(wide, BF), pltpu.VMEM(crossing, BF),
+            pltpu.VMEM((32, 8, chans), F32), pltpu.VMEM(wide, BF),
+            pltpu.VMEM((2 * size, chans), F32), pltpu.SemaphoreType.DMA((3,)),
+        ],
+        anywhere=[12],
     )
     mark = send[0:8]
     keep = keep + swap(send, "tm", 1)
-    keep, even_grad = lax.optimization_barrier((keep, even_grad))
     hops = [("tm", 1 << bit) for bit in range(1, tm.bit_length() - 1)]
     hops += [("bus", 1 << bit) for bit in range(1, bus.bit_length() - 1)] + [("bus", 1)]
     odd_grad = lax.ppermute(odd_grad, "bus", odds)
-    even_grad = lax.ppermute(even_grad, "bus", evens)
     for place, (axis, distance) in enumerate(hops):
         sent = keep.astype(BF)
         received = swap(sent, axis, distance)
-        if place == 0:
+        if place < len(hops) - 2:
             received, mark = pause(keep, received, mark)
-        if place == 1:
+            if place == 0:
+                even_grad, mark = lax.optimization_barrier((even_grad, mark))
+                even_grad = lax.ppermute(even_grad, "bus", evens)
+        elif place == len(hops) - 2:
             (spread,) = call(
-                functools.partial(fold_body, True), [(wide, F32)], spread, odd_grad, cost=1 << 30
+                fold_body, [(wide, F32)], spread, odd_grad, steady, cost=1 << 36
             )
-            spread, mark = lax.optimization_barrier((spread, mark))
-            received, mark = pause(keep, received, mark)
-        if place == len(hops) - 2:
+            received, spread = lax.optimization_barrier((received, spread))
+        else:
             (grad_features,) = call(
-                final_body, [(features.shape, BF)], spread, even_grad, steady,
-                scratch=[pltpu.VMEM(wide, F32)], cost=1 << 36,
+                final_body, [(features.shape, BF)], spread, even_grad, cost=1 << 36
             )
             received, grad_features = lax.optimization_barrier((received, grad_features))
         keep = sent.astype(F32) + received.astype(F32)

time: 51.8 us -> 50.4 us (0.973)
  starting transfers between devices: 20.2 us -> 18.1 us
  waiting for transfers between devices: 12.4 us -> 13.3 us
    ppermute x1, starting transfers between devices: 4.04 us -> 1.64 us  [shards(): even_grad = lax.ppermute(even_grad, 'bus', evens)]
    ppermute x9, waiting for transfers between devices: 11.4 us -> 13.3 us  [swap(): return lax.ppermute(value, axis, [(i, i ^ distance) for i in range(size)])]
    ppermute x1, waiting for transfers between devices: 1 us -> 0.01 us  [shards(): even_grad = lax.ppermute(even_grad, 'bus', evens)]
    pallas_call x12 -> x11, Pallas kernels: 18.2 us -> 17.9 us  [call(): pl.pallas_call(body, out_shape=[jax.ShapeDtypeStruct(shape, dtype) for sh...]
  transfers between devices with their start and end apart: 13 -> 13, of which waited for: 7 -> 8; matrix products, arithmetic and copies ran while one was open for 0% -> 0% of each run, Pallas kernels for 19% -> 19%
where the time goes in v4:
time: 50.4 us; the launch traced here: 50.1 us
  starting transfers between devices  18.1 us (36%)
  Pallas kernels  17.9 us (36%)
  waiting for transfers between devices  13.3 us (26%)
  between operations  0.75 us (1%)
    pallas_call x11, Pallas kernels, call(): pl.pallas_call(body, out_shape=[jax.ShapeDtypeStruct(shape, dtype) for sh...  17.9 us
    ppermute x9, starting transfers between devices, swap(): return lax.ppermute(value, axis, [(i, i ^ distance) for i in range(size)])  13.5 us
    ppermute x9, waiting for transfers between devices, swap(): return lax.ppermute(value, axis, [(i, i ^ distance) for i in range(size)])  13.3 us
    ppermute x1, starting transfers between devices, shards(): even_grad = lax.ppermute(even_grad, 'bus', evens)  1.64 us
    ppermute x1, starting transfers between devices, shards(): even_edge = lax.ppermute(even_own, 'bus', evens)  1.58 us
  transfers between devices with their start and end apart: 13, of which 8 were waited for; matrix products, arithmetic and copies ran while one was open for 0% of the time, Pallas kernels for 19%

profile of v4, /device:TPU:0, one launch (start us, length us, event | category | flops | bytes accessed | tf_op | source)
XLA Modules:
  0.0 50.1 jit_solution(12324025542356363243)
XLA Ops:
  0.6 0.5 %collective-permute-start.3 = (bf16[128,16,128]{2,1,0:T(8,128)(2,1)}, bf16[128,16,128]{2,1,0:T(8,128)(2,1)S(1)}, u32[]{:S(2)}, u32[]{:S(2)}) collective-permute-start(bf16[128,16,128]{2,1,0:T(8,128)(2,1)} %cot_src.1), channel_id=1, source_target_pairs={{0,1},{1,0},{2,3},{3,2},{4,5},{5,4},{6,7},{7,6},{8,9},{9,8},{10,11... | collective-permute-start | bytes 1572872 | tf_op jit(solution)/shard_map/ppermute | solution.py:355
  1.1 2.6 %collective-permute-start.2 = (bf16[128,16,128]{2,1,0:T(8,128)(2,1)}, bf16[128,16,128]{2,1,0:T(8,128)(2,1)S(1)}, u32[]{:S(2)}, u32[]{:S(2)}) collective-permute-start(bf16[128,16,128]{2,1,0:T(8,128)(2,1)} %cot_src.1), channel_id=1, source_target_pairs={{0,2},{1,3},{2,0},{3,1},{4,6},{5,7},{6,4},{7,5},{8,10},{9,11},{10,... | collective-permute-start | bytes 1572872 | tf_op jit(solution)/shard_map/ppermute | solution.py:355
  3.7 1.0 %shard_map.102.even_own = bf16[16,64,128]{2,1,0:T(8,128)(2,1)S(1)} custom-call(bf16[128,16,128]{2,1,0:T(8,128)(2,1)} %source_ref.3), custom_call_target="tpu_custom_call" | custom-call | flops 1 | bytes 1 | tf_op jit(solution)/shard_map/pallas_call | solution.py:32
  4.7 1.6 %collective-permute-start = (bf16[16,64,128]{2,1,0:T(8,128)(2,1)S(1)}, bf16[16,64,128]{2,1,0:T(8,128)(2,1)S(1)}, u32[]{:S(2)}, u32[]{:S(2)}) collective-permute-start(bf16[16,64,128]{2,1,0:T(8,128)(2,1)S(1)} %shard_map.102.even_own), channel_id=1, source_target_pairs={{0,4},{4,0},{8,12},{12,8},{16,20},{20,16},{24,28},{28,24},{1,5},{5... | collective-permute-start | bytes 786440 | tf_op jit(solution)/shard_map/ppermute | solution.py:388
  6.3 1.0 %shard_map.103.odd_own = bf16[16,64,128]{2,1,0:T(8,128)(2,1)S(1)} custom-call(bf16[128,16,128]{2,1,0:T(8,128)(2,1)} %source_ref.3), custom_call_target="tpu_custom_call" | custom-call | flops 1 | bytes 1 | tf_op jit(solution)/shard_map/pallas_call | solution.py:32
  7.3 0.7 %collective-permute-start.1 = (bf16[16,64,128]{2,1,0:T(8,128)(2,1)S(1)}, bf16[16,64,128]{2,1,0:T(8,128)(2,1)S(1)}, u32[]{:S(2)}, u32[]{:S(2)}) collective-permute-start(bf16[16,64,128]{2,1,0:T(8,128)(2,1)S(1)} %shard_map.103.odd_own), channel_id=1, source_target_pairs={{4,8},{12,16},{20,24},{8,4},{16,12},{24,20},{0,0},{28,28},{5,9},{1... | collective-permute-start | bytes 786440 | tf_op jit(solution)/shard_map/ppermute | solution.py:387
  8.0 0.0 collective-permute-done.3.near_ref
  8.0 4.5 %shard_map.104 = (f32[16,128,128]{2,1,0:T(8,128)S(1)}, bf16[32,128,256]{2,1,0:T(8,128)(2,1)S(1)}, bf16[128,256]{1,0:T(8,128)(2,1)S(1)}, bf16[256,128]{1,0:T(8,12...) custom-call(s32[2,8]{1,0:T(2,128)} %ids_src.1, ...), custom_call_target="tpu_custom_call" | custom-call | flops 1 | bytes 1 | tf_op jit(solution)/shard_map/pallas_call | solution.py:32
  12.6 3.9 %collective-permute-done.2.block_ref = bf16[128,16,128]{2,1,0:T(8,128)(2,1)S(1)} collective-permute-done((bf16[128,16,128]{2,1,0:T(8,128)(2,1)}, bf16[128,16,128]{2,1,0:T(8,128)(2,1)S(1)}, u32[]{:S(2)}, u32[]{:S(2)}) %collective-permute-start.2) | collective-permute-done | bytes 524320 | tf_op jit(solution)/shard_map/ppermute | solution.py:355
  16.4 0.0 collective-permute-start.4
  16.4 1.8 %shard_map.105 = (f32[16,128,128]{2,1,0:T(8,128)S(1)}, bf16[32,128,256]{2,1,0:T(8,128)(2,1)S(1)}) custom-call(f32[16,128,128]{2,1,0:T(8,128)S(1)} %get-tuple-element.41.sum_ref, bf16[32,128,256]{2,1,0:T(8,128)(2,1)S(1)} %get-tuple-element.42.crossed_ref, bf16[128,16,128]{2,1,0:T(8,128)(2,1)S(1)} %collective-permute-done.2.block_ref, ...), custom_call_target="tpu_custom_call", output_to_operand_aliasing={{1}: (1, {})} | custom-call | flops 1 | bytes 1 | tf_op jit(solution)/shard_map/pallas_call | solution.py:32
  18.3 0.0 collective-permute-done.1.second_ref.odd_ref
  18.3 0.1 collective-permute-done.4.swapped_ref
  18.4 7.7 %shard_map.107 = (f32[160,128]{1,0:T(8,128)S(1)}, f32[160,128]{1,0:T(8,128)S(1)}, f32[16,128,128]{2,1,0:T(8,128)S(1)}, bf16[16,64,128]{2,1,0:T(8,128)(2,1)S(1)}, bf16[16,64,128]{2,1,0:T(8,128)(2,1)S(1)}) custom-call(bf16[16,64,128]{2,1,0:T(8,128)(2,1)S(1)} %shard_map.102.even_own, bf16[16,64,128]{2,1,0:T(8,128)(2,1)S(1)} %shard_map.103.odd_own, ...), custom_call_target="tpu_custom_call" | custom-call | flops 1 | bytes 1 | tf_op jit(solution)/shard_map/pallas_call | solution.py:32
  26.0 0.5 %collective-permute-start.5 = (f32[160,128]{1,0:T(8,128)S(1)}, f32[160,128]{1,0:T(8,128)S(1)}, u32[]{:S(2)}, u32[]{:S(2)}) collective-permute-start(f32[160,128]{1,0:T(8,128)S(1)} %get-tuple-element.58), channel_id=1, source_target_pairs={{0,1},{1,0},{2,3},{3,2},{4,5},{5,4},{6,7},{7,6},{8,9},{9,8},{10,11... | collective-permute-start | bytes 245768 | tf_op jit(solution)/shard_map/ppermute | solution.py:355
  26.6 0.7 %collective-permute-start.9 = (bf16[16,64,128]{2,1,0:T(8,128)(2,1)S(1)}, bf16[16,64,128]{2,1,0:T(8,128)(2,1)S(1)}, u32[]{:S(2)}, u32[]{:S(2)}) collective-permute-start(bf16[16,64,128]{2,1,0:T(8,128)(2,1)S(1)} %get-tuple-element.65), channel_id=1, source_target_pairs={{4,8},{12,16},{20,24},{8,4},{16,12},{24,20},{0,0},{28,28},{5,9},{1... | collective-permute-start | bytes 786440 | tf_op jit(solution)/shard_map/ppermute | solution.py:444
  27.2 0.2 collective-permute-done.5
  27.5 1.8 %collective-permute-start.6 = (bf16[160,128]{1,0:T(8,128)(2,1)S(1)}, bf16[160,128]{1,0:T(8,128)(2,1)S(1)}, u32[]{:S(2)}, u32[]{:S(2)}) collective-permute-start(bf16[160,128]{1,0:T(8,128)(2,1)S(1)} %get-tuple-element.76), channel_id=1, source_target_pairs={{0,2},{1,3},{2,0},{3,1},{4,6},{5,7},{6,4},{7,5},{8,10},{9,11},{10,... | collective-permute-start | bytes 122888 | tf_op jit(solution)/shard_map/ppermute | solution.py:355
  29.3 2.2 %collective-permute-done.6 = bf16[160,128]{1,0:T(8,128)(2,1)S(1)} collective-permute-done((bf16[160,128]{1,0:T(8,128)(2,1)S(1)}, bf16[160,128]{1,0:T(8,128)(2,1)S(1)}, u32[]{:S(2)}, u32[]{:S(2)}) %collective-permute-start.6) | collective-permute-done | bytes 40992 | tf_op jit(solution)/shard_map/ppermute | solution.py:355
  31.6 4.3 %collective-permute-start.7 = (bf16[160,128]{1,0:T(8,128)(2,1)S(1)}, bf16[160,128]{1,0:T(8,128)(2,1)S(1)}, u32[]{:S(2)}, u32[]{:S(2)}) collective-permute-start(bf16[160,128]{1,0:T(8,128)(2,1)S(1)} %get-tuple-element.79), channel_id=1, source_target_pairs={{0,8},{4,12},{8,0},{12,4},{16,24},{20,28},{24,16},{28,20},{1,9},{5... | collective-permute-start | bytes 122888 | tf_op jit(solution)/shard_map/ppermute | solution.py:355
  35.9 1.6 %collective-permute-start.11 = (bf16[16,64,128]{2,1,0:T(8,128)(2,1)S(1)}, bf16[16,64,128]{2,1,0:T(8,128)(2,1)S(1)}, u32[]{:S(2)}, u32[]{:S(2)}) collective-permute-start(bf16[16,64,128]{2,1,0:T(8,128)(2,1)S(1)} %get-tuple-element.69), channel_id=1, source_target_pairs={{0,4},{4,0},{8,12},{12,8},{16,20},{20,16},{24,28},{28,24},{1,5},{5... | collective-permute-start | bytes 786440 | tf_op jit(solution)/shard_map/ppermute | solution.py:452
  37.5 1.4 %collective-permute-done.7 = bf16[160,128]{1,0:T(8,128)(2,1)S(1)} collective-permute-done((bf16[160,128]{1,0:T(8,128)(2,1)S(1)}, bf16[160,128]{1,0:T(8,128)(2,1)S(1)}, u32[]{:S(2)}, u32[]{:S(2)}) %collective-permute-start.7) | collective-permute-done | bytes 40992 | tf_op jit(solution)/shard_map/ppermute | solution.py:355
  39.0 2.7 %collective-permute-start.8 = (bf16[160,128]{1,0:T(8,128)(2,1)S(1)}, bf16[160,128]{1,0:T(8,128)(2,1)S(1)}, u32[]{:S(2)}, u32[]{:S(2)}) collective-permute-start(bf16[160,128]{1,0:T(8,128)(2,1)S(1)} %add_convert_fusion.1), channel_id=1, source_target_pairs={{0,16},{4,20},{8,24},{12,28},{16,0},{20,4},{24,8},{28,12},{1,17},{... | collective-permute-start | bytes 122888 | tf_op jit(solution)/shard_map/ppermute | solution.py:355
  41.7 0.1 shard_map.110.spread_ref
  41.8 2.2 %collective-permute-done.8 = bf16[160,128]{1,0:T(8,128)(2,1)S(1)} collective-permute-done((bf16[160,128]{1,0:T(8,128)(2,1)S(1)}, bf16[160,128]{1,0:T(8,128)(2,1)S(1)}, u32[]{:S(2)}, u32[]{:S(2)}) %collective-permute-start.8) | collective-permute-done | bytes 40992 | tf_op jit(solution)/shard_map/ppermute | solution.py:355
  44.0 1.0 %collective-permute-start.10 = (bf16[160,128]{1,0:T(8,128)(2,1)S(1)}, bf16[160,128]{1,0:T(8,128)(2,1)S(1)}, u32[]{:S(2)}, u32[]{:S(2)}) collective-permute-start(bf16[160,128]{1,0:T(8,128)(2,1)S(1)} %add_convert_fusion), channel_id=1, source_target_pairs={{0,4},{4,0},{8,12},{12,8},{16,20},{20,16},{24,28},{28,24},{1,5},{5... | collective-permute-start | bytes 122888 | tf_op jit(solution)/shard_map/ppermute | solution.py:355
  45.0 0.0 collective-permute-done.11.even_ref
  45.0 1.0 %shard_map.111 = bf16[128,16,128]{2,1,0:T(8,128)(2,1)} custom-call(f32[16,128,128]{2,1,0:T(8,128)S(1)} %shard_map.110.spread_ref, bf16[16,64,128]{2,1,0:T(8,128)(2,1)S(1)} %collective-permute-done.11.even_ref), custom_call_target="tpu_custom_call" | custom-call | flops 68719476736 | bytes 1 | tf_op jit(solution)/shard_map/pallas_call | solution.py:32
  46.1 2.0 %collective-permute-done.10 = bf16[160,128]{1,0:T(8,128)(2,1)S(1)} collective-permute-done((bf16[160,128]{1,0:T(8,128)(2,1)S(1)}, bf16[160,128]{1,0:T(8,128)(2,1)S(1)}, u32[]{:S(2)}, u32[]{:S(2)}) %collective-permute-start.10) | collective-permute-done | bytes 40992 | tf_op jit(solution)/shard_map/ppermute | solution.py:355
  48.1 0.1 collective-permute-start.12
  48.2 1.3 %collective-permute-done.12.other_ref = f32[160,128]{1,0:T(8,128)S(1)} collective-permute-done((f32[160,128]{1,0:T(8,128)S(1)}, f32[160,128]{1,0:T(8,128)S(1)}, u32[]{:S(2)}, u32[]{:S(2)}) %collective-permute-start.12) | collective-permute-done | bytes 81952 | tf_op jit(solution)/shard_map/ppermute | solution.py:355
  49.4 0.7 %shard_map.112 = (f32[128,128]{1,0:T(8,128)}, f32[128,128]{1,0:T(8,128)}, f32[64,128]{1,0:T(8,128)}) custom-call(f32[160,128]{1,0:T(8,128)S(1)} %convert_add_fusion.mine_ref, f32[160,128]{1,0:T(8,128)S(1)} %collective-permute-done.12.other_ref, f32[8,128]{1,0:T(8,128)S(1)} %shard_map.109.mark_ref), custom_call_target="tpu_custom_call" | custom-call | flops 1 | bytes 1 | tf_op jit(solution)/shard_map/pallas_call | solution.py:32
  (11 shorter events, 0.1 us)
Async XLA Ops:
  0.6 7.4 %collective-permute-start.3 = (bf16[128,16,128]{2,1,0:T(8,128)(2,1)}, bf16[128,16,128]{2,1,0:T(8,128)(2,1)S(1)}, u32[]{:S(2)}, u32[]{:S(2)}) collective-permute-start(bf16[128,16,128]{2,1,0:T(8,128)(2,1)} %cot_src.1), channel_id=1, source_target_pairs={{0,1},{1,0},{2,3},{3,2},{4,5},{5,4},{6,7},{7,6},{8,9},{9,8},{10,11... | collective-permute-start | bytes 1572872 | tf_op jit(solution)/shard_map/ppermute | solution.py:355
  1.1 15.3 %collective-permute-start.2 = (bf16[128,16,128]{2,1,0:T(8,128)(2,1)}, bf16[128,16,128]{2,1,0:T(8,128)(2,1)S(1)}, u32[]{:S(2)}, u32[]{:S(2)}) collective-permute-start(bf16[128,16,128]{2,1,0:T(8,128)(2,1)} %cot_src.1), channel_id=1, source_target_pairs={{0,2},{1,3},{2,0},{3,1},{4,6},{5,7},{6,4},{7,5},{8,10},{9,11},{10,... | collective-permute-start | bytes 1572872 | tf_op jit(solution)/shard_map/ppermute | solution.py:355
  4.7 13.5 %collective-permute-start = (bf16[16,64,128]{2,1,0:T(8,128)(2,1)S(1)}, bf16[16,64,128]{2,1,0:T(8,128)(2,1)S(1)}, u32[]{:S(2)}, u32[]{:S(2)}) collective-permute-start(bf16[16,64,128]{2,1,0:T(8,128)(2,1)S(1)} %shard_map.102.even_own), channel_id=1, source_target_pairs={{0,4},{4,0},{8,12},{12,8},{16,20},{20,16},{24,28},{28,24},{1,5},{5... | collective-permute-start | bytes 786440 | tf_op jit(solution)/shard_map/ppermute | solution.py:388
  7.3 11.0 %collective-permute-start.1 = (bf16[16,64,128]{2,1,0:T(8,128)(2,1)S(1)}, bf16[16,64,128]{2,1,0:T(8,128)(2,1)S(1)}, u32[]{:S(2)}, u32[]{:S(2)}) collective-permute-start(bf16[16,64,128]{2,1,0:T(8,128)(2,1)S(1)} %shard_map.103.odd_own), channel_id=1, source_target_pairs={{4,8},{12,16},{20,24},{8,4},{16,12},{24,20},{0,0},{28,28},{5,9},{1... | collective-permute-start | bytes 786440 | tf_op jit(solution)/shard_map/ppermute | solution.py:387
  16.4 1.9 %collective-permute-start.4 = (bf16[128,16,128]{2,1,0:T(8,128)(2,1)S(1)}, bf16[128,16,128]{2,1,0:T(8,128)(2,1)S(1)}, u32[]{:S(2)}, u32[]{:S(2)}) collective-permute-start(bf16[128,16,128]{2,1,0:T(8,128)(2,1)S(1)} %collective-permute-done.2.block_ref), channel_id=1, source_target_pairs={{0,1},{1,0},{2,3},{3,2},{4,5},{5,4},{6,7},{7,6},{8,9},{9,8},{10,11... | collective-permute-start | bytes 1572872 | tf_op jit(solution)/shard_map/ppermute | solution.py:355
  26.0 1.5 %collective-permute-start.5 = (f32[160,128]{1,0:T(8,128)S(1)}, f32[160,128]{1,0:T(8,128)S(1)}, u32[]{:S(2)}, u32[]{:S(2)}) collective-permute-start(f32[160,128]{1,0:T(8,128)S(1)} %get-tuple-element.58), channel_id=1, source_target_pairs={{0,1},{1,0},{2,3},{3,2},{4,5},{5,4},{6,7},{7,6},{8,9},{9,8},{10,11... | collective-permute-start | bytes 245768 | tf_op jit(solution)/shard_map/ppermute | solution.py:355
  26.6 15.1 %collective-permute-start.9 = (bf16[16,64,128]{2,1,0:T(8,128)(2,1)S(1)}, bf16[16,64,128]{2,1,0:T(8,128)(2,1)S(1)}, u32[]{:S(2)}, u32[]{:S(2)}) collective-permute-start(bf16[16,64,128]{2,1,0:T(8,128)(2,1)S(1)} %get-tuple-element.65), channel_id=1, source_target_pairs={{4,8},{12,16},{20,24},{8,4},{16,12},{24,20},{0,0},{28,28},{5,9},{1... | collective-permute-start | bytes 786440 | tf_op jit(solution)/shard_map/ppermute | solution.py:444
  27.5 4.1 %collective-permute-start.6 = (bf16[160,128]{1,0:T(8,128)(2,1)S(1)}, bf16[160,128]{1,0:T(8,128)(2,1)S(1)}, u32[]{:S(2)}, u32[]{:S(2)}) collective-permute-start(bf16[160,128]{1,0:T(8,128)(2,1)S(1)} %get-tuple-element.76), channel_id=1, source_target_pairs={{0,2},{1,3},{2,0},{3,1},{4,6},{5,7},{6,4},{7,5},{8,10},{9,11},{10,... | collective-permute-start | bytes 122888 | tf_op jit(solution)/shard_map/ppermute | solution.py:355
  31.6 7.4 %collective-permute-start.7 = (bf16[160,128]{1,0:T(8,128)(2,1)S(1)}, bf16[160,128]{1,0:T(8,128)(2,1)S(1)}, u32[]{:S(2)}, u32[]{:S(2)}) collective-permute-start(bf16[160,128]{1,0:T(8,128)(2,1)S(1)} %get-tuple-element.79), channel_id=1, source_target_pairs={{0,8},{4,12},{8,0},{12,4},{16,24},{20,28},{24,16},{28,20},{1,9},{5... | collective-permute-start | bytes 122888 | tf_op jit(solution)/shard_map/ppermute | solution.py:355
  35.9 9.1 %collective-permute-start.11 = (bf16[16,64,128]{2,1,0:T(8,128)(2,1)S(1)}, bf16[16,64,128]{2,1,0:T(8,128)(2,1)S(1)}, u32[]{:S(2)}, u32[]{:S(2)}) collective-permute-start(bf16[16,64,128]{2,1,0:T(8,128)(2,1)S(1)} %get-tuple-element.69), channel_id=1, source_target_pairs={{0,4},{4,0},{8,12},{12,8},{16,20},{20,16},{24,28},{28,24},{1,5},{5... | collective-permute-start | bytes 786440 | tf_op jit(solution)/shard_map/ppermute | solution.py:452
  39.0 5.0 %collective-permute-start.8 = (bf16[160,128]{1,0:T(8,128)(2,1)S(1)}, bf16[160,128]{1,0:T(8,128)(2,1)S(1)}, u32[]{:S(2)}, u32[]{:S(2)}) collective-permute-start(bf16[160,128]{1,0:T(8,128)(2,1)S(1)} %add_convert_fusion.1), channel_id=1, source_target_pairs={{0,16},{4,20},{8,24},{12,28},{16,0},{20,4},{24,8},{28,12},{1,17},{... | collective-permute-start | bytes 122888 | tf_op jit(solution)/shard_map/ppermute | solution.py:355
  44.0 4.1 %collective-permute-start.10 = (bf16[160,128]{1,0:T(8,128)(2,1)S(1)}, bf16[160,128]{1,0:T(8,128)(2,1)S(1)}, u32[]{:S(2)}, u32[]{:S(2)}) collective-permute-start(bf16[160,128]{1,0:T(8,128)(2,1)S(1)} %add_convert_fusion), channel_id=1, source_target_pairs={{0,4},{4,0},{8,12},{12,8},{16,20},{20,16},{24,28},{28,24},{1,5},{5... | collective-permute-start | bytes 122888 | tf_op jit(solution)/shard_map/ppermute | solution.py:355
  48.1 1.3 %collective-permute-start.12 = (f32[160,128]{1,0:T(8,128)S(1)}, f32[160,128]{1,0:T(8,128)S(1)}, u32[]{:S(2)}, u32[]{:S(2)}) collective-permute-start(f32[160,128]{1,0:T(8,128)S(1)} %convert_add_fusion.mine_ref), channel_id=1, source_target_pairs={{0,1},{1,0},{2,3},{3,2},{4,5},{5,4},{6,7},{7,6},{8,9},{9,8},{10,11... | collective-permute-start | bytes 245768 | tf_op jit(solution)/shard_map/ppermute | solution.py:355

commit v5 on v4

--- a/solution.py
+++ b/solution.py
@@ -1,4 +1,5 @@
 import functools
+import itertools
 import math
 
 import jax
@@ -73,19 +74,27 @@
         ).astype(BF)
 
 
-def take_block(block_ref, wout, steady, part, conv, valid=None):
+def block_steps(block_ref, wout, steady, part, conv, valid=None):
     steps, rows, chans = steady.shape
     for start in range(0, rows, 16):
         block = block_ref[start : start + 16].astype(F32)
         if valid is not None:
             block = jnp.where(valid, block, 0.0)
         steady[:, start : start + 16] = jnp.swapaxes(block, 0, 1).astype(BF)
+        yield
     for s in range(0, steps, 4):
         block = steady[s : s + 4].reshape(4 * rows, chans)
         conv[s : s + 4] = dot(block, wout, ((1,), (1,))).astype(BF).reshape(4, rows, chans)
+        yield
     for s in range(0, steps, 2):
         part[s // 2, :, 0:rows] = steady[s].T
         part[s // 2, :, rows : 2 * rows] = steady[s + 1].T
+        yield
+
+
+def take_block(*args):
+    for _ in block_steps(*args):
+        pass
 
 
 def place_part(part, cross_ref, slot, sem):
@@ -166,19 +175,30 @@
 
 def far_body(sum_ref, crossed_ref, block_ref, lags_ref, wout_ref, out_ref, cross_ref, steady, part, conv, sems):
     steps, rows, chans = conv.shape
-    take_block(block_ref, wout_ref[...], steady, part, conv, lax.axis_index("tm") < 2)
-    sent = place_part(part, cross_ref, 2, sems.at[0])
-
-    def tile(index, carry):
-        where = pl.ds(pl.multiple_of(index * 16, 16), 16)
-        sums = [[sum_ref[s, where, :][:8], sum_ref[s, where, :][8:]] for s in range(steps)]
-        add_lags(sums, conv, lags_ref, 2 * steps, where, False)
-        for s in range(steps):
-            out_ref[s, where, :] = jnp.concatenate(sums[s], axis=0)
-        return carry
-
-    lax.fori_loop(0, rows // 16, tile, 0)
-    sent.wait()
+    valid = lax.axis_index("tm") < 2
+
+    @pl.when(valid)
+    def _():
+        take_block(block_ref, wout_ref[...], steady, part, conv)
+        sent = place_part(part, cross_ref, 2, sems.at[0])
+
+        def tile(index, carry):
+            where = pl.ds(pl.multiple_of(index * 16, 16), 16)
+            sums = [[sum_ref[s, where, :][:8], sum_ref[s, where, :][8:]] for s in range(steps)]
+            add_lags(sums, conv, lags_ref, 2 * steps, where, False)
+            for s in range(steps):
+                out_ref[s, where, :] = jnp.concatenate(sums[s], axis=0)
+            return carry
+
+        lax.fori_loop(0, rows // 16, tile, 0)
+        sent.wait()
+
+    @pl.when(jnp.logical_not(valid))
+    def _():
+        part[...] = jnp.zeros_like(part)
+        sent = place_part(part, cross_ref, 2, sems.at[0])
+        out_ref[...] = sum_ref[...]
+        sent.wait()
 
 
 def lag_steps(sum_ref, conv, lags, base, grad_ref, start):
@@ -222,6 +242,9 @@
     group = 4
     mix, wg = mix_ref[...], wg_ref[...]
     zero = jnp.zeros((rows, chans), BF)
+    other = block_steps(
+        swapped_ref, wout_ref[...], steady, cross.at[pl.ds(slot * block, block)], conv, tm < 2
+    )
     stack[0, 0:rows, chans : 2 * chans] = zero
     stack[block, 0:rows, 0:chans] = zero
     for s in range(0, steps, group):
@@ -237,8 +260,10 @@
             [mixed[:, t * chans : (t + 1) * chans] for t in range(group)], axis=0
         )
         mixed_ref[s : s + group] = mixed.reshape(group, rows, chans)
+        for _ in range(2):
+            next(other, None)
         pre = dot(mixed, wg)
-        gate = 1.0 / (1.0 + jnp.exp(-pre))
+        gate = 0.5 + 0.5 * jnp.tanh(0.5 * pre)
         act = (pre * gate).astype(BF).reshape(group, rows, chans)
         slope = gate * (1.0 + pre * (1.0 - gate))
         slope_ref[s : s + group] = slope.reshape(group, rows, chans)
@@ -247,18 +272,23 @@
             stack[t // 2, low : low + rows, 0:chans] = act[t - s]
             low = ((t + 1) % 2) * rows
             stack[(t + 1) // 2, low : low + rows, chans : 2 * chans] = act[t - s]
-
-    take_block(swapped_ref, wout_ref[...], steady, cross.at[pl.ds(slot * block, block)], conv, tm < 2)
+        for _ in range(3):
+            next(other, None)
+
+    for _ in other:
+        pass
     window[0:31] = lags_ref[pl.ds(slot * steps - 15, 31)]
     for copy in copies:
         copy.wait()
 
     weight = wout_ref[...].astype(F32).T
     taps = taps_ref[...].astype(F32)
-    out = jnp.zeros((chans, chans), F32)
-    found = []
-    for at in range(0, pairs, group):
-        work = lag_steps(sum_ref, conv, window, 15, grad_ref, at * 4)
+    out_at, lag_at = chans, 2 * chans
+
+    def lag_group(at, tiles):
+        work = itertools.chain.from_iterable(
+            [lag_steps(sum_ref, conv, window, 15, grad_ref, tile) for tile in tiles]
+        )
         total = [None] * group
         for i in range(block + 1):
             count = min(group, pairs - at - i)
@@ -269,16 +299,36 @@
                 for g in range(count):
                     piece = part[g * rows : (g + 1) * rows]
                     total[g] = piece if total[g] is None else total[g] + piece
-            for _ in range(2):
+            for _ in range(4):
                 next(work, None)
         for _ in work:
             pass
+        out, found = jnp.zeros((chans, chans), F32), []
         for g in range(group):
             for side in range(2):
                 lag = 2 * (at + g) + side
                 part = total[g][:, side * chans : (side + 1) * chans]
                 out += part * taps[lag : lag + 1]
                 found.append(jnp.sum(part * weight, axis=0, keepdims=True))
+        pack[lag_at + 2 * at : lag_at + 2 * (at + group)] = jnp.concatenate(found, axis=0)
+        return out
+
+    middle = pairs // 2
+    out = jnp.zeros((chans, chans), F32)
+    for at in range(0, middle, group):
+        out += lag_group(at, range(at * 8, at * 8 + 32, 16))
+    pack[out_at:lag_at] = out
+
+    @pl.when(tm < 2)
+    def _():
+        out = pack[out_at:lag_at]
+        for at in range(middle, pairs, group):
+            out += lag_group(at, ())
+        pack[out_at:lag_at] = out
+
+    @pl.when(tm >= 2)
+    def _():
+        pack[lag_at + 2 * middle :] = jnp.zeros((2 * (pairs - middle), chans), F32)
 
     mixt = mixt_ref[...]
     graph = jnp.zeros((chans, chans), F32)
@@ -299,8 +349,7 @@
             odd_out[s + t] = part[half + rows :].astype(BF)
 
     pack[0:chans] = graph
-    pack[chans : 2 * chans] = out.T
-    pack[2 * chans :] = jnp.concatenate(found, axis=0)
+    pack[out_at:lag_at] = pack[out_at:lag_at].T
     size = keep_ref.shape[0]
     keep_ref[...] = pack[pl.ds(pl.multiple_of(odd * size, size), size)]
     send_ref[...] = pack[pl.ds(pl.multiple_of((1 - odd) * size, size), size)]
@@ -310,27 +359,31 @@
     mark_ref[...] = first_ref[0, 0:8].astype(F32) + second_ref[0, 0:8].astype(F32)
 
 
-def fold_body(spread_ref, odd_edge_ref, cot_ref, out_ref):
-    half = odd_edge_ref.shape[1]
+def fold_body(spread_ref, cot_ref, out_ref):
+    half = spread_ref.shape[1] // 2
     odd = lax.axis_index("bus") & 1
     low, high = pl.multiple_of(odd * half, half), pl.multiple_of((1 - odd) * half, half)
     for s in range(spread_ref.shape[0]):
         out_ref[s, :half] = spread_ref[s, :half] + cot_ref[s, pl.ds(high, half)].astype(F32)
-        out_ref[s, half:] = (
-            spread_ref[s, half:]
-            + cot_ref[s, pl.ds(low, half)].astype(F32)
-            + odd_edge_ref[s].astype(F32)
-        )
-
-
-def final_body(spread_ref, even_ref, out_ref):
+        out_ref[s, half:] = spread_ref[s, half:] + cot_ref[s, pl.ds(low, half)].astype(F32)
+
+
+def edge_add_body(spread_ref, even_ref, out_ref):
     half = even_ref.shape[1]
+    for s in range(spread_ref.shape[0]):
+        out_ref[s, :half] = spread_ref[s, :half] + even_ref[s].astype(F32)
+        out_ref[s, half:] = spread_ref[s, half:]
+
+
+def final_body(spread_ref, odd_ref, out_ref):
+    half = odd_ref.shape[1]
     odd = lax.axis_index("bus") & 1
     for start in range(0, half, 16):
-        part = spread_ref[:, start : start + 16] + even_ref[:, start : start + 16].astype(F32)
+        part = spread_ref[:, start : start + 16]
         where = pl.ds((1 - odd) * half + start, 16)
         out_ref[where] = jnp.swapaxes(part, 0, 1).astype(BF)
         part = spread_ref[:, half + start : half + start + 16]
+        part = part + odd_ref[:, start : start + 16].astype(F32)
         where = pl.ds(odd * half + start, 16)
         out_ref[where] = jnp.swapaxes(part, 0, 1).astype(BF)
 
@@ -438,30 +491,33 @@
         anywhere=[12],
     )
     mark = send[0:8]
+    odd_grad = lax.ppermute(odd_grad, "bus", evens)
     keep = keep + swap(send, "tm", 1)
-    hops = [("tm", 1 << bit) for bit in range(1, tm.bit_length() - 1)]
-    hops += [("bus", 1 << bit) for bit in range(1, bus.bit_length() - 1)] + [("bus", 1)]
-    odd_grad = lax.ppermute(odd_grad, "bus", odds)
+    keep, even_grad = lax.optimization_barrier((keep, even_grad))
+    even_grad = lax.ppermute(even_grad, "bus", evens)
+    hops = [("bus", 1 << bit) for bit in range(1, bus.bit_length() - 1)]
+    hops += [("tm", 1 << bit) for bit in range(1, tm.bit_length() - 1)] + [("bus", 1)]
+    onward = [(i, i + 2) for i in range(0, bus - 2, 2)] + [(i, i - 2) for i in range(3, bus, 2)]
     for place, (axis, distance) in enumerate(hops):
         sent = keep.astype(BF)
         received = swap(sent, axis, distance)
         if place < len(hops) - 2:
             received, mark = pause(keep, received, mark)
             if place == 0:
-                even_grad, mark = lax.optimization_barrier((even_grad, mark))
-                even_grad = lax.ppermute(even_grad, "bus", evens)
+                odd_grad, mark = lax.optimization_barrier((odd_grad, mark))
+                odd_grad = lax.ppermute(odd_grad, "bus", onward)
         elif place == len(hops) - 2:
-            (spread,) = call(
-                fold_body, [(wide, F32)], spread, odd_grad, steady, cost=1 << 36
-            )
+            (spread,) = call(fold_body, [(wide, F32)], spread, steady, cost=1 << 36)
             received, spread = lax.optimization_barrier((received, spread))
         else:
-            (grad_features,) = call(
-                final_body, [(features.shape, BF)], spread, even_grad, cost=1 << 36
-            )
-            received, grad_features = lax.optimization_barrier((received, grad_features))
+            (spread,) = call(edge_add_body, [(wide, F32)], spread, even_grad, cost=1 << 36)
+            received, spread = lax.optimization_barrier((received, spread))
         keep = sent.astype(F32) + received.astype(F32)
     other = swap(keep, "tm", 1)
+    (grad_features,) = call(
+        final_body, [(features.shape, BF)], spread, odd_grad, cost=1 << 36
+    )
+    other, grad_features = lax.optimization_barrier((other, grad_features))
     scale = 1.0 / math.sqrt(bus * rows * steps * tm)
     grad_graph, grad_out, grad_taps = call(
         functools.partial(finish_body, scale),

time: 50.4 us -> 47.6 us (0.944)
  waiting for transfers between devices: 13.3 us -> 11.2 us
    ppermute x1 -> x2, starting transfers between devices: 0.67 us -> 5.31 us  [the longest x1 3.5 us: shards(): odd_grad = lax.ppermute(odd_grad, 'bus', onward)]
    ppermute x9, starting transfers between devices: 13.5 us -> 9.08 us  [swap(): return lax.ppermute(value, axis, [(i, i ^ distance) for i in range(size)])]
    ppermute x9, waiting for transfers between devices: 13.3 us -> 10.6 us  [swap(): return lax.ppermute(value, axis, [(i, i ^ distance) for i in range(size)])]
    ppermute x1, starting transfers between devices: 1.64 us -> 1.03 us  [shards(): even_grad = lax.ppermute(even_grad, 'bus', evens)]
    ppermute x1 -> x2, waiting for transfers between devices: 0.01 us -> 0.55 us  [the longest x1 0.55 us: shards(): odd_grad = lax.ppermute(odd_grad, 'bus', evens)]
    pallas_call x11 -> x12, Pallas kernels: 17.9 us -> 17.6 us  [call(): pl.pallas_call(body, out_shape=[jax.ShapeDtypeStruct(shape, dtype) for sh...]
  transfers between devices with their start and end apart: 13 -> 14, of which waited for: 8 -> 8; matrix products, arithmetic and copies ran while one was open for 0% -> 0% of each run, Pallas kernels for 19% -> 20%
where the time goes in v5:
time: 47.6 us; the launch traced here: 47.3 us
  starting transfers between devices  17.7 us (37%)
  Pallas kernels  17.6 us (37%)
  waiting for transfers between devices  11.2 us (24%)
  between operations  0.79 us (2%)
    pallas_call x12, Pallas kernels, call(): pl.pallas_call(body, out_shape=[jax.ShapeDtypeStruct(shape, dtype) for sh...  17.6 us
    ppermute x9, waiting for transfers between devices, swap(): return lax.ppermute(value, axis, [(i, i ^ distance) for i in range(size)])  10.6 us
    ppermute x9, starting transfers between devices, swap(): return lax.ppermute(value, axis, [(i, i ^ distance) for i in range(size)])  9.08 us
    ppermute x1, starting transfers between devices, shards(): odd_grad = lax.ppermute(odd_grad, 'bus', onward)  3.5 us
    ppermute x1, starting transfers between devices, shards(): odd_grad = lax.ppermute(odd_grad, 'bus', evens)  1.81 us
    ppermute x1, starting transfers between devices, shards(): even_edge = lax.ppermute(even_own, 'bus', evens)  1.58 us
    ppermute x1, starting transfers between devices, shards(): even_grad = lax.ppermute(even_grad, 'bus', evens)  1.03 us
  transfers between devices with their start and end apart: 14, of which 8 were waited for; matrix products, arithmetic and copies ran while one was open for 0% of the time, Pallas kernels for 20%

profile of v5, /device:TPU:0, one launch (start us, length us, event | category | flops | bytes accessed | tf_op | source)
XLA Modules:
  0.0 47.3 jit_solution(14309388290085579136)
XLA Ops:
  0.6 0.5 %collective-permute-start.3 = (bf16[128,16,128]{2,1,0:T(8,128)(2,1)}, bf16[128,16,128]{2,1,0:T(8,128)(2,1)S(1)}, u32[]{:S(2)}, u32[]{:S(2)}) collective-permute-start(bf16[128,16,128]{2,1,0:T(8,128)(2,1)} %cot_src.1), channel_id=1, source_target_pairs={{0,1},{1,0},{2,3},{3,2},{4,5},{5,4},{6,7},{7,6},{8,9},{9,8},{10,11... | collective-permute-start | bytes 1572872 | tf_op jit(solution)/shard_map/ppermute | solution.py:408
  1.1 2.6 %collective-permute-start.2 = (bf16[128,16,128]{2,1,0:T(8,128)(2,1)}, bf16[128,16,128]{2,1,0:T(8,128)(2,1)S(1)}, u32[]{:S(2)}, u32[]{:S(2)}) collective-permute-start(bf16[128,16,128]{2,1,0:T(8,128)(2,1)} %cot_src.1), channel_id=1, source_target_pairs={{0,2},{1,3},{2,0},{3,1},{4,6},{5,7},{6,4},{7,5},{8,10},{9,11},{10,... | collective-permute-start | bytes 1572872 | tf_op jit(solution)/shard_map/ppermute | solution.py:408
  3.7 1.0 %shard_map.102.even_own = bf16[16,64,128]{2,1,0:T(8,128)(2,1)S(1)} custom-call(bf16[128,16,128]{2,1,0:T(8,128)(2,1)} %source_ref.3), custom_call_target="tpu_custom_call" | custom-call | flops 1 | bytes 1 | tf_op jit(solution)/shard_map/pallas_call | solution.py:33
  4.7 1.6 %collective-permute-start = (bf16[16,64,128]{2,1,0:T(8,128)(2,1)S(1)}, bf16[16,64,128]{2,1,0:T(8,128)(2,1)S(1)}, u32[]{:S(2)}, u32[]{:S(2)}) collective-permute-start(bf16[16,64,128]{2,1,0:T(8,128)(2,1)S(1)} %shard_map.102.even_own), channel_id=1, source_target_pairs={{0,4},{4,0},{8,12},{12,8},{16,20},{20,16},{24,28},{28,24},{1,5},{5... | collective-permute-start | bytes 786440 | tf_op jit(solution)/shard_map/ppermute | solution.py:441
  6.3 1.0 %shard_map.103.odd_own = bf16[16,64,128]{2,1,0:T(8,128)(2,1)S(1)} custom-call(bf16[128,16,128]{2,1,0:T(8,128)(2,1)} %source_ref.3), custom_call_target="tpu_custom_call" | custom-call | flops 1 | bytes 1 | tf_op jit(solution)/shard_map/pallas_call | solution.py:33
  7.3 0.7 %collective-permute-start.1 = (bf16[16,64,128]{2,1,0:T(8,128)(2,1)S(1)}, bf16[16,64,128]{2,1,0:T(8,128)(2,1)S(1)}, u32[]{:S(2)}, u32[]{:S(2)}) collective-permute-start(bf16[16,64,128]{2,1,0:T(8,128)(2,1)S(1)} %shard_map.103.odd_own), channel_id=1, source_target_pairs={{4,8},{12,16},{20,24},{8,4},{16,12},{24,20},{0,0},{28,28},{5,9},{1... | collective-permute-start | bytes 786440 | tf_op jit(solution)/shard_map/ppermute | solution.py:440
  8.0 0.0 collective-permute-done.3.near_ref
  8.0 4.5 %shard_map.104 = (f32[16,128,128]{2,1,0:T(8,128)S(1)}, bf16[32,128,256]{2,1,0:T(8,128)(2,1)S(1)}, bf16[128,256]{1,0:T(8,128)(2,1)S(1)}, bf16[256,128]{1,0:T(8,12...) custom-call(s32[2,8]{1,0:T(2,128)} %ids_src.1, ...), custom_call_target="tpu_custom_call" | custom-call | flops 1 | bytes 1 | tf_op jit(solution)/shard_map/pallas_call | solution.py:33
  12.6 3.9 %collective-permute-done.2.block_ref = bf16[128,16,128]{2,1,0:T(8,128)(2,1)S(1)} collective-permute-done((bf16[128,16,128]{2,1,0:T(8,128)(2,1)}, bf16[128,16,128]{2,1,0:T(8,128)(2,1)S(1)}, u32[]{:S(2)}, u32[]{:S(2)}) %collective-permute-start.2) | collective-permute-done | bytes 524320 | tf_op jit(solution)/shard_map/ppermute | solution.py:408
  16.4 1.8 %shard_map.105 = (f32[16,128,128]{2,1,0:T(8,128)S(1)}, bf16[32,128,256]{2,1,0:T(8,128)(2,1)S(1)}) custom-call(f32[16,128,128]{2,1,0:T(8,128)S(1)} %get-tuple-element.45.sum_ref, bf16[32,128,256]{2,1,0:T(8,128)(2,1)S(1)} %get-tuple-element.46.crossed_ref, bf16[128,16,128]{2,1,0:T(8,128)(2,1)S(1)} %collective-permute-done.2.block_ref, ...), custom_call_target="tpu_custom_call", output_to_operand_aliasing={{1}: (1, {})} | custom-call | flops 1 | bytes 1 | tf_op jit(solution)/shard_map/pallas_call | solution.py:33
  18.2 0.0 collective-permute-done.first_ref.even_ref
  18.3 0.1 collective-permute-done.4.swapped_ref
  18.4 7.4 %shard_map.107 = (f32[160,128]{1,0:T(8,128)S(1)}, f32[160,128]{1,0:T(8,128)S(1)}, f32[16,128,128]{2,1,0:T(8,128)S(1)}, bf16[16,64,128]{2,1,0:T(8,128)(2,1)S(1)}, bf16[16,64,128]{2,1,0:T(8,128)(2,1)S(1)}) custom-call(bf16[16,64,128]{2,1,0:T(8,128)(2,1)S(1)} %shard_map.102.even_own, bf16[16,64,128]{2,1,0:T(8,128)(2,1)S(1)} %shard_map.103.odd_own, ...), custom_call_target="tpu_custom_call" | custom-call | flops 1 | bytes 1 | tf_op jit(solution)/shard_map/pallas_call | solution.py:33
  25.7 0.5 collective-permute-start.5
  26.2 1.8 %collective-permute-start.8 = (bf16[16,64,128]{2,1,0:T(8,128)(2,1)S(1)}, bf16[16,64,128]{2,1,0:T(8,128)(2,1)S(1)}, u32[]{:S(2)}, u32[]{:S(2)}) collective-permute-start(bf16[16,64,128]{2,1,0:T(8,128)(2,1)S(1)} %get-tuple-element.66), channel_id=1, source_target_pairs={{0,4},{4,0},{8,12},{12,8},{16,20},{20,16},{24,28},{28,24},{1,5},{5... | collective-permute-start | bytes 786440 | tf_op jit(solution)/shard_map/ppermute | solution.py:494
  28.1 1.6 %collective-permute-start.6 = (bf16[160,128]{1,0:T(8,128)(2,1)S(1)}, bf16[160,128]{1,0:T(8,128)(2,1)S(1)}, u32[]{:S(2)}, u32[]{:S(2)}) collective-permute-start(bf16[160,128]{1,0:T(8,128)(2,1)S(1)} %convert_element_type.36), channel_id=1, source_target_pairs={{0,8},{4,12},{8,0},{12,4},{16,24},{20,28},{24,16},{28,20},{1,9},{5... | collective-permute-start | bytes 122888 | tf_op jit(solution)/shard_map/ppermute | solution.py:408
  29.7 1.0 %collective-permute-start.11 = (bf16[16,64,128]{2,1,0:T(8,128)(2,1)S(1)}, bf16[16,64,128]{2,1,0:T(8,128)(2,1)S(1)}, u32[]{:S(2)}, u32[]{:S(2)}) collective-permute-start(bf16[16,64,128]{2,1,0:T(8,128)(2,1)S(1)} %get-tuple-element.74), channel_id=1, source_target_pairs={{0,4},{4,0},{8,12},{12,8},{16,20},{20,16},{24,28},{28,24},{1,5},{5... | collective-permute-start | bytes 786440 | tf_op jit(solution)/shard_map/ppermute | solution.py:497
  30.7 1.4 %collective-permute-done.6 = bf16[160,128]{1,0:T(8,128)(2,1)S(1)} collective-permute-done((bf16[160,128]{1,0:T(8,128)(2,1)S(1)}, bf16[160,128]{1,0:T(8,128)(2,1)S(1)}, u32[]{:S(2)}, u32[]{:S(2)}) %collective-permute-start.6) | collective-permute-done | bytes 40992 | tf_op jit(solution)/shard_map/ppermute | solution.py:408
  32.1 2.6 %collective-permute-start.7 = (bf16[160,128]{1,0:T(8,128)(2,1)S(1)}, bf16[160,128]{1,0:T(8,128)(2,1)S(1)}, u32[]{:S(2)}, u32[]{:S(2)}) collective-permute-start(bf16[160,128]{1,0:T(8,128)(2,1)S(1)} %get-tuple-element.85), channel_id=1, source_target_pairs={{0,16},{4,20},{8,24},{12,28},{16,0},{20,4},{24,8},{28,12},{1,17},{... | collective-permute-start | bytes 122888 | tf_op jit(solution)/shard_map/ppermute | solution.py:408
  34.8 0.5 %collective-permute-done.8 = bf16[16,64,128]{2,1,0:T(8,128)(2,1)S(1)} collective-permute-done((bf16[16,64,128]{2,1,0:T(8,128)(2,1)S(1)}, bf16[16,64,128]{2,1,0:T(8,128)(2,1)S(1)}, u32[]{:S(2)}, u32[]{:S(2)}) %collective-permute-start.8) | collective-permute-done | bytes 262176 | tf_op jit(solution)/shard_map/ppermute | solution.py:494
  35.3 1.8 %collective-permute-done.7 = bf16[160,128]{1,0:T(8,128)(2,1)S(1)} collective-permute-done((bf16[160,128]{1,0:T(8,128)(2,1)S(1)}, bf16[160,128]{1,0:T(8,128)(2,1)S(1)}, u32[]{:S(2)}, u32[]{:S(2)}) %collective-permute-start.7) | collective-permute-done | bytes 40992 | tf_op jit(solution)/shard_map/ppermute | solution.py:408
  37.1 0.1 collective-permute-start.9
  37.2 0.1 shard_map.110.spread_ref
  37.3 3.5 %collective-permute-start.13 = (bf16[16,64,128]{2,1,0:T(8,128)(2,1)S(1)}, bf16[16,64,128]{2,1,0:T(8,128)(2,1)S(1)}, u32[]{:S(2)}, u32[]{:S(2)}) collective-permute-start(bf16[16,64,128]{2,1,0:T(8,128)(2,1)S(1)} %collective-permute-done.8), channel_id=1, source_target_pairs={{0,8},{8,16},{16,24},{12,4},{20,12},{28,20},{1,9},{9,17},{17,25},{... | collective-permute-start | bytes 786440 | tf_op jit(solution)/shard_map/ppermute | solution.py:508
  40.8 0.4 collective-permute-done.9
  41.2 1.1 %collective-permute-start.10 = (bf16[160,128]{1,0:T(8,128)(2,1)S(1)}, bf16[160,128]{1,0:T(8,128)(2,1)S(1)}, u32[]{:S(2)}, u32[]{:S(2)}) collective-permute-start(bf16[160,128]{1,0:T(8,128)(2,1)S(1)} %add_convert_fusion), channel_id=1, source_target_pairs={{0,4},{4,0},{8,12},{12,8},{16,20},{20,16},{24,28},{28,24},{1,5},{5... | collective-permute-start | bytes 122888 | tf_op jit(solution)/shard_map/ppermute | solution.py:408
  42.3 0.1 shard_map.111.spread_ref
  42.4 2.9 %collective-permute-done.10 = bf16[160,128]{1,0:T(8,128)(2,1)S(1)} collective-permute-done((bf16[160,128]{1,0:T(8,128)(2,1)S(1)}, bf16[160,128]{1,0:T(8,128)(2,1)S(1)}, u32[]{:S(2)}, u32[]{:S(2)}) %collective-permute-start.10) | collective-permute-done | bytes 40992 | tf_op jit(solution)/shard_map/ppermute | solution.py:408
  45.3 0.1 collective-permute-start.12
  45.4 1.0 %shard_map.112 = bf16[128,16,128]{2,1,0:T(8,128)(2,1)} custom-call(f32[16,128,128]{2,1,0:T(8,128)S(1)} %shard_map.111.spread_ref, bf16[16,64,128]{2,1,0:T(8,128)(2,1)S(1)} %collective-permute-done.13.odd_ref), custom_call_target="tpu_custom_call" | custom-call | flops 68719476736 | bytes 1 | tf_op jit(solution)/shard_map/pallas_call | solution.py:33
  46.4 0.2 collective-permute-done.12.other_ref
  46.6 0.7 %shard_map.113 = (f32[128,128]{1,0:T(8,128)}, f32[128,128]{1,0:T(8,128)}, f32[64,128]{1,0:T(8,128)}) custom-call(f32[160,128]{1,0:T(8,128)S(1)} %convert_add_fusion.mine_ref, f32[160,128]{1,0:T(8,128)S(1)} %collective-permute-done.12.other_ref, f32[8,128]{1,0:T(8,128)S(1)} %shard_map.109.mark_ref), custom_call_target="tpu_custom_call" | custom-call | flops 1 | bytes 1 | tf_op jit(solution)/shard_map/pallas_call | solution.py:33
  (15 shorter events, 0.1 us)
Async XLA Ops:
  0.6 7.4 %collective-permute-start.3 = (bf16[128,16,128]{2,1,0:T(8,128)(2,1)}, bf16[128,16,128]{2,1,0:T(8,128)(2,1)S(1)}, u32[]{:S(2)}, u32[]{:S(2)}) collective-permute-start(bf16[128,16,128]{2,1,0:T(8,128)(2,1)} %cot_src.1), channel_id=1, source_target_pairs={{0,1},{1,0},{2,3},{3,2},{4,5},{5,4},{6,7},{7,6},{8,9},{9,8},{10,11... | collective-permute-start | bytes 1572872 | tf_op jit(solution)/shard_map/ppermute | solution.py:408
  1.1 15.3 %collective-permute-start.2 = (bf16[128,16,128]{2,1,0:T(8,128)(2,1)}, bf16[128,16,128]{2,1,0:T(8,128)(2,1)S(1)}, u32[]{:S(2)}, u32[]{:S(2)}) collective-permute-start(bf16[128,16,128]{2,1,0:T(8,128)(2,1)} %cot_src.1), channel_id=1, source_target_pairs={{0,2},{1,3},{2,0},{3,1},{4,6},{5,7},{6,4},{7,5},{8,10},{9,11},{10,... | collective-permute-start | bytes 1572872 | tf_op jit(solution)/shard_map/ppermute | solution.py:408
  4.7 13.5 %collective-permute-start = (bf16[16,64,128]{2,1,0:T(8,128)(2,1)S(1)}, bf16[16,64,128]{2,1,0:T(8,128)(2,1)S(1)}, u32[]{:S(2)}, u32[]{:S(2)}) collective-permute-start(bf16[16,64,128]{2,1,0:T(8,128)(2,1)S(1)} %shard_map.102.even_own), channel_id=1, source_target_pairs={{0,4},{4,0},{8,12},{12,8},{16,20},{20,16},{24,28},{28,24},{1,5},{5... | collective-permute-start | bytes 786440 | tf_op jit(solution)/shard_map/ppermute | solution.py:441
  7.3 10.9 %collective-permute-start.1 = (bf16[16,64,128]{2,1,0:T(8,128)(2,1)S(1)}, bf16[16,64,128]{2,1,0:T(8,128)(2,1)S(1)}, u32[]{:S(2)}, u32[]{:S(2)}) collective-permute-start(bf16[16,64,128]{2,1,0:T(8,128)(2,1)S(1)} %shard_map.103.odd_own), channel_id=1, source_target_pairs={{4,8},{12,16},{20,24},{8,4},{16,12},{24,20},{0,0},{28,28},{5,9},{1... | collective-permute-start | bytes 786440 | tf_op jit(solution)/shard_map/ppermute | solution.py:440
  16.4 1.9 %collective-permute-start.4 = (bf16[128,16,128]{2,1,0:T(8,128)(2,1)S(1)}, bf16[128,16,128]{2,1,0:T(8,128)(2,1)S(1)}, u32[]{:S(2)}, u32[]{:S(2)}) collective-permute-start(bf16[128,16,128]{2,1,0:T(8,128)(2,1)S(1)} %collective-permute-done.2.block_ref), channel_id=1, source_target_pairs={{0,1},{1,0},{2,3},{3,2},{4,5},{5,4},{6,7},{7,6},{8,9},{9,8},{10,11... | collective-permute-start | bytes 1572872 | tf_op jit(solution)/shard_map/ppermute | solution.py:408
  25.7 2.3 %collective-permute-start.5 = (f32[160,128]{1,0:T(8,128)S(1)}, f32[160,128]{1,0:T(8,128)S(1)}, u32[]{:S(2)}, u32[]{:S(2)}) collective-permute-start(f32[160,128]{1,0:T(8,128)S(1)} %get-tuple-element.62), channel_id=1, source_target_pairs={{0,1},{1,0},{2,3},{3,2},{4,5},{5,4},{6,7},{7,6},{8,9},{9,8},{10,11... | collective-permute-start | bytes 245768 | tf_op jit(solution)/shard_map/ppermute | solution.py:408
  26.2 9.1 %collective-permute-start.8 = (bf16[16,64,128]{2,1,0:T(8,128)(2,1)S(1)}, bf16[16,64,128]{2,1,0:T(8,128)(2,1)S(1)}, u32[]{:S(2)}, u32[]{:S(2)}) collective-permute-start(bf16[16,64,128]{2,1,0:T(8,128)(2,1)S(1)} %get-tuple-element.66), channel_id=1, source_target_pairs={{0,4},{4,0},{8,12},{12,8},{16,20},{20,16},{24,28},{28,24},{1,5},{5... | collective-permute-start | bytes 786440 | tf_op jit(solution)/shard_map/ppermute | solution.py:494
  28.1 4.1 %collective-permute-start.6 = (bf16[160,128]{1,0:T(8,128)(2,1)S(1)}, bf16[160,128]{1,0:T(8,128)(2,1)S(1)}, u32[]{:S(2)}, u32[]{:S(2)}) collective-permute-start(bf16[160,128]{1,0:T(8,128)(2,1)S(1)} %convert_element_type.36), channel_id=1, source_target_pairs={{0,8},{4,12},{8,0},{12,4},{16,24},{20,28},{24,16},{28,20},{1,9},{5... | collective-permute-start | bytes 122888 | tf_op jit(solution)/shard_map/ppermute | solution.py:408
  29.7 12.6 %collective-permute-start.11 = (bf16[16,64,128]{2,1,0:T(8,128)(2,1)S(1)}, bf16[16,64,128]{2,1,0:T(8,128)(2,1)S(1)}, u32[]{:S(2)}, u32[]{:S(2)}) collective-permute-start(bf16[16,64,128]{2,1,0:T(8,128)(2,1)S(1)} %get-tuple-element.74), channel_id=1, source_target_pairs={{0,4},{4,0},{8,12},{12,8},{16,20},{20,16},{24,28},{28,24},{1,5},{5... | collective-permute-start | bytes 786440 | tf_op jit(solution)/shard_map/ppermute | solution.py:497
  32.1 5.0 %collective-permute-start.7 = (bf16[160,128]{1,0:T(8,128)(2,1)S(1)}, bf16[160,128]{1,0:T(8,128)(2,1)S(1)}, u32[]{:S(2)}, u32[]{:S(2)}) collective-permute-start(bf16[160,128]{1,0:T(8,128)(2,1)S(1)} %get-tuple-element.85), channel_id=1, source_target_pairs={{0,16},{4,20},{8,24},{12,28},{16,0},{20,4},{24,8},{28,12},{1,17},{... | collective-permute-start | bytes 122888 | tf_op jit(solution)/shard_map/ppermute | solution.py:408
  37.1 4.1 %collective-permute-start.9 = (bf16[160,128]{1,0:T(8,128)(2,1)S(1)}, bf16[160,128]{1,0:T(8,128)(2,1)S(1)}, u32[]{:S(2)}, u32[]{:S(2)}) collective-permute-start(bf16[160,128]{1,0:T(8,128)(2,1)S(1)} %add_convert_fusion.1), channel_id=1, source_target_pairs={{0,2},{1,3},{2,0},{3,1},{4,6},{5,7},{6,4},{7,5},{8,10},{9,11},{10,... | collective-permute-start | bytes 122888 | tf_op jit(solution)/shard_map/ppermute | solution.py:408
  37.3 8.1 %collective-permute-start.13 = (bf16[16,64,128]{2,1,0:T(8,128)(2,1)S(1)}, bf16[16,64,128]{2,1,0:T(8,128)(2,1)S(1)}, u32[]{:S(2)}, u32[]{:S(2)}) collective-permute-start(bf16[16,64,128]{2,1,0:T(8,128)(2,1)S(1)} %collective-permute-done.8), channel_id=1, source_target_pairs={{0,8},{8,16},{16,24},{12,4},{20,12},{28,20},{1,9},{9,17},{17,25},{... | collective-permute-start | bytes 786440 | tf_op jit(solution)/shard_map/ppermute | solution.py:508
  41.2 4.1 %collective-permute-start.10 = (bf16[160,128]{1,0:T(8,128)(2,1)S(1)}, bf16[160,128]{1,0:T(8,128)(2,1)S(1)}, u32[]{:S(2)}, u32[]{:S(2)}) collective-permute-start(bf16[160,128]{1,0:T(8,128)(2,1)S(1)} %add_convert_fusion), channel_id=1, source_target_pairs={{0,4},{4,0},{8,12},{12,8},{16,20},{20,16},{24,28},{28,24},{1,5},{5... | collective-permute-start | bytes 122888 | tf_op jit(solution)/shard_map/ppermute | solution.py:408
  45.3 1.3 %collective-permute-start.12 = (f32[160,128]{1,0:T(8,128)S(1)}, f32[160,128]{1,0:T(8,128)S(1)}, u32[]{:S(2)}, u32[]{:S(2)}) collective-permute-start(f32[160,128]{1,0:T(8,128)S(1)} %convert_add_fusion.mine_ref), channel_id=1, source_target_pairs={{0,1},{1,0},{2,3},{3,2},{4,5},{5,4},{6,7},{7,6},{8,9},{9,8},{10,11... | collective-permute-start | bytes 245768 | tf_op jit(solution)/shard_map/ppermute | solution.py:408

commit v6 on v5

--- a/solution.py
+++ b/solution.py
@@ -46,6 +46,24 @@
     return lax.dot_general(left, right, (dims, ((), ())), preferred_element_type=F32)
 
 
+def doubled(weight):
+    zero = jnp.zeros_like(weight)
+    top = jnp.concatenate([weight, zero], axis=1)
+    return jnp.concatenate([top, jnp.concatenate([zero, weight], axis=1)], axis=0)
+
+
+def two_halves(values, weight, dims=((1,), (0,))):
+    count, rows, chans = values.shape
+    flat = values.reshape(count * rows, chans)
+    middle = count * rows // 2
+    both = dot(jnp.concatenate([flat[:middle], flat[middle:]], axis=1), weight, dims)
+    return [
+        both[t * rows : (t + 1) * rows, h * chans : (h + 1) * chans]
+        for h in range(2)
+        for t in range(count // 2)
+    ]
+
+
 def load_all(sems, pairs):
     copies = [
         pltpu.make_async_copy(source, target, sems.at[i])
@@ -82,9 +100,10 @@
             block = jnp.where(valid, block, 0.0)
         steady[:, start : start + 16] = jnp.swapaxes(block, 0, 1).astype(BF)
         yield
-    for s in range(0, steps, 4):
-        block = steady[s : s + 4].reshape(4 * rows, chans)
-        conv[s : s + 4] = dot(block, wout, ((1,), (1,))).astype(BF).reshape(4, rows, chans)
+    wout = doubled(wout)
+    for s in range(0, steps, 8):
+        for t, piece in enumerate(two_halves(steady[s : s + 8], wout, ((1,), (1,)))):
+            conv[s + t] = piece.astype(BF)
         yield
     for s in range(0, steps, 2):
         part[s // 2, :, 0:rows] = steady[s].T
@@ -240,41 +259,41 @@
         copies[-1].start()
 
     group = 4
-    mix, wg = mix_ref[...], wg_ref[...]
+    mix, wg = mix_ref[...], doubled(wg_ref[...])
     zero = jnp.zeros((rows, chans), BF)
     other = block_steps(
         swapped_ref, wout_ref[...], steady, cross.at[pl.ds(slot * block, block)], conv, tm < 2
     )
     stack[0, 0:rows, chans : 2 * chans] = zero
-    stack[block, 0:rows, 0:chans] = zero
-    for s in range(0, steps, group):
-        ext = jnp.concatenate(
-            [
-                jnp.concatenate([even_ref[t], even_own[t], odd_own[t], odd_ref[t]], axis=0)
-                for t in range(s, s + group)
-            ],
-            axis=1,
-        )
-        mixed = dot(mix, ext).astype(BF)
-        mixed = jnp.concatenate(
-            [mixed[:, t * chans : (t + 1) * chans] for t in range(group)], axis=0
-        )
-        mixed_ref[s : s + group] = mixed.reshape(group, rows, chans)
-        for _ in range(2):
+    stack[block, 0:rows, chans : 2 * chans] = zero
+    stack[block, rows : 2 * rows, 0:chans] = zero
+    wide_group = 2 * group
+    for s in range(0, steps, wide_group):
+        mixed = []
+        for start in range(s, s + wide_group, group):
+            ext = jnp.concatenate(
+                [
+                    jnp.concatenate([even_ref[t], even_own[t], odd_own[t], odd_ref[t]], axis=0)
+                    for t in range(start, start + group)
+                ],
+                axis=1,
+            )
+            found = dot(mix, ext).astype(BF)
+            mixed += [found[:, t * chans : (t + 1) * chans] for t in range(group)]
             next(other, None)
-        pre = dot(mixed, wg)
-        gate = 0.5 + 0.5 * jnp.tanh(0.5 * pre)
-        act = (pre * gate).astype(BF).reshape(group, rows, chans)
-        slope = gate * (1.0 + pre * (1.0 - gate))
-        slope_ref[s : s + group] = slope.reshape(group, rows, chans)
-        for t in range(s, s + group):
+        mixed = jnp.stack(mixed)
+        mixed_ref[s : s + wide_group] = mixed
+        for t, pre in enumerate(two_halves(mixed, wg), s):
+            gate = 0.5 + 0.5 * jnp.tanh(0.5 * pre)
+            act = (pre * gate).astype(BF)
+            slope_ref[t] = gate * (1.0 + pre * (1.0 - gate))
             low = (t % 2) * rows
-            stack[t // 2, low : low + rows, 0:chans] = act[t - s]
-            low = ((t + 1) % 2) * rows
-            stack[(t + 1) // 2, low : low + rows, chans : 2 * chans] = act[t - s]
-        for _ in range(3):
+            stack[t // 2, low : low + rows, 0:chans] = act
+            low = ((t + 1) % 2) * rows if t < steps - 1 else rows
+            stack[(t + 1) // 2, low : low + rows, chans : 2 * chans] = act
+            if t == steps - 1:
+                stack[block, 0:rows, 0:chans] = act
             next(other, None)
-
     for _ in other:
         pass
     window[0:31] = lags_ref[pl.ds(slot * steps - 15, 31)]
@@ -289,40 +308,58 @@
         work = itertools.chain.from_iterable(
             [lag_steps(sum_ref, conv, window, 15, grad_ref, tile) for tile in tiles]
         )
-        total = [None] * group
-        for i in range(block + 1):
-            count = min(group, pairs - at - i)
-            if count > 0:
-                depth = 2 * rows if i < block else rows
-                left = cross[at + i : at + i + count, :, 0:depth].reshape(count * rows, depth)
-                part = dot(left, stack[i, 0:depth])
-                for g in range(count):
-                    piece = part[g * rows : (g + 1) * rows]
-                    total[g] = piece if total[g] is None else total[g] + piece
-            for _ in range(4):
-                next(work, None)
+        totals = []
+        for first in (at, at + group):
+            total = [None] * group
+            for i in range(block):
+                count = min(group, pairs - first - i)
+                if count > 0:
+                    left = cross[first + i : first + i + count].reshape(count * rows, 2 * rows)
+                    part = dot(left, stack[i])
+                    for g in range(count):
+                        piece = part[g * rows : (g + 1) * rows]
+                        total[g] = piece if total[g] is None else total[g] + piece
+                for _ in range(5):
+                    next(work, None)
+            totals.append(total)
         for _ in work:
             pass
+        last = None
+        if at + 2 * group + block <= pairs:
+            left = jnp.concatenate(
+                [
+                    cross[first + block : first + block + group, :, 0:rows].reshape(
+                        group * rows, rows
+                    )
+                    for first in (at, at + group)
+                ],
+                axis=1,
+            )
+            last = dot(left, stack[block])
         out, found = jnp.zeros((chans, chans), F32), []
-        for g in range(group):
-            for side in range(2):
-                lag = 2 * (at + g) + side
-                part = total[g][:, side * chans : (side + 1) * chans]
-                out += part * taps[lag : lag + 1]
-                found.append(jnp.sum(part * weight, axis=0, keepdims=True))
-        pack[lag_at + 2 * at : lag_at + 2 * (at + group)] = jnp.concatenate(found, axis=0)
+        for half_at, total in enumerate(totals):
+            for g in range(group):
+                for side in range(2):
+                    lag = 2 * (at + half_at * group + g) + side
+                    part = total[g][:, side * chans : (side + 1) * chans]
+                    if side == 1 and last is not None:
+                        lanes = slice(half_at * chans, (half_at + 1) * chans)
+                        part = part + last[g * rows : (g + 1) * rows, lanes]
+                    out += part * taps[lag : lag + 1]
+                    found.append(jnp.sum(part * weight, axis=0, keepdims=True))
+        pack[lag_at + 2 * at : lag_at + 2 * (at + 2 * group)] = jnp.concatenate(found, axis=0)
         return out
 
     middle = pairs // 2
     out = jnp.zeros((chans, chans), F32)
-    for at in range(0, middle, group):
-        out += lag_group(at, range(at * 8, at * 8 + 32, 16))
+    for at in range(0, middle, 2 * group):
+        out += lag_group(at, range(at * 8, at * 8 + 64, 16))
     pack[out_at:lag_at] = out
 
     @pl.when(tm < 2)
     def _():
         out = pack[out_at:lag_at]
-        for at in range(middle, pairs, group):
+        for at in range(middle, pairs, 2 * group):
             out += lag_group(at, ())
         pack[out_at:lag_at] = out
 
@@ -332,21 +369,20 @@
 
     mixt = mixt_ref[...]
     graph = jnp.zeros((chans, chans), F32)
-    for s in range(0, steps, group):
-        grad = grad_ref[s : s + group].astype(F32) * slope_ref[s : s + group]
-        grad_pre = grad.astype(BF).reshape(group * rows, chans)
-        mixed = mixed_ref[s : s + group].reshape(group * rows, chans)
-        graph += dot(mixed, grad_pre, ((0,), (0,)))
-        grad_mixed = dot(grad_pre, wg, ((1,), (1,))).astype(BF)
-        grad_mixed = jnp.concatenate(
-            [grad_mixed[t * rows : (t + 1) * rows] for t in range(group)], axis=1
-        )
-        spread = dot(mixt, grad_mixed)
-        for t in range(group):
-            part = spread[:, t * chans : (t + 1) * chans]
-            even_out[s + t] = part[:half].astype(BF)
-            spread_ref[s + t] = part[half : half + rows]
-            odd_out[s + t] = part[half + rows :].astype(BF)
+    for s in range(0, steps, wide_group):
+        grad = grad_ref[s : s + wide_group].astype(F32) * slope_ref[s : s + wide_group]
+        grad_pre = grad.astype(BF)
+        flat = (wide_group * rows, chans)
+        mixed = mixed_ref[s : s + wide_group].reshape(flat)
+        graph += dot(mixed, grad_pre.reshape(flat), ((0,), (0,)))
+        grad_mixed = [piece.astype(BF) for piece in two_halves(grad_pre, wg, ((1,), (1,)))]
+        for start in range(0, wide_group, group):
+            spread = dot(mixt, jnp.concatenate(grad_mixed[start : start + group], axis=1))
+            for t in range(group):
+                part = spread[:, t * chans : (t + 1) * chans]
+                even_out[s + start + t] = part[:half].astype(BF)
+                spread_ref[s + start + t] = part[half : half + rows]
+                odd_out[s + start + t] = part[half + rows :].astype(BF)
 
     pack[0:chans] = graph
     pack[out_at:lag_at] = pack[out_at:lag_at].T

time: 47.6 us -> 47.2 us (level)
  no operation moved by 1% of the time
where the time goes in v6:
time: 47.2 us; the launch traced here: 46.9 us
  starting transfers between devices  17.7 us (38%)
  Pallas kernels  17.2 us (36%)
  waiting for transfers between devices  11.2 us (24%)
  between operations  0.79 us (2%)
    pallas_call x12, Pallas kernels, call(): pl.pallas_call(body, out_shape=[jax.ShapeDtypeStruct(shape, dtype) for sh...  17.2 us
    ppermute x9, waiting for transfers between devices, swap(): return lax.ppermute(value, axis, [(i, i ^ distance) for i in range(size)])  10.6 us
    ppermute x9, starting transfers between devices, swap(): return lax.ppermute(value, axis, [(i, i ^ distance) for i in range(size)])  9.12 us
    ppermute x1, starting transfers between devices, shards(): odd_grad = lax.ppermute(odd_grad, 'bus', onward)  3.5 us
    ppermute x1, starting transfers between devices, shards(): odd_grad = lax.ppermute(odd_grad, 'bus', evens)  1.79 us
    ppermute x1, starting transfers between devices, shards(): even_edge = lax.ppermute(even_own, 'bus', evens)  1.58 us
    ppermute x1, starting transfers between devices, shards(): even_grad = lax.ppermute(even_grad, 'bus', evens)  1.01 us
  transfers between devices with their start and end apart: 14, of which 8 were waited for; matrix products, arithmetic and copies ran while one was open for 0% of the time, Pallas kernels for 20%

profile of v6, /device:TPU:0, one launch (start us, length us, event | category | flops | bytes accessed | tf_op | source)
XLA Modules:
  0.0 46.9 jit_solution(12492845762802465321)
XLA Ops:
  0.6 0.5 %collective-permute-start.3 = (bf16[128,16,128]{2,1,0:T(8,128)(2,1)}, bf16[128,16,128]{2,1,0:T(8,128)(2,1)S(1)}, u32[]{:S(2)}, u32[]{:S(2)}) collective-permute-start(bf16[128,16,128]{2,1,0:T(8,128)(2,1)} %cot_src.1), channel_id=1, source_target_pairs={{0,1},{1,0},{2,3},{3,2},{4,5},{5,4},{6,7},{7,6},{8,9},{9,8},{10,11... | collective-permute-start | bytes 1572872 | tf_op jit(solution)/shard_map/ppermute | solution.py:444
  1.1 2.6 %collective-permute-start.2 = (bf16[128,16,128]{2,1,0:T(8,128)(2,1)}, bf16[128,16,128]{2,1,0:T(8,128)(2,1)S(1)}, u32[]{:S(2)}, u32[]{:S(2)}) collective-permute-start(bf16[128,16,128]{2,1,0:T(8,128)(2,1)} %cot_src.1), channel_id=1, source_target_pairs={{0,2},{1,3},{2,0},{3,1},{4,6},{5,7},{6,4},{7,5},{8,10},{9,11},{10,... | collective-permute-start | bytes 1572872 | tf_op jit(solution)/shard_map/ppermute | solution.py:444
  3.7 1.0 %shard_map.102.even_own = bf16[16,64,128]{2,1,0:T(8,128)(2,1)S(1)} custom-call(bf16[128,16,128]{2,1,0:T(8,128)(2,1)} %source_ref.3), custom_call_target="tpu_custom_call" | custom-call | flops 1 | bytes 1 | tf_op jit(solution)/shard_map/pallas_call | solution.py:33
  4.7 1.6 %collective-permute-start = (bf16[16,64,128]{2,1,0:T(8,128)(2,1)S(1)}, bf16[16,64,128]{2,1,0:T(8,128)(2,1)S(1)}, u32[]{:S(2)}, u32[]{:S(2)}) collective-permute-start(bf16[16,64,128]{2,1,0:T(8,128)(2,1)S(1)} %shard_map.102.even_own), channel_id=1, source_target_pairs={{0,4},{4,0},{8,12},{12,8},{16,20},{20,16},{24,28},{28,24},{1,5},{5... | collective-permute-start | bytes 786440 | tf_op jit(solution)/shard_map/ppermute | solution.py:477
  6.3 1.0 %shard_map.103.odd_own = bf16[16,64,128]{2,1,0:T(8,128)(2,1)S(1)} custom-call(bf16[128,16,128]{2,1,0:T(8,128)(2,1)} %source_ref.3), custom_call_target="tpu_custom_call" | custom-call | flops 1 | bytes 1 | tf_op jit(solution)/shard_map/pallas_call | solution.py:33
  7.3 0.7 %collective-permute-start.1 = (bf16[16,64,128]{2,1,0:T(8,128)(2,1)S(1)}, bf16[16,64,128]{2,1,0:T(8,128)(2,1)S(1)}, u32[]{:S(2)}, u32[]{:S(2)}) collective-permute-start(bf16[16,64,128]{2,1,0:T(8,128)(2,1)S(1)} %shard_map.103.odd_own), channel_id=1, source_target_pairs={{4,8},{12,16},{20,24},{8,4},{16,12},{24,20},{0,0},{28,28},{5,9},{1... | collective-permute-start | bytes 786440 | tf_op jit(solution)/shard_map/ppermute | solution.py:476
  8.0 4.6 %shard_map.104 = (f32[16,128,128]{2,1,0:T(8,128)S(1)}, bf16[32,128,256]{2,1,0:T(8,128)(2,1)S(1)}, bf16[128,256]{1,0:T(8,128)(2,1)S(1)}, bf16[256,128]{1,0:T(8,12...) custom-call(s32[2,8]{1,0:T(2,128)} %ids_src.1, ...), custom_call_target="tpu_custom_call" | custom-call | flops 1 | bytes 1 | tf_op jit(solution)/shard_map/pallas_call | solution.py:33
  12.6 3.8 %collective-permute-done.2.block_ref = bf16[128,16,128]{2,1,0:T(8,128)(2,1)S(1)} collective-permute-done((bf16[128,16,128]{2,1,0:T(8,128)(2,1)}, bf16[128,16,128]{2,1,0:T(8,128)(2,1)S(1)}, u32[]{:S(2)}, u32[]{:S(2)}) %collective-permute-start.2) | collective-permute-done | bytes 524320 | tf_op jit(solution)/shard_map/ppermute | solution.py:444
  16.4 0.0 collective-permute-start.4
  16.4 1.8 %shard_map.105 = (f32[16,128,128]{2,1,0:T(8,128)S(1)}, bf16[32,128,256]{2,1,0:T(8,128)(2,1)S(1)}) custom-call(f32[16,128,128]{2,1,0:T(8,128)S(1)} %get-tuple-element.45.sum_ref, bf16[32,128,256]{2,1,0:T(8,128)(2,1)S(1)} %get-tuple-element.46.crossed_ref, bf16[128,16,128]{2,1,0:T(8,128)(2,1)S(1)} %collective-permute-done.2.block_ref, ...), custom_call_target="tpu_custom_call", output_to_operand_aliasing={{1}: (1, {})} | custom-call | flops 1 | bytes 1 | tf_op jit(solution)/shard_map/pallas_call | solution.py:33
  18.2 0.0 collective-permute-done.first_ref.even_ref
  18.3 0.1 collective-permute-done.4.swapped_ref
  18.4 7.0 %shard_map.107 = (f32[160,128]{1,0:T(8,128)S(1)}, f32[160,128]{1,0:T(8,128)S(1)}, f32[16,128,128]{2,1,0:T(8,128)S(1)}, bf16[16,64,128]{2,1,0:T(8,128)(2,1)S(1)}, bf16[16,64,128]{2,1,0:T(8,128)(2,1)S(1)}) custom-call(bf16[16,64,128]{2,1,0:T(8,128)(2,1)S(1)} %shard_map.102.even_own, bf16[16,64,128]{2,1,0:T(8,128)(2,1)S(1)} %shard_map.103.odd_own, ...), custom_call_target="tpu_custom_call" | custom-call | flops 1 | bytes 1 | tf_op jit(solution)/shard_map/pallas_call | solution.py:33
  25.3 0.5 %collective-permute-start.5 = (f32[160,128]{1,0:T(8,128)S(1)}, f32[160,128]{1,0:T(8,128)S(1)}, u32[]{:S(2)}, u32[]{:S(2)}) collective-permute-start(f32[160,128]{1,0:T(8,128)S(1)} %get-tuple-element.62), channel_id=1, source_target_pairs={{0,1},{1,0},{2,3},{3,2},{4,5},{5,4},{6,7},{7,6},{8,9},{9,8},{10,11... | collective-permute-start | bytes 245768 | tf_op jit(solution)/shard_map/ppermute | solution.py:444
  25.8 1.8 %collective-permute-start.8 = (bf16[16,64,128]{2,1,0:T(8,128)(2,1)S(1)}, bf16[16,64,128]{2,1,0:T(8,128)(2,1)S(1)}, u32[]{:S(2)}, u32[]{:S(2)}) collective-permute-start(bf16[16,64,128]{2,1,0:T(8,128)(2,1)S(1)} %get-tuple-element.66), channel_id=1, source_target_pairs={{0,4},{4,0},{8,12},{12,8},{16,20},{20,16},{24,28},{28,24},{1,5},{5... | collective-permute-start | bytes 786440 | tf_op jit(solution)/shard_map/ppermute | solution.py:530
  27.7 1.6 %collective-permute-start.6 = (bf16[160,128]{1,0:T(8,128)(2,1)S(1)}, bf16[160,128]{1,0:T(8,128)(2,1)S(1)}, u32[]{:S(2)}, u32[]{:S(2)}) collective-permute-start(bf16[160,128]{1,0:T(8,128)(2,1)S(1)} %convert_element_type.36), channel_id=1, source_target_pairs={{0,8},{4,12},{8,0},{12,4},{16,24},{20,28},{24,16},{28,20},{1,9},{5... | collective-permute-start | bytes 122888 | tf_op jit(solution)/shard_map/ppermute | solution.py:444
  29.3 1.0 %collective-permute-start.11 = (bf16[16,64,128]{2,1,0:T(8,128)(2,1)S(1)}, bf16[16,64,128]{2,1,0:T(8,128)(2,1)S(1)}, u32[]{:S(2)}, u32[]{:S(2)}) collective-permute-start(bf16[16,64,128]{2,1,0:T(8,128)(2,1)S(1)} %get-tuple-element.74), channel_id=1, source_target_pairs={{0,4},{4,0},{8,12},{12,8},{16,20},{20,16},{24,28},{28,24},{1,5},{5... | collective-permute-start | bytes 786440 | tf_op jit(solution)/shard_map/ppermute | solution.py:533
  30.3 1.4 %collective-permute-done.6 = bf16[160,128]{1,0:T(8,128)(2,1)S(1)} collective-permute-done((bf16[160,128]{1,0:T(8,128)(2,1)S(1)}, bf16[160,128]{1,0:T(8,128)(2,1)S(1)}, u32[]{:S(2)}, u32[]{:S(2)}) %collective-permute-start.6) | collective-permute-done | bytes 40992 | tf_op jit(solution)/shard_map/ppermute | solution.py:444
  31.7 2.7 %collective-permute-start.7 = (bf16[160,128]{1,0:T(8,128)(2,1)S(1)}, bf16[160,128]{1,0:T(8,128)(2,1)S(1)}, u32[]{:S(2)}, u32[]{:S(2)}) collective-permute-start(bf16[160,128]{1,0:T(8,128)(2,1)S(1)} %get-tuple-element.85), channel_id=1, source_target_pairs={{0,16},{4,20},{8,24},{12,28},{16,0},{20,4},{24,8},{28,12},{1,17},{... | collective-permute-start | bytes 122888 | tf_op jit(solution)/shard_map/ppermute | solution.py:444
  34.4 0.6 %collective-permute-done.8 = bf16[16,64,128]{2,1,0:T(8,128)(2,1)S(1)} collective-permute-done((bf16[16,64,128]{2,1,0:T(8,128)(2,1)S(1)}, bf16[16,64,128]{2,1,0:T(8,128)(2,1)S(1)}, u32[]{:S(2)}, u32[]{:S(2)}) %collective-permute-start.8) | collective-permute-done | bytes 262176 | tf_op jit(solution)/shard_map/ppermute | solution.py:530
  35.0 1.7 %collective-permute-done.7 = bf16[160,128]{1,0:T(8,128)(2,1)S(1)} collective-permute-done((bf16[160,128]{1,0:T(8,128)(2,1)S(1)}, bf16[160,128]{1,0:T(8,128)(2,1)S(1)}, u32[]{:S(2)}, u32[]{:S(2)}) %collective-permute-start.7) | collective-permute-done | bytes 40992 | tf_op jit(solution)/shard_map/ppermute | solution.py:444
  36.7 0.1 collective-permute-start.9
  36.8 0.1 shard_map.110.spread_ref
  36.9 3.5 %collective-permute-start.13 = (bf16[16,64,128]{2,1,0:T(8,128)(2,1)S(1)}, bf16[16,64,128]{2,1,0:T(8,128)(2,1)S(1)}, u32[]{:S(2)}, u32[]{:S(2)}) collective-permute-start(bf16[16,64,128]{2,1,0:T(8,128)(2,1)S(1)} %collective-permute-done.8), channel_id=1, source_target_pairs={{0,8},{8,16},{16,24},{12,4},{20,12},{28,20},{1,9},{9,17},{17,25},{... | collective-permute-start | bytes 786440 | tf_op jit(solution)/shard_map/ppermute | solution.py:544
  40.4 0.4 collective-permute-done.9
  40.8 1.1 %collective-permute-start.10 = (bf16[160,128]{1,0:T(8,128)(2,1)S(1)}, bf16[160,128]{1,0:T(8,128)(2,1)S(1)}, u32[]{:S(2)}, u32[]{:S(2)}) collective-permute-start(bf16[160,128]{1,0:T(8,128)(2,1)S(1)} %add_convert_fusion), channel_id=1, source_target_pairs={{0,4},{4,0},{8,12},{12,8},{16,20},{20,16},{24,28},{28,24},{1,5},{5... | collective-permute-start | bytes 122888 | tf_op jit(solution)/shard_map/ppermute | solution.py:444
  41.9 0.1 shard_map.111.spread_ref
  42.0 2.9 %collective-permute-done.10 = bf16[160,128]{1,0:T(8,128)(2,1)S(1)} collective-permute-done((bf16[160,128]{1,0:T(8,128)(2,1)S(1)}, bf16[160,128]{1,0:T(8,128)(2,1)S(1)}, u32[]{:S(2)}, u32[]{:S(2)}) %collective-permute-start.10) | collective-permute-done | bytes 40992 | tf_op jit(solution)/shard_map/ppermute | solution.py:444
  44.9 0.1 collective-permute-start.12
  45.0 1.0 %shard_map.112 = bf16[128,16,128]{2,1,0:T(8,128)(2,1)} custom-call(f32[16,128,128]{2,1,0:T(8,128)S(1)} %shard_map.111.spread_ref, bf16[16,64,128]{2,1,0:T(8,128)(2,1)S(1)} %collective-permute-done.13.odd_ref), custom_call_target="tpu_custom_call" | custom-call | flops 68719476736 | bytes 1 | tf_op jit(solution)/shard_map/pallas_call | solution.py:33
  46.0 0.2 collective-permute-done.12.other_ref
  46.2 0.7 %shard_map.113 = (f32[128,128]{1,0:T(8,128)}, f32[128,128]{1,0:T(8,128)}, f32[64,128]{1,0:T(8,128)}) custom-call(f32[160,128]{1,0:T(8,128)S(1)} %convert_add_fusion.mine_ref, f32[160,128]{1,0:T(8,128)S(1)} %collective-permute-done.12.other_ref, f32[8,128]{1,0:T(8,128)S(1)} %shard_map.109.mark_ref), custom_call_target="tpu_custom_call" | custom-call | flops 1 | bytes 1 | tf_op jit(solution)/shard_map/pallas_call | solution.py:33
  (15 shorter events, 0.1 us)
Async XLA Ops:
  0.6 7.4 %collective-permute-start.3 = (bf16[128,16,128]{2,1,0:T(8,128)(2,1)}, bf16[128,16,128]{2,1,0:T(8,128)(2,1)S(1)}, u32[]{:S(2)}, u32[]{:S(2)}) collective-permute-start(bf16[128,16,128]{2,1,0:T(8,128)(2,1)} %cot_src.1), channel_id=1, source_target_pairs={{0,1},{1,0},{2,3},{3,2},{4,5},{5,4},{6,7},{7,6},{8,9},{9,8},{10,11... | collective-permute-start | bytes 1572872 | tf_op jit(solution)/shard_map/ppermute | solution.py:444
  1.1 15.3 %collective-permute-start.2 = (bf16[128,16,128]{2,1,0:T(8,128)(2,1)}, bf16[128,16,128]{2,1,0:T(8,128)(2,1)S(1)}, u32[]{:S(2)}, u32[]{:S(2)}) collective-permute-start(bf16[128,16,128]{2,1,0:T(8,128)(2,1)} %cot_src.1), channel_id=1, source_target_pairs={{0,2},{1,3},{2,0},{3,1},{4,6},{5,7},{6,4},{7,5},{8,10},{9,11},{10,... | collective-permute-start | bytes 1572872 | tf_op jit(solution)/shard_map/ppermute | solution.py:444
  4.7 13.5 %collective-permute-start = (bf16[16,64,128]{2,1,0:T(8,128)(2,1)S(1)}, bf16[16,64,128]{2,1,0:T(8,128)(2,1)S(1)}, u32[]{:S(2)}, u32[]{:S(2)}) collective-permute-start(bf16[16,64,128]{2,1,0:T(8,128)(2,1)S(1)} %shard_map.102.even_own), channel_id=1, source_target_pairs={{0,4},{4,0},{8,12},{12,8},{16,20},{20,16},{24,28},{28,24},{1,5},{5... | collective-permute-start | bytes 786440 | tf_op jit(solution)/shard_map/ppermute | solution.py:477
  7.3 10.9 %collective-permute-start.1 = (bf16[16,64,128]{2,1,0:T(8,128)(2,1)S(1)}, bf16[16,64,128]{2,1,0:T(8,128)(2,1)S(1)}, u32[]{:S(2)}, u32[]{:S(2)}) collective-permute-start(bf16[16,64,128]{2,1,0:T(8,128)(2,1)S(1)} %shard_map.103.odd_own), channel_id=1, source_target_pairs={{4,8},{12,16},{20,24},{8,4},{16,12},{24,20},{0,0},{28,28},{5,9},{1... | collective-permute-start | bytes 786440 | tf_op jit(solution)/shard_map/ppermute | solution.py:476
  16.4 1.9 %collective-permute-start.4 = (bf16[128,16,128]{2,1,0:T(8,128)(2,1)S(1)}, bf16[128,16,128]{2,1,0:T(8,128)(2,1)S(1)}, u32[]{:S(2)}, u32[]{:S(2)}) collective-permute-start(bf16[128,16,128]{2,1,0:T(8,128)(2,1)S(1)} %collective-permute-done.2.block_ref), channel_id=1, source_target_pairs={{0,1},{1,0},{2,3},{3,2},{4,5},{5,4},{6,7},{7,6},{8,9},{9,8},{10,11... | collective-permute-start | bytes 1572872 | tf_op jit(solution)/shard_map/ppermute | solution.py:444
  25.3 2.3 %collective-permute-start.5 = (f32[160,128]{1,0:T(8,128)S(1)}, f32[160,128]{1,0:T(8,128)S(1)}, u32[]{:S(2)}, u32[]{:S(2)}) collective-permute-start(f32[160,128]{1,0:T(8,128)S(1)} %get-tuple-element.62), channel_id=1, source_target_pairs={{0,1},{1,0},{2,3},{3,2},{4,5},{5,4},{6,7},{7,6},{8,9},{9,8},{10,11... | collective-permute-start | bytes 245768 | tf_op jit(solution)/shard_map/ppermute | solution.py:444
  25.8 9.1 %collective-permute-start.8 = (bf16[16,64,128]{2,1,0:T(8,128)(2,1)S(1)}, bf16[16,64,128]{2,1,0:T(8,128)(2,1)S(1)}, u32[]{:S(2)}, u32[]{:S(2)}) collective-permute-start(bf16[16,64,128]{2,1,0:T(8,128)(2,1)S(1)} %get-tuple-element.66), channel_id=1, source_target_pairs={{0,4},{4,0},{8,12},{12,8},{16,20},{20,16},{24,28},{28,24},{1,5},{5... | collective-permute-start | bytes 786440 | tf_op jit(solution)/shard_map/ppermute | solution.py:530
  27.7 4.1 %collective-permute-start.6 = (bf16[160,128]{1,0:T(8,128)(2,1)S(1)}, bf16[160,128]{1,0:T(8,128)(2,1)S(1)}, u32[]{:S(2)}, u32[]{:S(2)}) collective-permute-start(bf16[160,128]{1,0:T(8,128)(2,1)S(1)} %convert_element_type.36), channel_id=1, source_target_pairs={{0,8},{4,12},{8,0},{12,4},{16,24},{20,28},{24,16},{28,20},{1,9},{5... | collective-permute-start | bytes 122888 | tf_op jit(solution)/shard_map/ppermute | solution.py:444
  29.3 12.6 %collective-permute-start.11 = (bf16[16,64,128]{2,1,0:T(8,128)(2,1)S(1)}, bf16[16,64,128]{2,1,0:T(8,128)(2,1)S(1)}, u32[]{:S(2)}, u32[]{:S(2)}) collective-permute-start(bf16[16,64,128]{2,1,0:T(8,128)(2,1)S(1)} %get-tuple-element.74), channel_id=1, source_target_pairs={{0,4},{4,0},{8,12},{12,8},{16,20},{20,16},{24,28},{28,24},{1,5},{5... | collective-permute-start | bytes 786440 | tf_op jit(solution)/shard_map/ppermute | solution.py:533
  31.7 5.0 %collective-permute-start.7 = (bf16[160,128]{1,0:T(8,128)(2,1)S(1)}, bf16[160,128]{1,0:T(8,128)(2,1)S(1)}, u32[]{:S(2)}, u32[]{:S(2)}) collective-permute-start(bf16[160,128]{1,0:T(8,128)(2,1)S(1)} %get-tuple-element.85), channel_id=1, source_target_pairs={{0,16},{4,20},{8,24},{12,28},{16,0},{20,4},{24,8},{28,12},{1,17},{... | collective-permute-start | bytes 122888 | tf_op jit(solution)/shard_map/ppermute | solution.py:444
  36.7 4.1 %collective-permute-start.9 = (bf16[160,128]{1,0:T(8,128)(2,1)S(1)}, bf16[160,128]{1,0:T(8,128)(2,1)S(1)}, u32[]{:S(2)}, u32[]{:S(2)}) collective-permute-start(bf16[160,128]{1,0:T(8,128)(2,1)S(1)} %add_convert_fusion.1), channel_id=1, source_target_pairs={{0,2},{1,3},{2,0},{3,1},{4,6},{5,7},{6,4},{7,5},{8,10},{9,11},{10,... | collective-permute-start | bytes 122888 | tf_op jit(solution)/shard_map/ppermute | solution.py:444
  36.9 8.1 %collective-permute-start.13 = (bf16[16,64,128]{2,1,0:T(8,128)(2,1)S(1)}, bf16[16,64,128]{2,1,0:T(8,128)(2,1)S(1)}, u32[]{:S(2)}, u32[]{:S(2)}) collective-permute-start(bf16[16,64,128]{2,1,0:T(8,128)(2,1)S(1)} %collective-permute-done.8), channel_id=1, source_target_pairs={{0,8},{8,16},{16,24},{12,4},{20,12},{28,20},{1,9},{9,17},{17,25},{... | collective-permute-start | bytes 786440 | tf_op jit(solution)/shard_map/ppermute | solution.py:544
  40.8 4.1 %collective-permute-start.10 = (bf16[160,128]{1,0:T(8,128)(2,1)S(1)}, bf16[160,128]{1,0:T(8,128)(2,1)S(1)}, u32[]{:S(2)}, u32[]{:S(2)}) collective-permute-start(bf16[160,128]{1,0:T(8,128)(2,1)S(1)} %add_convert_fusion), channel_id=1, source_target_pairs={{0,4},{4,0},{8,12},{12,8},{16,20},{20,16},{24,28},{28,24},{1,5},{5... | collective-permute-start | bytes 122888 | tf_op jit(solution)/shard_map/ppermute | solution.py:444
  44.9 1.3 %collective-permute-start.12 = (f32[160,128]{1,0:T(8,128)S(1)}, f32[160,128]{1,0:T(8,128)S(1)}, u32[]{:S(2)}, u32[]{:S(2)}) collective-permute-start(f32[160,128]{1,0:T(8,128)S(1)} %convert_add_fusion.mine_ref), channel_id=1, source_target_pairs={{0,1},{1,0},{2,3},{3,2},{4,5},{5,4},{6,7},{7,6},{8,9},{9,8},{10,11... | collective-permute-start | bytes 245768 | tf_op jit(solution)/shard_map/ppermute | solution.py:444

commit v7 on v6

--- a/solution.py
+++ b/solution.py
@@ -242,7 +242,7 @@
 def tail_body(
     even_own, odd_own, even_ref, odd_ref, mix_ref, mixt_ref, wg_ref, wout_ref, taps_ref, lags_ref,
     sum_ref, swapped_ref, crossed_ref, mark_ref,
-    keep_ref, send_ref, spread_ref, even_out, odd_out,
+    keep_ref, send_ref, mixed_out, even_out, odd_out,
     slope_ref, mixed_ref, stack, steady, conv, cross, window, grad_ref, pack, sems,
 ):
     steps, rows, chans = mixed_ref.shape
@@ -367,7 +367,7 @@
     def _():
         pack[lag_at + 2 * middle :] = jnp.zeros((2 * (pairs - middle), chans), F32)
 
-    mixt = mixt_ref[...]
+    mixt = jnp.concatenate([mixt_ref[:half], mixt_ref[half + rows :]], axis=0)
     graph = jnp.zeros((chans, chans), F32)
     for s in range(0, steps, wide_group):
         grad = grad_ref[s : s + wide_group].astype(F32) * slope_ref[s : s + wide_group]
@@ -381,8 +381,8 @@
             for t in range(group):
                 part = spread[:, t * chans : (t + 1) * chans]
                 even_out[s + start + t] = part[:half].astype(BF)
-                spread_ref[s + start + t] = part[half : half + rows]
-                odd_out[s + start + t] = part[half + rows :].astype(BF)
+                odd_out[s + start + t] = part[half:].astype(BF)
+                mixed_out[s + start + t] = grad_mixed[start + t]
 
     pack[0:chans] = graph
     pack[out_at:lag_at] = pack[out_at:lag_at].T
@@ -395,13 +395,19 @@
     mark_ref[...] = first_ref[0, 0:8].astype(F32) + second_ref[0, 0:8].astype(F32)
 
 
-def fold_body(spread_ref, cot_ref, out_ref):
-    half = spread_ref.shape[1] // 2
+def fold_body(grad_ref, mixt_ref, cot_ref, out_ref):
+    steps, rows, chans = grad_ref.shape
+    half = rows // 2
     odd = lax.axis_index("bus") & 1
     low, high = pl.multiple_of(odd * half, half), pl.multiple_of((1 - odd) * half, half)
-    for s in range(spread_ref.shape[0]):
-        out_ref[s, :half] = spread_ref[s, :half] + cot_ref[s, pl.ds(high, half)].astype(F32)
-        out_ref[s, half:] = spread_ref[s, half:] + cot_ref[s, pl.ds(low, half)].astype(F32)
+    mixt = mixt_ref[half : half + rows]
+    for s in range(0, steps, 4):
+        grads = jnp.concatenate([grad_ref[t] for t in range(s, s + 4)], axis=1)
+        spread = dot(mixt, grads)
+        for t in range(4):
+            part = spread[:, t * chans : (t + 1) * chans]
+            out_ref[s + t, :half] = part[:half] + cot_ref[s + t, pl.ds(high, half)].astype(F32)
+            out_ref[s + t, half:] = part[half:] + cot_ref[s + t, pl.ds(low, half)].astype(F32)
 
 
 def edge_add_body(spread_ref, even_ref, out_ref):
@@ -512,9 +518,9 @@
     (mark,) = call(mark_body, [((8, chans), F32)], even_edge, odd_edge, cost=1 << 36)
     swapped, mark = lax.optimization_barrier((swapped, mark))
     size = (2 * chans + total) // 2
-    keep, send, spread, even_grad, odd_grad = call(
+    keep, send, grad_mixed, even_grad, odd_grad = call(
         tail_body,
-        [((size, chans), F32), ((size, chans), F32), (wide, F32), (edge, BF), (edge, BF)],
+        [((size, chans), F32), ((size, chans), F32), (wide, BF), (edge, BF), (edge, BF)],
         even_own, odd_own, even_edge, odd_edge, mix, mixt, wg, wout, taps, lags,
         sums, swapped, crossed, mark,
         scratch=[
@@ -543,7 +549,9 @@
                 odd_grad, mark = lax.optimization_barrier((odd_grad, mark))
                 odd_grad = lax.ppermute(odd_grad, "bus", onward)
         elif place == len(hops) - 2:
-            (spread,) = call(fold_body, [(wide, F32)], spread, steady, cost=1 << 36)
+            (spread,) = call(
+                fold_body, [(wide, F32)], grad_mixed, mixt, steady, cost=1 << 36
+            )
             received, spread = lax.optimization_barrier((received, spread))
         else:
             (spread,) = call(edge_add_body, [(wide, F32)], spread, even_grad, cost=1 << 36)

time: 47.2 us -> 47 us (level)
  transfers between devices with their start and end apart: 14 -> 14, of which waited for: 8 -> 8; matrix products, arithmetic and copies ran while one was open for 0% -> 0% of each run, Pallas kernels for 20% -> 21%
where the time goes in v7:
time: 47 us; the launch traced here: 46.7 us
  starting transfers between devices  17.7 us (38%)
  Pallas kernels  17.2 us (37%)
  waiting for transfers between devices  11 us (23%)
  between operations  0.79 us (2%)
    pallas_call x12, Pallas kernels, call(): pl.pallas_call(body, out_shape=[jax.ShapeDtypeStruct(shape, dtype) for sh...  17.2 us
    ppermute x9, waiting for transfers between devices, swap(): return lax.ppermute(value, axis, [(i, i ^ distance) for i in range(size)])  10.4 us
    ppermute x9, starting transfers between devices, swap(): return lax.ppermute(value, axis, [(i, i ^ distance) for i in range(size)])  9.12 us
    ppermute x1, starting transfers between devices, shards(): odd_grad = lax.ppermute(odd_grad, 'bus', onward)  3.5 us
    ppermute x1, starting transfers between devices, shards(): odd_grad = lax.ppermute(odd_grad, 'bus', evens)  1.79 us
    ppermute x1, starting transfers between devices, shards(): even_edge = lax.ppermute(even_own, 'bus', evens)  1.58 us
    ppermute x1, starting transfers between devices, shards(): even_grad = lax.ppermute(even_grad, 'bus', evens)  1.01 us
  transfers between devices with their start and end apart: 14, of which 8 were waited for; matrix products, arithmetic and copies ran while one was open for 0% of the time, Pallas kernels for 21%

profile of v7, /device:TPU:0, one launch (start us, length us, event | category | flops | bytes accessed | tf_op | source)
XLA Modules:
  0.0 46.7 jit_solution(18201636664975130977)
XLA Ops:
  0.6 0.5 %collective-permute-start.3 = (bf16[128,16,128]{2,1,0:T(8,128)(2,1)}, bf16[128,16,128]{2,1,0:T(8,128)(2,1)S(1)}, u32[]{:S(2)}, u32[]{:S(2)}) collective-permute-start(bf16[128,16,128]{2,1,0:T(8,128)(2,1)} %cot_src.1), channel_id=1, source_target_pairs={{0,1},{1,0},{2,3},{3,2},{4,5},{5,4},{6,7},{7,6},{8,9},{9,8},{10,11... | collective-permute-start | bytes 1572872 | tf_op jit(solution)/shard_map/ppermute | solution.py:450
  1.1 2.6 %collective-permute-start.2 = (bf16[128,16,128]{2,1,0:T(8,128)(2,1)}, bf16[128,16,128]{2,1,0:T(8,128)(2,1)S(1)}, u32[]{:S(2)}, u32[]{:S(2)}) collective-permute-start(bf16[128,16,128]{2,1,0:T(8,128)(2,1)} %cot_src.1), channel_id=1, source_target_pairs={{0,2},{1,3},{2,0},{3,1},{4,6},{5,7},{6,4},{7,5},{8,10},{9,11},{10,... | collective-permute-start | bytes 1572872 | tf_op jit(solution)/shard_map/ppermute | solution.py:450
  3.7 1.0 %shard_map.102.even_own = bf16[16,64,128]{2,1,0:T(8,128)(2,1)S(1)} custom-call(bf16[128,16,128]{2,1,0:T(8,128)(2,1)} %source_ref.3), custom_call_target="tpu_custom_call" | custom-call | flops 1 | bytes 1 | tf_op jit(solution)/shard_map/pallas_call | solution.py:33
  4.7 1.6 %collective-permute-start = (bf16[16,64,128]{2,1,0:T(8,128)(2,1)S(1)}, bf16[16,64,128]{2,1,0:T(8,128)(2,1)S(1)}, u32[]{:S(2)}, u32[]{:S(2)}) collective-permute-start(bf16[16,64,128]{2,1,0:T(8,128)(2,1)S(1)} %shard_map.102.even_own), channel_id=1, source_target_pairs={{0,4},{4,0},{8,12},{12,8},{16,20},{20,16},{24,28},{28,24},{1,5},{5... | collective-permute-start | bytes 786440 | tf_op jit(solution)/shard_map/ppermute | solution.py:483
  6.3 1.0 %shard_map.103.odd_own = bf16[16,64,128]{2,1,0:T(8,128)(2,1)S(1)} custom-call(bf16[128,16,128]{2,1,0:T(8,128)(2,1)} %source_ref.3), custom_call_target="tpu_custom_call" | custom-call | flops 1 | bytes 1 | tf_op jit(solution)/shard_map/pallas_call | solution.py:33
  7.3 0.7 %collective-permute-start.1 = (bf16[16,64,128]{2,1,0:T(8,128)(2,1)S(1)}, bf16[16,64,128]{2,1,0:T(8,128)(2,1)S(1)}, u32[]{:S(2)}, u32[]{:S(2)}) collective-permute-start(bf16[16,64,128]{2,1,0:T(8,128)(2,1)S(1)} %shard_map.103.odd_own), channel_id=1, source_target_pairs={{4,8},{12,16},{20,24},{8,4},{16,12},{24,20},{0,0},{28,28},{5,9},{1... | collective-permute-start | bytes 786440 | tf_op jit(solution)/shard_map/ppermute | solution.py:482
  8.0 4.6 %shard_map.104 = (f32[16,128,128]{2,1,0:T(8,128)S(1)}, bf16[32,128,256]{2,1,0:T(8,128)(2,1)S(1)}, bf16[128,256]{1,0:T(8,128)(2,1)S(1)}, bf16[256,128]{1,0:T(8,12...) custom-call(s32[2,8]{1,0:T(2,128)} %ids_src.1, ...), custom_call_target="tpu_custom_call" | custom-call | flops 1 | bytes 1 | tf_op jit(solution)/shard_map/pallas_call | solution.py:33
  12.6 3.8 %collective-permute-done.2.block_ref = bf16[128,16,128]{2,1,0:T(8,128)(2,1)S(1)} collective-permute-done((bf16[128,16,128]{2,1,0:T(8,128)(2,1)}, bf16[128,16,128]{2,1,0:T(8,128)(2,1)S(1)}, u32[]{:S(2)}, u32[]{:S(2)}) %collective-permute-start.2) | collective-permute-done | bytes 524320 | tf_op jit(solution)/shard_map/ppermute | solution.py:450
  16.4 1.8 %shard_map.105 = (f32[16,128,128]{2,1,0:T(8,128)S(1)}, bf16[32,128,256]{2,1,0:T(8,128)(2,1)S(1)}) custom-call(f32[16,128,128]{2,1,0:T(8,128)S(1)} %get-tuple-element.45.sum_ref, bf16[32,128,256]{2,1,0:T(8,128)(2,1)S(1)} %get-tuple-element.46.crossed_ref, bf16[128,16,128]{2,1,0:T(8,128)(2,1)S(1)} %collective-permute-done.2.block_ref, ...), custom_call_target="tpu_custom_call", output_to_operand_aliasing={{1}: (1, {})} | custom-call | flops 1 | bytes 1 | tf_op jit(solution)/shard_map/pallas_call | solution.py:33
  18.2 0.0 collective-permute-done.1.second_ref.odd_ref
  18.3 0.1 collective-permute-done.4.swapped_ref
  18.4 6.7 %shard_map.107 = (f32[160,128]{1,0:T(8,128)S(1)}, f32[160,128]{1,0:T(8,128)S(1)}, bf16[16,128,128]{2,1,0:T(8,128)(2,1)S(1)}, bf16[16,64,128]{2,1,0:T(8,128)(2,1)S(1)}, bf16[16,64,128]{2,1,0:T(8,128)(2,1)S(1)}) custom-call(bf16[16,64,128]{2,1,0:T(8,128)(2,1)S(1)} %shard_map.102.even_own, bf16[16,64,128]{2,1,0:T(8,128)(2,1)S(1)} %shard_map.103.odd_own, ...), custom_call_target="tpu_custom_call" | custom-call | flops 1 | bytes 1 | tf_op jit(solution)/shard_map/pallas_call | solution.py:33
  25.1 0.5 %collective-permute-start.5 = (f32[160,128]{1,0:T(8,128)S(1)}, f32[160,128]{1,0:T(8,128)S(1)}, u32[]{:S(2)}, u32[]{:S(2)}) collective-permute-start(f32[160,128]{1,0:T(8,128)S(1)} %get-tuple-element.62), channel_id=1, source_target_pairs={{0,1},{1,0},{2,3},{3,2},{4,5},{5,4},{6,7},{7,6},{8,9},{9,8},{10,11... | collective-permute-start | bytes 245768 | tf_op jit(solution)/shard_map/ppermute | solution.py:450
  25.6 1.8 %collective-permute-start.8 = (bf16[16,64,128]{2,1,0:T(8,128)(2,1)S(1)}, bf16[16,64,128]{2,1,0:T(8,128)(2,1)S(1)}, u32[]{:S(2)}, u32[]{:S(2)}) collective-permute-start(bf16[16,64,128]{2,1,0:T(8,128)(2,1)S(1)} %get-tuple-element.66), channel_id=1, source_target_pairs={{0,4},{4,0},{8,12},{12,8},{16,20},{20,16},{24,28},{28,24},{1,5},{5... | collective-permute-start | bytes 786440 | tf_op jit(solution)/shard_map/ppermute | solution.py:536
  27.4 0.0 collective-permute-done.5
  27.4 1.6 %collective-permute-start.6 = (bf16[160,128]{1,0:T(8,128)(2,1)S(1)}, bf16[160,128]{1,0:T(8,128)(2,1)S(1)}, u32[]{:S(2)}, u32[]{:S(2)}) collective-permute-start(bf16[160,128]{1,0:T(8,128)(2,1)S(1)} %convert_element_type.36), channel_id=1, source_target_pairs={{0,8},{4,12},{8,0},{12,4},{16,24},{20,28},{24,16},{28,20},{1,9},{5... | collective-permute-start | bytes 122888 | tf_op jit(solution)/shard_map/ppermute | solution.py:450
  29.1 1.0 %collective-permute-start.11 = (bf16[16,64,128]{2,1,0:T(8,128)(2,1)S(1)}, bf16[16,64,128]{2,1,0:T(8,128)(2,1)S(1)}, u32[]{:S(2)}, u32[]{:S(2)}) collective-permute-start(bf16[16,64,128]{2,1,0:T(8,128)(2,1)S(1)} %get-tuple-element.74), channel_id=1, source_target_pairs={{0,4},{4,0},{8,12},{12,8},{16,20},{20,16},{24,28},{28,24},{1,5},{5... | collective-permute-start | bytes 786440 | tf_op jit(solution)/shard_map/ppermute | solution.py:539
  30.1 1.4 %collective-permute-done.6 = bf16[160,128]{1,0:T(8,128)(2,1)S(1)} collective-permute-done((bf16[160,128]{1,0:T(8,128)(2,1)S(1)}, bf16[160,128]{1,0:T(8,128)(2,1)S(1)}, u32[]{:S(2)}, u32[]{:S(2)}) %collective-permute-start.6) | collective-permute-done | bytes 40992 | tf_op jit(solution)/shard_map/ppermute | solution.py:450
  31.5 2.7 %collective-permute-start.7 = (bf16[160,128]{1,0:T(8,128)(2,1)S(1)}, bf16[160,128]{1,0:T(8,128)(2,1)S(1)}, u32[]{:S(2)}, u32[]{:S(2)}) collective-permute-start(bf16[160,128]{1,0:T(8,128)(2,1)S(1)} %get-tuple-element.85), channel_id=1, source_target_pairs={{0,16},{4,20},{8,24},{12,28},{16,0},{20,4},{24,8},{28,12},{1,17},{... | collective-permute-start | bytes 122888 | tf_op jit(solution)/shard_map/ppermute | solution.py:450
  34.2 0.6 %collective-permute-done.8 = bf16[16,64,128]{2,1,0:T(8,128)(2,1)S(1)} collective-permute-done((bf16[16,64,128]{2,1,0:T(8,128)(2,1)S(1)}, bf16[16,64,128]{2,1,0:T(8,128)(2,1)S(1)}, u32[]{:S(2)}, u32[]{:S(2)}) %collective-permute-start.8) | collective-permute-done | bytes 262176 | tf_op jit(solution)/shard_map/ppermute | solution.py:536
  34.7 1.7 %collective-permute-done.7 = bf16[160,128]{1,0:T(8,128)(2,1)S(1)} collective-permute-done((bf16[160,128]{1,0:T(8,128)(2,1)S(1)}, bf16[160,128]{1,0:T(8,128)(2,1)S(1)}, u32[]{:S(2)}, u32[]{:S(2)}) %collective-permute-start.7) | collective-permute-done | bytes 40992 | tf_op jit(solution)/shard_map/ppermute | solution.py:450
  36.5 0.1 collective-permute-start.9
  36.6 0.3 shard_map.110.spread_ref
  36.9 3.5 %collective-permute-start.13 = (bf16[16,64,128]{2,1,0:T(8,128)(2,1)S(1)}, bf16[16,64,128]{2,1,0:T(8,128)(2,1)S(1)}, u32[]{:S(2)}, u32[]{:S(2)}) collective-permute-start(bf16[16,64,128]{2,1,0:T(8,128)(2,1)S(1)} %collective-permute-done.8), channel_id=1, source_target_pairs={{0,8},{8,16},{16,24},{12,4},{20,12},{28,20},{1,9},{9,17},{17,25},{... | collective-permute-start | bytes 786440 | tf_op jit(solution)/shard_map/ppermute | solution.py:550
  40.4 0.2 collective-permute-done.9
  40.6 1.1 %collective-permute-start.10 = (bf16[160,128]{1,0:T(8,128)(2,1)S(1)}, bf16[160,128]{1,0:T(8,128)(2,1)S(1)}, u32[]{:S(2)}, u32[]{:S(2)}) collective-permute-start(bf16[160,128]{1,0:T(8,128)(2,1)S(1)} %add_convert_fusion), channel_id=1, source_target_pairs={{0,4},{4,0},{8,12},{12,8},{16,20},{20,16},{24,28},{28,24},{1,5},{5... | collective-permute-start | bytes 122888 | tf_op jit(solution)/shard_map/ppermute | solution.py:450
  41.7 0.1 shard_map.111.spread_ref
  41.8 2.9 %collective-permute-done.10 = bf16[160,128]{1,0:T(8,128)(2,1)S(1)} collective-permute-done((bf16[160,128]{1,0:T(8,128)(2,1)S(1)}, bf16[160,128]{1,0:T(8,128)(2,1)S(1)}, u32[]{:S(2)}, u32[]{:S(2)}) %collective-permute-start.10) | collective-permute-done | bytes 40992 | tf_op jit(solution)/shard_map/ppermute | solution.py:450
  44.7 0.1 collective-permute-start.12
  44.8 1.0 %shard_map.112 = bf16[128,16,128]{2,1,0:T(8,128)(2,1)} custom-call(f32[16,128,128]{2,1,0:T(8,128)S(1)} %shard_map.111.spread_ref, bf16[16,64,128]{2,1,0:T(8,128)(2,1)S(1)} %collective-permute-done.13.odd_ref), custom_call_target="tpu_custom_call" | custom-call | flops 68719476736 | bytes 1 | tf_op jit(solution)/shard_map/pallas_call | solution.py:33
  45.8 0.2 collective-permute-done.12.other_ref
  46.0 0.7 %shard_map.113 = (f32[128,128]{1,0:T(8,128)}, f32[128,128]{1,0:T(8,128)}, f32[64,128]{1,0:T(8,128)}) custom-call(f32[160,128]{1,0:T(8,128)S(1)} %convert_add_fusion.mine_ref, f32[160,128]{1,0:T(8,128)S(1)} %collective-permute-done.12.other_ref, f32[8,128]{1,0:T(8,128)S(1)} %shard_map.109.mark_ref), custom_call_target="tpu_custom_call" | custom-call | flops 1 | bytes 1 | tf_op jit(solution)/shard_map/pallas_call | solution.py:33
  (15 shorter events, 0.1 us)
Async XLA Ops:
  0.6 7.4 %collective-permute-start.3 = (bf16[128,16,128]{2,1,0:T(8,128)(2,1)}, bf16[128,16,128]{2,1,0:T(8,128)(2,1)S(1)}, u32[]{:S(2)}, u32[]{:S(2)}) collective-permute-start(bf16[128,16,128]{2,1,0:T(8,128)(2,1)} %cot_src.1), channel_id=1, source_target_pairs={{0,1},{1,0},{2,3},{3,2},{4,5},{5,4},{6,7},{7,6},{8,9},{9,8},{10,11... | collective-permute-start | bytes 1572872 | tf_op jit(solution)/shard_map/ppermute | solution.py:450
  1.1 15.3 %collective-permute-start.2 = (bf16[128,16,128]{2,1,0:T(8,128)(2,1)}, bf16[128,16,128]{2,1,0:T(8,128)(2,1)S(1)}, u32[]{:S(2)}, u32[]{:S(2)}) collective-permute-start(bf16[128,16,128]{2,1,0:T(8,128)(2,1)} %cot_src.1), channel_id=1, source_target_pairs={{0,2},{1,3},{2,0},{3,1},{4,6},{5,7},{6,4},{7,5},{8,10},{9,11},{10,... | collective-permute-start | bytes 1572872 | tf_op jit(solution)/shard_map/ppermute | solution.py:450
  4.7 13.5 %collective-permute-start = (bf16[16,64,128]{2,1,0:T(8,128)(2,1)S(1)}, bf16[16,64,128]{2,1,0:T(8,128)(2,1)S(1)}, u32[]{:S(2)}, u32[]{:S(2)}) collective-permute-start(bf16[16,64,128]{2,1,0:T(8,128)(2,1)S(1)} %shard_map.102.even_own), channel_id=1, source_target_pairs={{0,4},{4,0},{8,12},{12,8},{16,20},{20,16},{24,28},{28,24},{1,5},{5... | collective-permute-start | bytes 786440 | tf_op jit(solution)/shard_map/ppermute | solution.py:483
  7.3 10.9 %collective-permute-start.1 = (bf16[16,64,128]{2,1,0:T(8,128)(2,1)S(1)}, bf16[16,64,128]{2,1,0:T(8,128)(2,1)S(1)}, u32[]{:S(2)}, u32[]{:S(2)}) collective-permute-start(bf16[16,64,128]{2,1,0:T(8,128)(2,1)S(1)} %shard_map.103.odd_own), channel_id=1, source_target_pairs={{4,8},{12,16},{20,24},{8,4},{16,12},{24,20},{0,0},{28,28},{5,9},{1... | collective-permute-start | bytes 786440 | tf_op jit(solution)/shard_map/ppermute | solution.py:482
  16.4 1.9 %collective-permute-start.4 = (bf16[128,16,128]{2,1,0:T(8,128)(2,1)S(1)}, bf16[128,16,128]{2,1,0:T(8,128)(2,1)S(1)}, u32[]{:S(2)}, u32[]{:S(2)}) collective-permute-start(bf16[128,16,128]{2,1,0:T(8,128)(2,1)S(1)} %collective-permute-done.2.block_ref), channel_id=1, source_target_pairs={{0,1},{1,0},{2,3},{3,2},{4,5},{5,4},{6,7},{7,6},{8,9},{9,8},{10,11... | collective-permute-start | bytes 1572872 | tf_op jit(solution)/shard_map/ppermute | solution.py:450
  25.1 2.3 %collective-permute-start.5 = (f32[160,128]{1,0:T(8,128)S(1)}, f32[160,128]{1,0:T(8,128)S(1)}, u32[]{:S(2)}, u32[]{:S(2)}) collective-permute-start(f32[160,128]{1,0:T(8,128)S(1)} %get-tuple-element.62), channel_id=1, source_target_pairs={{0,1},{1,0},{2,3},{3,2},{4,5},{5,4},{6,7},{7,6},{8,9},{9,8},{10,11... | collective-permute-start | bytes 245768 | tf_op jit(solution)/shard_map/ppermute | solution.py:450
  25.6 9.1 %collective-permute-start.8 = (bf16[16,64,128]{2,1,0:T(8,128)(2,1)S(1)}, bf16[16,64,128]{2,1,0:T(8,128)(2,1)S(1)}, u32[]{:S(2)}, u32[]{:S(2)}) collective-permute-start(bf16[16,64,128]{2,1,0:T(8,128)(2,1)S(1)} %get-tuple-element.66), channel_id=1, source_target_pairs={{0,4},{4,0},{8,12},{12,8},{16,20},{20,16},{24,28},{28,24},{1,5},{5... | collective-permute-start | bytes 786440 | tf_op jit(solution)/shard_map/ppermute | solution.py:536
  27.4 4.1 %collective-permute-start.6 = (bf16[160,128]{1,0:T(8,128)(2,1)S(1)}, bf16[160,128]{1,0:T(8,128)(2,1)S(1)}, u32[]{:S(2)}, u32[]{:S(2)}) collective-permute-start(bf16[160,128]{1,0:T(8,128)(2,1)S(1)} %convert_element_type.36), channel_id=1, source_target_pairs={{0,8},{4,12},{8,0},{12,4},{16,24},{20,28},{24,16},{28,20},{1,9},{5... | collective-permute-start | bytes 122888 | tf_op jit(solution)/shard_map/ppermute | solution.py:450
  29.1 12.6 %collective-permute-start.11 = (bf16[16,64,128]{2,1,0:T(8,128)(2,1)S(1)}, bf16[16,64,128]{2,1,0:T(8,128)(2,1)S(1)}, u32[]{:S(2)}, u32[]{:S(2)}) collective-permute-start(bf16[16,64,128]{2,1,0:T(8,128)(2,1)S(1)} %get-tuple-element.74), channel_id=1, source_target_pairs={{0,4},{4,0},{8,12},{12,8},{16,20},{20,16},{24,28},{28,24},{1,5},{5... | collective-permute-start | bytes 786440 | tf_op jit(solution)/shard_map/ppermute | solution.py:539
  31.5 5.0 %collective-permute-start.7 = (bf16[160,128]{1,0:T(8,128)(2,1)S(1)}, bf16[160,128]{1,0:T(8,128)(2,1)S(1)}, u32[]{:S(2)}, u32[]{:S(2)}) collective-permute-start(bf16[160,128]{1,0:T(8,128)(2,1)S(1)} %get-tuple-element.85), channel_id=1, source_target_pairs={{0,16},{4,20},{8,24},{12,28},{16,0},{20,4},{24,8},{28,12},{1,17},{... | collective-permute-start | bytes 122888 | tf_op jit(solution)/shard_map/ppermute | solution.py:450
  36.5 4.1 %collective-permute-start.9 = (bf16[160,128]{1,0:T(8,128)(2,1)S(1)}, bf16[160,128]{1,0:T(8,128)(2,1)S(1)}, u32[]{:S(2)}, u32[]{:S(2)}) collective-permute-start(bf16[160,128]{1,0:T(8,128)(2,1)S(1)} %add_convert_fusion.1), channel_id=1, source_target_pairs={{0,2},{1,3},{2,0},{3,1},{4,6},{5,7},{6,4},{7,5},{8,10},{9,11},{10,... | collective-permute-start | bytes 122888 | tf_op jit(solution)/shard_map/ppermute | solution.py:450
  36.9 7.9 %collective-permute-start.13 = (bf16[16,64,128]{2,1,0:T(8,128)(2,1)S(1)}, bf16[16,64,128]{2,1,0:T(8,128)(2,1)S(1)}, u32[]{:S(2)}, u32[]{:S(2)}) collective-permute-start(bf16[16,64,128]{2,1,0:T(8,128)(2,1)S(1)} %collective-permute-done.8), channel_id=1, source_target_pairs={{0,8},{8,16},{16,24},{12,4},{20,12},{28,20},{1,9},{9,17},{17,25},{... | collective-permute-start | bytes 786440 | tf_op jit(solution)/shard_map/ppermute | solution.py:550
  40.6 4.1 %collective-permute-start.10 = (bf16[160,128]{1,0:T(8,128)(2,1)S(1)}, bf16[160,128]{1,0:T(8,128)(2,1)S(1)}, u32[]{:S(2)}, u32[]{:S(2)}) collective-permute-start(bf16[160,128]{1,0:T(8,128)(2,1)S(1)} %add_convert_fusion), channel_id=1, source_target_pairs={{0,4},{4,0},{8,12},{12,8},{16,20},{20,16},{24,28},{28,24},{1,5},{5... | collective-permute-start | bytes 122888 | tf_op jit(solution)/shard_map/ppermute | solution.py:450
  44.7 1.3 %collective-permute-start.12 = (f32[160,128]{1,0:T(8,128)S(1)}, f32[160,128]{1,0:T(8,128)S(1)}, u32[]{:S(2)}, u32[]{:S(2)}) collective-permute-start(f32[160,128]{1,0:T(8,128)S(1)} %convert_add_fusion.mine_ref), channel_id=1, source_target_pairs={{0,1},{1,0},{2,3},{3,2},{4,5},{5,4},{6,7},{7,6},{8,9},{9,8},{10,11... | collective-permute-start | bytes 245768 | tf_op jit(solution)/shard_map/ppermute | solution.py:450

commit v8 on v7

--- a/solution.py
+++ b/solution.py
@@ -15,9 +15,9 @@
 LIMIT = 16 << 20
 
 
-def call(body, outs, *args, scratch=(), far=(), cost=1, kept=None, anywhere=()):
+def call(body, outs, *args, scratch=(), far=(), cost=1, kept=None, anywhere=(), placed=True):
     specs = [VMEM] * len(args)
-    results = [VMEM] * len(outs)
+    results = [VMEM if placed else pl.BlockSpec(memory_space=pl.ANY)] * len(outs)
     args = list(args)
     for i in anywhere:
         specs[i] = pl.BlockSpec(memory_space=pl.ANY)
@@ -434,15 +434,26 @@
     out_ref[...] = value_ref[0:8] + last_ref[...]
 
 
-def finish_body(scale, mine_ref, other_ref, mark_ref, graph_ref, out_ref, taps_ref, pack):
-    odd = lax.axis_index("tm") & 1
+def finish_body(mine_ref, other_ref, mark_ref, graph_ref, out_ref, taps_ref, sems):
     size = mine_ref.shape[0]
     chans = graph_ref.shape[0]
-    pack[pl.ds(pl.multiple_of(odd * size, size), size)] = mine_ref[...] * scale
-    pack[pl.ds(pl.multiple_of((1 - odd) * size, size), size)] = other_ref[...] * scale
-    graph_ref[...] = pack[0:chans]
-    out_ref[...] = pack[chans : 2 * chans]
-    taps_ref[...] = pack[2 * chans :]
+    extra = size - chans
+    odd = lax.axis_index("tm") & 1
+    for side, low, high in ((0, mine_ref, other_ref), (1, other_ref, mine_ref)):
+
+        @pl.when(odd == side)
+        def _():
+            copies = load_all(
+                sems,
+                [
+                    (low.at[pl.ds(0, chans)], graph_ref),
+                    (low.at[pl.ds(chans, extra)], out_ref.at[pl.ds(0, extra)]),
+                    (high.at[pl.ds(0, chans - extra)], out_ref.at[pl.ds(extra, chans - extra)]),
+                    (high.at[pl.ds(chans - extra, size - chans + extra)], taps_ref),
+                ],
+            )
+            for copy in copies:
+                copy.wait()
 
 
 def swap(value, axis, distance):
@@ -557,17 +568,17 @@
             (spread,) = call(edge_add_body, [(wide, F32)], spread, even_grad, cost=1 << 36)
             received, spread = lax.optimization_barrier((received, spread))
         keep = sent.astype(F32) + received.astype(F32)
+    keep = keep * (1.0 / math.sqrt(bus * rows * steps * tm))
     other = swap(keep, "tm", 1)
     (grad_features,) = call(
         final_body, [(features.shape, BF)], spread, odd_grad, cost=1 << 36
     )
     other, grad_features = lax.optimization_barrier((other, grad_features))
-    scale = 1.0 / math.sqrt(bus * rows * steps * tm)
     grad_graph, grad_out, grad_taps = call(
-        functools.partial(finish_body, scale),
+        finish_body,
         [(square, F32), (square, F32), ((total, chans), F32)],
         keep, other, mark,
-        scratch=[pltpu.VMEM((2 * size, chans), F32)],
+        scratch=[pltpu.SemaphoreType.DMA((4,))], placed=False,
     )
     return grad_features, grad_graph, grad_out, grad_taps
 

time: 47 us -> 47 us (level)
  no operation moved by 1% of the time
where the time goes in v8:
time: 47 us; the launch traced here: 46.7 us
  starting transfers between devices  17.7 us (38%)
  Pallas kernels  17.2 us (37%)
  waiting for transfers between devices  11 us (23%)
  between operations  0.79 us (2%)
    pallas_call x12, Pallas kernels, call(): pl.pallas_call(body, out_shape=[jax.ShapeDtypeStruct(shape, dtype) for sh...  17.2 us
    ppermute x9, waiting for transfers between devices, swap(): return lax.ppermute(value, axis, [(i, i ^ distance) for i in range(size)])  10.4 us
    ppermute x9, starting transfers between devices, swap(): return lax.ppermute(value, axis, [(i, i ^ distance) for i in range(size)])  9.12 us
    ppermute x1, starting transfers between devices, shards(): odd_grad = lax.ppermute(odd_grad, 'bus', onward)  3.5 us
    ppermute x1, starting transfers between devices, shards(): odd_grad = lax.ppermute(odd_grad, 'bus', evens)  1.79 us
    ppermute x1, starting transfers between devices, shards(): even_edge = lax.ppermute(even_own, 'bus', evens)  1.58 us
    ppermute x1, starting transfers between devices, shards(): even_grad = lax.ppermute(even_grad, 'bus', evens)  1.01 us
  transfers between devices with their start and end apart: 14, of which 8 were waited for; matrix products, arithmetic and copies ran while one was open for 0% of the time, Pallas kernels for 21%

profile of v8, /device:TPU:0, one launch (start us, length us, event | category | flops | bytes accessed | tf_op | source)
XLA Modules:
  0.0 46.7 jit_solution(17236462566600964081)
XLA Ops:
  0.6 0.5 %collective-permute-start.3 = (bf16[128,16,128]{2,1,0:T(8,128)(2,1)}, bf16[128,16,128]{2,1,0:T(8,128)(2,1)S(1)}, u32[]{:S(2)}, u32[]{:S(2)}) collective-permute-start(bf16[128,16,128]{2,1,0:T(8,128)(2,1)} %cot_src.1), channel_id=1, source_target_pairs={{0,1},{1,0},{2,3},{3,2},{4,5},{5,4},{6,7},{7,6},{8,9},{9,8},{10,11... | collective-permute-start | bytes 1572872 | tf_op jit(solution)/shard_map/ppermute | solution.py:461
  1.1 2.6 %collective-permute-start.2 = (bf16[128,16,128]{2,1,0:T(8,128)(2,1)}, bf16[128,16,128]{2,1,0:T(8,128)(2,1)S(1)}, u32[]{:S(2)}, u32[]{:S(2)}) collective-permute-start(bf16[128,16,128]{2,1,0:T(8,128)(2,1)} %cot_src.1), channel_id=1, source_target_pairs={{0,2},{1,3},{2,0},{3,1},{4,6},{5,7},{6,4},{7,5},{8,10},{9,11},{10,... | collective-permute-start | bytes 1572872 | tf_op jit(solution)/shard_map/ppermute | solution.py:461
  3.7 1.0 %shard_map.102.even_own = bf16[16,64,128]{2,1,0:T(8,128)(2,1)S(1)} custom-call(bf16[128,16,128]{2,1,0:T(8,128)(2,1)} %source_ref.3), custom_call_target="tpu_custom_call" | custom-call | flops 1 | bytes 1 | tf_op jit(solution)/shard_map/pallas_call | solution.py:33
  4.7 1.6 %collective-permute-start = (bf16[16,64,128]{2,1,0:T(8,128)(2,1)S(1)}, bf16[16,64,128]{2,1,0:T(8,128)(2,1)S(1)}, u32[]{:S(2)}, u32[]{:S(2)}) collective-permute-start(bf16[16,64,128]{2,1,0:T(8,128)(2,1)S(1)} %shard_map.102.even_own), channel_id=1, source_target_pairs={{0,4},{4,0},{8,12},{12,8},{16,20},{20,16},{24,28},{28,24},{1,5},{5... | collective-permute-start | bytes 786440 | tf_op jit(solution)/shard_map/ppermute | solution.py:494
  6.3 1.0 %shard_map.103.odd_own = bf16[16,64,128]{2,1,0:T(8,128)(2,1)S(1)} custom-call(bf16[128,16,128]{2,1,0:T(8,128)(2,1)} %source_ref.3), custom_call_target="tpu_custom_call" | custom-call | flops 1 | bytes 1 | tf_op jit(solution)/shard_map/pallas_call | solution.py:33
  7.3 0.7 %collective-permute-start.1 = (bf16[16,64,128]{2,1,0:T(8,128)(2,1)S(1)}, bf16[16,64,128]{2,1,0:T(8,128)(2,1)S(1)}, u32[]{:S(2)}, u32[]{:S(2)}) collective-permute-start(bf16[16,64,128]{2,1,0:T(8,128)(2,1)S(1)} %shard_map.103.odd_own), channel_id=1, source_target_pairs={{4,8},{12,16},{20,24},{8,4},{16,12},{24,20},{0,0},{28,28},{5,9},{1... | collective-permute-start | bytes 786440 | tf_op jit(solution)/shard_map/ppermute | solution.py:493
  8.0 0.0 collective-permute-done.3.near_ref
  8.0 4.6 %shard_map.104 = (f32[16,128,128]{2,1,0:T(8,128)S(1)}, bf16[32,128,256]{2,1,0:T(8,128)(2,1)S(1)}, bf16[128,256]{1,0:T(8,128)(2,1)S(1)}, bf16[256,128]{1,0:T(8,12...) custom-call(s32[2,8]{1,0:T(2,128)} %ids_src.1, ...), custom_call_target="tpu_custom_call" | custom-call | flops 1 | bytes 1 | tf_op jit(solution)/shard_map/pallas_call | solution.py:33
  12.6 3.8 %collective-permute-done.2.block_ref = bf16[128,16,128]{2,1,0:T(8,128)(2,1)S(1)} collective-permute-done((bf16[128,16,128]{2,1,0:T(8,128)(2,1)}, bf16[128,16,128]{2,1,0:T(8,128)(2,1)S(1)}, u32[]{:S(2)}, u32[]{:S(2)}) %collective-permute-start.2) | collective-permute-done | bytes 524320 | tf_op jit(solution)/shard_map/ppermute | solution.py:461
  16.4 1.8 %shard_map.105 = (f32[16,128,128]{2,1,0:T(8,128)S(1)}, bf16[32,128,256]{2,1,0:T(8,128)(2,1)S(1)}) custom-call(f32[16,128,128]{2,1,0:T(8,128)S(1)} %get-tuple-element.45.sum_ref, bf16[32,128,256]{2,1,0:T(8,128)(2,1)S(1)} %get-tuple-element.46.crossed_ref, bf16[128,16,128]{2,1,0:T(8,128)(2,1)S(1)} %collective-permute-done.2.block_ref, ...), custom_call_target="tpu_custom_call", output_to_operand_aliasing={{1}: (1, {})} | custom-call | flops 1 | bytes 1 | tf_op jit(solution)/shard_map/pallas_call | solution.py:33
  18.2 0.0 collective-permute-done.1.second_ref.odd_ref
  18.3 0.1 collective-permute-done.4.swapped_ref
  18.4 6.7 %shard_map.107 = (f32[160,128]{1,0:T(8,128)S(1)}, f32[160,128]{1,0:T(8,128)S(1)}, bf16[16,128,128]{2,1,0:T(8,128)(2,1)S(1)}, bf16[16,64,128]{2,1,0:T(8,128)(2,1)S(1)}, bf16[16,64,128]{2,1,0:T(8,128)(2,1)S(1)}) custom-call(bf16[16,64,128]{2,1,0:T(8,128)(2,1)S(1)} %shard_map.102.even_own, bf16[16,64,128]{2,1,0:T(8,128)(2,1)S(1)} %shard_map.103.odd_own, ...), custom_call_target="tpu_custom_call" | custom-call | flops 1 | bytes 1 | tf_op jit(solution)/shard_map/pallas_call | solution.py:33
  25.1 0.5 %collective-permute-start.5 = (f32[160,128]{1,0:T(8,128)S(1)}, f32[160,128]{1,0:T(8,128)S(1)}, u32[]{:S(2)}, u32[]{:S(2)}) collective-permute-start(f32[160,128]{1,0:T(8,128)S(1)} %get-tuple-element.62), channel_id=1, source_target_pairs={{0,1},{1,0},{2,3},{3,2},{4,5},{5,4},{6,7},{7,6},{8,9},{9,8},{10,11... | collective-permute-start | bytes 245768 | tf_op jit(solution)/shard_map/ppermute | solution.py:461
  25.6 1.8 %collective-permute-start.8 = (bf16[16,64,128]{2,1,0:T(8,128)(2,1)S(1)}, bf16[16,64,128]{2,1,0:T(8,128)(2,1)S(1)}, u32[]{:S(2)}, u32[]{:S(2)}) collective-permute-start(bf16[16,64,128]{2,1,0:T(8,128)(2,1)S(1)} %get-tuple-element.66), channel_id=1, source_target_pairs={{0,4},{4,0},{8,12},{12,8},{16,20},{20,16},{24,28},{28,24},{1,5},{5... | collective-permute-start | bytes 786440 | tf_op jit(solution)/shard_map/ppermute | solution.py:547
  27.4 1.6 %collective-permute-start.6 = (bf16[160,128]{1,0:T(8,128)(2,1)S(1)}, bf16[160,128]{1,0:T(8,128)(2,1)S(1)}, u32[]{:S(2)}, u32[]{:S(2)}) collective-permute-start(bf16[160,128]{1,0:T(8,128)(2,1)S(1)} %convert_element_type.36), channel_id=1, source_target_pairs={{0,8},{4,12},{8,0},{12,4},{16,24},{20,28},{24,16},{28,20},{1,9},{5... | collective-permute-start | bytes 122888 | tf_op jit(solution)/shard_map/ppermute | solution.py:461
  29.1 1.0 %collective-permute-start.11 = (bf16[16,64,128]{2,1,0:T(8,128)(2,1)S(1)}, bf16[16,64,128]{2,1,0:T(8,128)(2,1)S(1)}, u32[]{:S(2)}, u32[]{:S(2)}) collective-permute-start(bf16[16,64,128]{2,1,0:T(8,128)(2,1)S(1)} %get-tuple-element.74), channel_id=1, source_target_pairs={{0,4},{4,0},{8,12},{12,8},{16,20},{20,16},{24,28},{28,24},{1,5},{5... | collective-permute-start | bytes 786440 | tf_op jit(solution)/shard_map/ppermute | solution.py:550
  30.1 1.4 %collective-permute-done.6 = bf16[160,128]{1,0:T(8,128)(2,1)S(1)} collective-permute-done((bf16[160,128]{1,0:T(8,128)(2,1)S(1)}, bf16[160,128]{1,0:T(8,128)(2,1)S(1)}, u32[]{:S(2)}, u32[]{:S(2)}) %collective-permute-start.6) | collective-permute-done | bytes 40992 | tf_op jit(solution)/shard_map/ppermute | solution.py:461
  31.5 2.7 %collective-permute-start.7 = (bf16[160,128]{1,0:T(8,128)(2,1)S(1)}, bf16[160,128]{1,0:T(8,128)(2,1)S(1)}, u32[]{:S(2)}, u32[]{:S(2)}) collective-permute-start(bf16[160,128]{1,0:T(8,128)(2,1)S(1)} %get-tuple-element.85), channel_id=1, source_target_pairs={{0,16},{4,20},{8,24},{12,28},{16,0},{20,4},{24,8},{28,12},{1,17},{... | collective-permute-start | bytes 122888 | tf_op jit(solution)/shard_map/ppermute | solution.py:461
  34.2 0.6 %collective-permute-done.8 = bf16[16,64,128]{2,1,0:T(8,128)(2,1)S(1)} collective-permute-done((bf16[16,64,128]{2,1,0:T(8,128)(2,1)S(1)}, bf16[16,64,128]{2,1,0:T(8,128)(2,1)S(1)}, u32[]{:S(2)}, u32[]{:S(2)}) %collective-permute-start.8) | collective-permute-done | bytes 262176 | tf_op jit(solution)/shard_map/ppermute | solution.py:547
  34.7 1.7 %collective-permute-done.7 = bf16[160,128]{1,0:T(8,128)(2,1)S(1)} collective-permute-done((bf16[160,128]{1,0:T(8,128)(2,1)S(1)}, bf16[160,128]{1,0:T(8,128)(2,1)S(1)}, u32[]{:S(2)}, u32[]{:S(2)}) %collective-permute-start.7) | collective-permute-done | bytes 40992 | tf_op jit(solution)/shard_map/ppermute | solution.py:461
  36.5 0.1 collective-permute-start.9
  36.6 0.3 shard_map.110.spread_ref
  36.9 3.5 %collective-permute-start.13 = (bf16[16,64,128]{2,1,0:T(8,128)(2,1)S(1)}, bf16[16,64,128]{2,1,0:T(8,128)(2,1)S(1)}, u32[]{:S(2)}, u32[]{:S(2)}) collective-permute-start(bf16[16,64,128]{2,1,0:T(8,128)(2,1)S(1)} %collective-permute-done.8), channel_id=1, source_target_pairs={{0,8},{8,16},{16,24},{12,4},{20,12},{28,20},{1,9},{9,17},{17,25},{... | collective-permute-start | bytes 786440 | tf_op jit(solution)/shard_map/ppermute | solution.py:561
  40.4 0.2 collective-permute-done.9
  40.6 1.1 %collective-permute-start.10 = (bf16[160,128]{1,0:T(8,128)(2,1)S(1)}, bf16[160,128]{1,0:T(8,128)(2,1)S(1)}, u32[]{:S(2)}, u32[]{:S(2)}) collective-permute-start(bf16[160,128]{1,0:T(8,128)(2,1)S(1)} %add_convert_fusion), channel_id=1, source_target_pairs={{0,4},{4,0},{8,12},{12,8},{16,20},{20,16},{24,28},{28,24},{1,5},{5... | collective-permute-start | bytes 122888 | tf_op jit(solution)/shard_map/ppermute | solution.py:461
  41.7 0.1 shard_map.111.spread_ref
  41.8 2.9 %collective-permute-done.10 = bf16[160,128]{1,0:T(8,128)(2,1)S(1)} collective-permute-done((bf16[160,128]{1,0:T(8,128)(2,1)S(1)}, bf16[160,128]{1,0:T(8,128)(2,1)S(1)}, u32[]{:S(2)}, u32[]{:S(2)}) %collective-permute-start.10) | collective-permute-done | bytes 40992 | tf_op jit(solution)/shard_map/ppermute | solution.py:461
  44.7 0.1 collective-permute-start.12
  44.8 1.0 %shard_map.112 = bf16[128,16,128]{2,1,0:T(8,128)(2,1)} custom-call(f32[16,128,128]{2,1,0:T(8,128)S(1)} %shard_map.111.spread_ref, bf16[16,64,128]{2,1,0:T(8,128)(2,1)S(1)} %collective-permute-done.13.odd_ref), custom_call_target="tpu_custom_call" | custom-call | flops 68719476736 | bytes 1 | tf_op jit(solution)/shard_map/pallas_call | solution.py:33
  45.8 0.2 collective-permute-done.12.other_ref
  46.0 0.7 %shard_map.113 = (f32[128,128]{1,0:T(8,128)}, f32[128,128]{1,0:T(8,128)}, f32[64,128]{1,0:T(8,128)}) custom-call(f32[160,128]{1,0:T(8,128)S(1)} %add_multiply_fusion.mine_ref, f32[160,128]{1,0:T(8,128)S(1)} %collective-permute-done.12.other_ref, f32[8,128]{1,0:T(8,128)S(1)} %shard_map.109.mark_ref), custom_call_target="tpu_custom_call" | custom-call | flops 1 | bytes 1 | tf_op jit(solution)/shard_map/pallas_call | solution.py:33
  (15 shorter events, 0.1 us)
Async XLA Ops:
  0.6 7.4 %collective-permute-start.3 = (bf16[128,16,128]{2,1,0:T(8,128)(2,1)}, bf16[128,16,128]{2,1,0:T(8,128)(2,1)S(1)}, u32[]{:S(2)}, u32[]{:S(2)}) collective-permute-start(bf16[128,16,128]{2,1,0:T(8,128)(2,1)} %cot_src.1), channel_id=1, source_target_pairs={{0,1},{1,0},{2,3},{3,2},{4,5},{5,4},{6,7},{7,6},{8,9},{9,8},{10,11... | collective-permute-start | bytes 1572872 | tf_op jit(solution)/shard_map/ppermute | solution.py:461
  1.1 15.3 %collective-permute-start.2 = (bf16[128,16,128]{2,1,0:T(8,128)(2,1)}, bf16[128,16,128]{2,1,0:T(8,128)(2,1)S(1)}, u32[]{:S(2)}, u32[]{:S(2)}) collective-permute-start(bf16[128,16,128]{2,1,0:T(8,128)(2,1)} %cot_src.1), channel_id=1, source_target_pairs={{0,2},{1,3},{2,0},{3,1},{4,6},{5,7},{6,4},{7,5},{8,10},{9,11},{10,... | collective-permute-start | bytes 1572872 | tf_op jit(solution)/shard_map/ppermute | solution.py:461
  4.7 13.5 %collective-permute-start = (bf16[16,64,128]{2,1,0:T(8,128)(2,1)S(1)}, bf16[16,64,128]{2,1,0:T(8,128)(2,1)S(1)}, u32[]{:S(2)}, u32[]{:S(2)}) collective-permute-start(bf16[16,64,128]{2,1,0:T(8,128)(2,1)S(1)} %shard_map.102.even_own), channel_id=1, source_target_pairs={{0,4},{4,0},{8,12},{12,8},{16,20},{20,16},{24,28},{28,24},{1,5},{5... | collective-permute-start | bytes 786440 | tf_op jit(solution)/shard_map/ppermute | solution.py:494
  7.3 10.9 %collective-permute-start.1 = (bf16[16,64,128]{2,1,0:T(8,128)(2,1)S(1)}, bf16[16,64,128]{2,1,0:T(8,128)(2,1)S(1)}, u32[]{:S(2)}, u32[]{:S(2)}) collective-permute-start(bf16[16,64,128]{2,1,0:T(8,128)(2,1)S(1)} %shard_map.103.odd_own), channel_id=1, source_target_pairs={{4,8},{12,16},{20,24},{8,4},{16,12},{24,20},{0,0},{28,28},{5,9},{1... | collective-permute-start | bytes 786440 | tf_op jit(solution)/shard_map/ppermute | solution.py:493
  16.4 1.9 %collective-permute-start.4 = (bf16[128,16,128]{2,1,0:T(8,128)(2,1)S(1)}, bf16[128,16,128]{2,1,0:T(8,128)(2,1)S(1)}, u32[]{:S(2)}, u32[]{:S(2)}) collective-permute-start(bf16[128,16,128]{2,1,0:T(8,128)(2,1)S(1)} %collective-permute-done.2.block_ref), channel_id=1, source_target_pairs={{0,1},{1,0},{2,3},{3,2},{4,5},{5,4},{6,7},{7,6},{8,9},{9,8},{10,11... | collective-permute-start | bytes 1572872 | tf_op jit(solution)/shard_map/ppermute | solution.py:461
  25.1 2.3 %collective-permute-start.5 = (f32[160,128]{1,0:T(8,128)S(1)}, f32[160,128]{1,0:T(8,128)S(1)}, u32[]{:S(2)}, u32[]{:S(2)}) collective-permute-start(f32[160,128]{1,0:T(8,128)S(1)} %get-tuple-element.62), channel_id=1, source_target_pairs={{0,1},{1,0},{2,3},{3,2},{4,5},{5,4},{6,7},{7,6},{8,9},{9,8},{10,11... | collective-permute-start | bytes 245768 | tf_op jit(solution)/shard_map/ppermute | solution.py:461
  25.6 9.1 %collective-permute-start.8 = (bf16[16,64,128]{2,1,0:T(8,128)(2,1)S(1)}, bf16[16,64,128]{2,1,0:T(8,128)(2,1)S(1)}, u32[]{:S(2)}, u32[]{:S(2)}) collective-permute-start(bf16[16,64,128]{2,1,0:T(8,128)(2,1)S(1)} %get-tuple-element.66), channel_id=1, source_target_pairs={{0,4},{4,0},{8,12},{12,8},{16,20},{20,16},{24,28},{28,24},{1,5},{5... | collective-permute-start | bytes 786440 | tf_op jit(solution)/shard_map/ppermute | solution.py:547
  27.4 4.1 %collective-permute-start.6 = (bf16[160,128]{1,0:T(8,128)(2,1)S(1)}, bf16[160,128]{1,0:T(8,128)(2,1)S(1)}, u32[]{:S(2)}, u32[]{:S(2)}) collective-permute-start(bf16[160,128]{1,0:T(8,128)(2,1)S(1)} %convert_element_type.36), channel_id=1, source_target_pairs={{0,8},{4,12},{8,0},{12,4},{16,24},{20,28},{24,16},{28,20},{1,9},{5... | collective-permute-start | bytes 122888 | tf_op jit(solution)/shard_map/ppermute | solution.py:461
  29.1 12.6 %collective-permute-start.11 = (bf16[16,64,128]{2,1,0:T(8,128)(2,1)S(1)}, bf16[16,64,128]{2,1,0:T(8,128)(2,1)S(1)}, u32[]{:S(2)}, u32[]{:S(2)}) collective-permute-start(bf16[16,64,128]{2,1,0:T(8,128)(2,1)S(1)} %get-tuple-element.74), channel_id=1, source_target_pairs={{0,4},{4,0},{8,12},{12,8},{16,20},{20,16},{24,28},{28,24},{1,5},{5... | collective-permute-start | bytes 786440 | tf_op jit(solution)/shard_map/ppermute | solution.py:550
  31.5 5.0 %collective-permute-start.7 = (bf16[160,128]{1,0:T(8,128)(2,1)S(1)}, bf16[160,128]{1,0:T(8,128)(2,1)S(1)}, u32[]{:S(2)}, u32[]{:S(2)}) collective-permute-start(bf16[160,128]{1,0:T(8,128)(2,1)S(1)} %get-tuple-element.85), channel_id=1, source_target_pairs={{0,16},{4,20},{8,24},{12,28},{16,0},{20,4},{24,8},{28,12},{1,17},{... | collective-permute-start | bytes 122888 | tf_op jit(solution)/shard_map/ppermute | solution.py:461
  36.5 4.1 %collective-permute-start.9 = (bf16[160,128]{1,0:T(8,128)(2,1)S(1)}, bf16[160,128]{1,0:T(8,128)(2,1)S(1)}, u32[]{:S(2)}, u32[]{:S(2)}) collective-permute-start(bf16[160,128]{1,0:T(8,128)(2,1)S(1)} %add_convert_fusion.1), channel_id=1, source_target_pairs={{0,2},{1,3},{2,0},{3,1},{4,6},{5,7},{6,4},{7,5},{8,10},{9,11},{10,... | collective-permute-start | bytes 122888 | tf_op jit(solution)/shard_map/ppermute | solution.py:461
  36.9 7.9 %collective-permute-start.13 = (bf16[16,64,128]{2,1,0:T(8,128)(2,1)S(1)}, bf16[16,64,128]{2,1,0:T(8,128)(2,1)S(1)}, u32[]{:S(2)}, u32[]{:S(2)}) collective-permute-start(bf16[16,64,128]{2,1,0:T(8,128)(2,1)S(1)} %collective-permute-done.8), channel_id=1, source_target_pairs={{0,8},{8,16},{16,24},{12,4},{20,12},{28,20},{1,9},{9,17},{17,25},{... | collective-permute-start | bytes 786440 | tf_op jit(solution)/shard_map/ppermute | solution.py:561
  40.6 4.1 %collective-permute-start.10 = (bf16[160,128]{1,0:T(8,128)(2,1)S(1)}, bf16[160,128]{1,0:T(8,128)(2,1)S(1)}, u32[]{:S(2)}, u32[]{:S(2)}) collective-permute-start(bf16[160,128]{1,0:T(8,128)(2,1)S(1)} %add_convert_fusion), channel_id=1, source_target_pairs={{0,4},{4,0},{8,12},{12,8},{16,20},{20,16},{24,28},{28,24},{1,5},{5... | collective-permute-start | bytes 122888 | tf_op jit(solution)/shard_map/ppermute | solution.py:461
  44.7 1.3 %collective-permute-start.12 = (f32[160,128]{1,0:T(8,128)S(1)}, f32[160,128]{1,0:T(8,128)S(1)}, u32[]{:S(2)}, u32[]{:S(2)}) collective-permute-start(f32[160,128]{1,0:T(8,128)S(1)} %add_multiply_fusion.mine_ref), channel_id=1, source_target_pairs={{0,1},{1,0},{2,3},{3,2},{4,5},{5,4},{6,7},{7,6},{8,9},{9,8},{10,11... | collective-permute-start | bytes 245768 | tf_op jit(solution)/shard_map/ppermute | solution.py:461
